TPU v7x, 32 devices: a whole 2x2x4 slice. The times are simulated.
32 devices in a mesh: side: 2 (over x), grp: 4 (over z), blk: 4 (over y, core).
Axes of the slice: x: 2, y: 2, z: 4, core: 2. Of those that a mesh axis runs over, the one named last changes fastest.
Arguments:
- embed_codes: bfloat16 [2, 8192, 128], P('side', ('grp', 'blk')), may hold values from -4 to 4
- embed_exps: int32 [2, 64], P('side', ('grp', 'blk')), may hold values from -1 to 1
- degrees: int32 [2, 8192], P('side', ('grp', 'blk')), may hold values from 16 to 128
- adjacency: bfloat16 [2, 1536, 128, 128], P('side', ('grp', 'blk')), may hold values from 0 to 1
- block_index: int32 [2, 2, 1536], P('side', None, ('grp', 'blk')), may hold values from 0 to 16, as said below
Outputs:
- layer_rows: bfloat16 [2, 8192, 128], P('side', ('grp', 'blk'))
Inputs may be any that keep to these rules, and one draw needn't show every extreme that they name: `block_index`: each device's list of 96 slots: its used slots come first, in non-decreasing source tile (row 1 below 16), with distinct (destination, source) pairs and destination tiles below 16; the remaining slots have source 16 and destination 0. Every list uses 96 // 4 slots or more, and in each section one list uses all 96.
All inputs are finite; a program needn't handle non-finite values.
Results may differ from a plain program's by a relative error of at most 0.0048.
Values may be sent and summed in bfloat16 or wider, within the bound.
No kernel may reach another device: no remote copies, remote signals or barrier semaphores. Data moves between devices by JAX's collectives and lax.ppermute only.
A program may use at most 128 MiB of HBM per device.

v0:
```python
import functools

import jax
import jax.numpy as jnp
from jax import lax
from jax.experimental import pallas as pl
from jax.experimental.pallas import tpu as pltpu
from jax.sharding import PartitionSpec as P

UNROLL = 8
STAGES = 5
VMEM = pl.BlockSpec(memory_space=pltpu.VMEM)
SMEM = pl.BlockSpec(memory_space=pltpu.SMEM)
HBM = pl.BlockSpec(memory_space=pltpu.HBM)
LIMIT = pltpu.CompilerParams(vmem_limit_bytes=48 * 1024 * 1024)


def in_hbm(*arrays):
    return [pltpu.with_memory_space_constraint(array, pltpu.HBM) for array in arrays]


def split(value, size):
    if size & (size - 1) == 0:
        return value >> (size.bit_length() - 1), value & (size - 1)
    return value // size, value % size


def scale_kernel(
    exps_hbm, degrees_hbm, codes_hbm, rows, factors, scales, exps_ref, degrees, codes, sems
):
    pairs = [(exps_hbm, exps_ref), (degrees_hbm, degrees), (codes_hbm, codes)]
    fetches = [
        pltpu.make_async_copy(held, wanted, sems.at[at])
        for at, (held, wanted) in enumerate(pairs)
    ]
    for fetch in fetches:
        fetch.start()
    fetches[0].wait()
    fetches[1].wait()
    tiles_dev, tile_rows, row_width = rows.shape
    inverse = lax.rsqrt(degrees[...].astype(jnp.float32))
    for tile in range(tiles_dev):
        lanes = inverse[:, tile * tile_rows : (tile + 1) * tile_rows]
        factors[tile] = jnp.broadcast_to(lanes, (row_width, tile_rows)).T
        scale = jnp.exp2(jnp.full((1, 1), exps_ref[0, tile], jnp.int32).astype(jnp.float32))
        scales[tile : tile + 1, :] = lanes * scale
    fetches[2].wait()
    for tile in range(tiles_dev):
        scale = jnp.exp2(jnp.full((1, 1), exps_ref[0, tile], jnp.int32).astype(jnp.float32))
        scaled = codes[tile].astype(jnp.float32) * scale * factors[tile]
        rows[tile] = scaled.astype(rows.dtype)


def scale_rows(codes, exps, degrees):
    return pl.pallas_call(
        scale_kernel,
        out_shape=[
            jax.ShapeDtypeStruct(codes.shape, jnp.bfloat16),
            jax.ShapeDtypeStruct(codes.shape, jnp.float32),
            jax.ShapeDtypeStruct(codes.shape[:2], jnp.float32),
        ],
        in_specs=[HBM] * 3,
        out_specs=[VMEM] * 3,
        scratch_shapes=[
            pltpu.SMEM(exps.shape, exps.dtype),
            pltpu.VMEM(degrees.shape, degrees.dtype),
            pltpu.VMEM(codes.shape, codes.dtype),
            pltpu.SemaphoreType.DMA((3,)),
        ],
        compiler_params=LIMIT,
        cost_estimate=pl.CostEstimate(
            flops=codes.size, bytes_accessed=4 * codes.size, transcendentals=0
        ),
    )(*in_hbm(exps, degrees, codes))


def count_up(shape, axis):
    return lax.broadcasted_iota(jnp.int32, shape, axis)


def stage_kernel(
    blks, groups, tiles_dev, place_ref, index_hbm, blocks_hbm, order_ref, blocks, index_ref, sems
):
    fetch = pltpu.make_async_copy(index_hbm, index_ref, sems.at[0])
    fetch.start()
    copy = pltpu.make_async_copy(blocks_hbm, blocks, sems.at[1])
    copy.start()
    fetch.wait()
    my_blk = place_ref[0]
    my_grp = place_ref[1]
    capacity = index_ref.shape[1]
    width = order_ref.shape[1]
    source_tiles = blks * tiles_dev
    half = blks // 2
    role = my_blk & 1

    target = index_ref[0:1, :]
    origin = index_ref[1:2, :]
    hop, row = split(origin, tiles_dev)
    chunk, tile = split(target, tiles_dev)
    hop = hop ^ my_blk
    chunk = chunk ^ my_grp
    odd = hop & 1
    rank = jnp.where(odd == role, half - 1 - (hop >> 1), hop >> 1)
    far = (chunk >= 2) & ((chunk & 1) == 1)
    kept = jnp.where(chunk == 1, 1 + role * (groups // 2 - 1), (chunk >> 1) + 1 - role)
    kept = jnp.where(chunk == 0, 0, jnp.where(far, (chunk >> 1) - 1, kept))
    stage = jnp.where(far, jnp.where(odd == 1, 2, jnp.minimum(rank, 1)), 4)
    stage = jnp.where(far | (kept != 1), stage, 3)
    kept = jnp.where(far, kept, jnp.where(stage == 3, 0, kept - (kept > 1).astype(jnp.int32)))
    stage = jnp.where(origin < source_tiles, stage, STAGES)
    panel = jnp.where(stage == 1, rank - 1, jnp.where(stage == 2, rank, rank + odd * half))
    slot = count_up((1, capacity), 1)

    stages = (count_up((8, capacity), 0) == stage).astype(jnp.float32)
    earlier = count_up((capacity, capacity), 0) < count_up((capacity, capacity), 1)
    before = jnp.dot(
        stages.astype(jnp.bfloat16), earlier.astype(jnp.bfloat16), preferred_element_type=jnp.float32
    )
    position = jnp.sum(stages * before, axis=0, keepdims=True).astype(jnp.int32)
    parts = (slot & 127, slot >> 7, panel * tiles_dev + row, kept * tiles_dev + tile)
    values = sum(
        jnp.where(count_up((8, capacity), 0) == at, part, 0) for at, part in enumerate(parts)
    ).astype(jnp.bfloat16)
    far_tiles = (groups // 2 - 1) * tiles_dev
    tops = [far_tiles] * 3 + [tiles_dev, groups // 2 * tiles_dev]
    lanes = count_up((1, width), 1)
    for at, top in enumerate(tops):
        where = jnp.where(stage == at, position, -1)
        chosen = (count_up((width, capacity), 0) == where).astype(jnp.bfloat16)
        listed = lax.dot_general(
            values, chosen, (((1,), (1,)), ((), ())), preferred_element_type=jnp.float32
        ).astype(jnp.int32)
        word = pack(listed[0:1] + (listed[1:2] << 7), listed[2:3], listed[3:4])
        count = jnp.sum((stage == at).astype(jnp.int32), axis=1, keepdims=True)
        word = jnp.where(lanes < count, word, pack(0, 0, top))
        batches = split(count + (UNROLL - 1), UNROLL)[0]
        order_ref[at : at + 1, :] = jnp.where(lanes == width - UNROLL, batches, word)
    copy.wait()


def pack(slot, row, target):
    return (slot << 16) | (row << 8) | target


def unpack(word):
    return word >> 16, (word >> 8) & 255, word & 255


def stage_blocks(index, place, blocks, blks, groups, tiles_dev):
    capacity = blocks.shape[0]
    assert blks * tiles_dev < 256 and groups * tiles_dev < 256 and capacity < 2**15
    width = -(-(capacity + 2 * UNROLL) // 128) * 128
    return pl.pallas_call(
        functools.partial(stage_kernel, blks, groups, tiles_dev),
        out_shape=[
            jax.ShapeDtypeStruct((8, width), jnp.int32),
            jax.ShapeDtypeStruct(blocks.shape, blocks.dtype),
        ],
        in_specs=[SMEM, HBM, HBM],
        out_specs=[VMEM, VMEM],
        scratch_shapes=[
            pltpu.VMEM(index.shape, index.dtype),
            pltpu.SemaphoreType.DMA((2,)),
        ],
        compiler_params=LIMIT,
        cost_estimate=pl.CostEstimate(flops=0, bytes_accessed=0, transcendentals=0),
    )(place, *in_hbm(index, blocks))


def add_products(stage, order_ref, blocks, source, total):
    @pl.loop(0, order_ref[stage, order_ref.shape[1] - UNROLL])
    def _(batch):
        made = []
        for part in range(UNROLL):
            slot, row, target = unpack(order_ref[stage, batch * UNROLL + part])
            product = jnp.dot(blocks[slot], source[row], preferred_element_type=jnp.float32)
            made.append((target, product))
        for target, product in made:
            total[target] += product


def gather_panels(panels, source):
    for at, panel in enumerate(panels):
        rows = panel.shape[0]
        source[at * rows : (at + 1) * rows] = panel[...]


def early_kernel(order_ref, panel, blocks, total):
    total[...] = jnp.zeros_like(total)
    add_products(0, order_ref, blocks, panel, total)


def middle_kernel(order_ref, *refs):
    *panels, blocks, _, total, source = refs
    gather_panels(panels, source)
    add_products(1, order_ref, blocks, source, total)


def far_kernel(order_ref, *refs):
    *panels, blocks, total, far, source = refs
    gather_panels(panels, source)
    add_products(2, order_ref, blocks, source, total)
    far[...] = total[: far.shape[0]].astype(far.dtype)


def first_kernel(order_ref, *refs):
    *panels, blocks, first, source, total = refs
    gather_panels(panels, source)
    total[...] = jnp.zeros_like(total)
    add_products(3, order_ref, blocks, source, total)
    first[...] = total[: first.shape[0]].astype(first.dtype)


def rest_kernel(order_ref, *refs):
    *panels, blocks, own, later, source, total = refs
    gather_panels(panels, source)
    total[...] = jnp.zeros_like(total)
    add_products(4, order_ref, blocks, source, total)
    tiles_dev = own.shape[0]
    own[...] = total[:tiles_dev]
    later[...] = total[tiles_dev : tiles_dev + later.shape[0]]


def final_kernel(factors, own, *refs):
    *arrived, out_hbm, out, sems = refs
    copies = []
    for tile in range(out.shape[0]):
        value = own[tile]
        for piece in arrived:
            value = value + piece[tile].astype(jnp.float32)
        out[tile] = (value * factors[tile]).astype(out.dtype)
        copies.append(pltpu.make_async_copy(out.at[tile], out_hbm.at[tile], sems.at[tile]))
        copies[-1].start()
    for copy in copies:
        copy.wait()


def cost_of(slots, tile_rows, row_width):
    return pl.CostEstimate(
        flops=2 * slots * tile_rows * tile_rows * row_width,
        bytes_accessed=2 * slots * tile_rows * tile_rows,
        transcendentals=0,
    )


def shards(embed_codes, embed_exps, degrees, adjacency, block_index):
    tile_rows = adjacency.shape[2]
    row_width = embed_codes.shape[2]
    row_count = embed_codes.shape[1]
    capacity = adjacency.shape[1]
    tiles_dev = row_count // tile_rows
    groups = lax.axis_size("grp")
    blks = lax.axis_size("blk")
    part = (tiles_dev, tile_rows, row_width)
    codes = embed_codes.reshape(part)
    source, factors, scales = scale_rows(codes, embed_exps, degrees)

    def across(value, step):
        pairs = [
            (side * blks + at, (1 - side) * blks + (at ^ (2 * step if at & 1 else blks - 2 - 2 * step)))
            for side in range(2)
            for at in range(blks)
        ]
        return lax.ppermute(value, ("side", "blk"), pairs)

    def paired(value, axis, hop):
        return lax.ppermute(value, axis, [(at, at ^ hop) for at in range(lax.axis_size(axis))])

    place = jnp.stack([lax.axis_index("blk"), lax.axis_index("grp")]).astype(jnp.int32)
    early = across(codes, 0)
    middle = [across(source, step) for step in range(1, blks // 2)]
    early_scales = across(scales, 0)
    order, blocks = stage_blocks(block_index[0], place, adjacency[0], blks, groups, tiles_dev)
    early, early_scales, order = lax.optimization_barrier((early, early_scales, order))
    early = (early.astype(jnp.float32) * early_scales[:, :, None]).astype(jnp.bfloat16)
    other = paired(early, "blk", 1)
    far_tiles = (groups // 2 - 1) * tiles_dev

    def held(count, dtype):
        return pltpu.VMEM((count, tile_rows, row_width), dtype)

    total = pl.pallas_call(
        early_kernel,
        out_shape=jax.ShapeDtypeStruct((far_tiles + 1, tile_rows, row_width), jnp.float32),
        in_specs=[SMEM] + [VMEM] * 2,
        out_specs=VMEM,
        compiler_params=LIMIT,
        cost_estimate=cost_of(capacity // 8, tile_rows, row_width),
    )(order, early, blocks)
    *middle, total = lax.optimization_barrier((*middle, total))
    others = [other] + [paired(panel, "blk", 1) for panel in middle]
    total = pl.pallas_call(
        middle_kernel,
        out_shape=jax.ShapeDtypeStruct(total.shape, total.dtype),
        in_specs=[SMEM] + [VMEM] * (len(middle) + 2),
        out_specs=VMEM,
        input_output_aliases={len(middle) + 2: 0},
        scratch_shapes=[held(len(middle) * tiles_dev, jnp.bfloat16)],
        compiler_params=LIMIT,
        cost_estimate=cost_of(capacity // 8, tile_rows, row_width),
    )(order, *middle, blocks, total)
    *others, total = lax.optimization_barrier((*others, total))
    far = pl.pallas_call(
        far_kernel,
        out_shape=jax.ShapeDtypeStruct((far_tiles, tile_rows, row_width), jnp.bfloat16),
        in_specs=[SMEM] + [VMEM] * (len(others) + 2),
        out_specs=VMEM,
        scratch_shapes=[held(len(others) * tiles_dev, jnp.bfloat16)],
        compiler_params=LIMIT,
        cost_estimate=cost_of(capacity // 8, tile_rows, row_width),
    )(order, *others, blocks, total)
    far, order = lax.optimization_barrier((far, order))
    panels = [early] + middle + others
    first = pl.pallas_call(
        first_kernel,
        out_shape=jax.ShapeDtypeStruct(part, jnp.bfloat16),
        in_specs=[SMEM] + [VMEM] * (len(panels) + 1),
        out_specs=VMEM,
        scratch_shapes=[
            held(len(panels) * tiles_dev, jnp.bfloat16),
            held(tiles_dev + 1, jnp.float32),
        ],
        compiler_params=LIMIT,
        cost_estimate=cost_of(capacity // 4, tile_rows, row_width),
    )(order, *panels, blocks)
    first, order = lax.optimization_barrier((first, order))
    own, later = pl.pallas_call(
        rest_kernel,
        out_shape=[
            jax.ShapeDtypeStruct(part, jnp.float32),
            jax.ShapeDtypeStruct((far_tiles, tile_rows, row_width), jnp.float32),
        ],
        in_specs=[SMEM] + [VMEM] * (len(panels) + 1),
        out_specs=[VMEM] * 2,
        scratch_shapes=[
            held(len(panels) * tiles_dev, jnp.bfloat16),
            held(groups // 2 * tiles_dev + 1, jnp.float32),
        ],
        compiler_params=LIMIT,
        cost_estimate=cost_of(capacity // 2, tile_rows, row_width),
    )(order, *panels, blocks)

    def turned(value, even_hop, odd_hop):
        hops = (even_hop, odd_hop)
        pairs = [
            (at * blks + blk, (at ^ hops[blk & 1]) * blks + blk)
            for at in range(groups)
            for blk in range(blks)
        ]
        return lax.ppermute(value, ("grp", "blk"), pairs)

    steps = groups // 2 - 1
    even_core = lax.axis_index("blk") % 2 == 0
    pieces = [slice(at * tiles_dev, (at + 1) * tiles_dev) for at in range(steps)]
    handed = [turned(far[pieces[at]], 1, 2 * at + 2).astype(jnp.float32) for at in range(steps)]
    arrived = [turned(first, 1, 2)]
    for at in range(steps):
        value = later[pieces[at]]
        for step, extra in enumerate(handed):
            if step == at == steps - 1:
                value = value + extra
            elif step == at:
                value = value + jnp.where(even_core, extra, 0.0)
            elif at == steps - 1:
                value = value + jnp.where(even_core, 0.0, extra)
        odd_hop = 1 if at == steps - 1 else 2 * at + 4
        arrived.append(turned(value.astype(jnp.bfloat16), 2 * at + 2, odd_hop))
    own = own + arrived[0].astype(jnp.float32)
    own, *sums = lax.optimization_barrier((own, *arrived[1:]))
    out = pl.pallas_call(
        final_kernel,
        out_shape=jax.ShapeDtypeStruct(part, jnp.bfloat16),
        in_specs=[VMEM] * (2 + len(sums)),
        out_specs=HBM,
        scratch_shapes=[
            held(tiles_dev, jnp.bfloat16),
            pltpu.SemaphoreType.DMA((tiles_dev,)),
        ],
        compiler_params=LIMIT,
        cost_estimate=cost_of(0, tile_rows, row_width),
    )(factors, own, *sums)
    return out.reshape(1, row_count, row_width)


def solution(mesh):
    placed = (
        P("side", ("grp", "blk"), None),
        P("side", ("grp", "blk")),
        P("side", ("grp", "blk")),
        P("side", ("grp", "blk"), None, None),
        P("side", None, ("grp", "blk")),
    )
    return jax.shard_map(
        shards,
        mesh=mesh,
        in_specs=placed,
        out_specs=P("side", ("grp", "blk"), None),
        check_vma=False,
    )
```

profile of v0, /device:TPU:0, one launch (start us, length us, event | category | flops | bytes accessed | tf_op | source)
XLA Modules:
  0.0 27.1 jit_solution(15130604291012020372)
XLA Ops:
  0.0 3.9 %collective-permute-start = (bf16[4,128,128]{2,1,0:T(8,128)(2,1)}, bf16[4,128,128]{2,1,0:T(8,128)(2,1)S(1)}, u32[]{:S(2)}, u32[]{:S(2)}) collective-permute-start(bf16[4,128,128]{2,1,0:T(8,128)(2,1)} %bitcast.7), channel_id=1, source_target_pairs={{0,18},{1,17},{2,16},{3,19},{16,2},{17,1},{18,0},{19,3},{4,22},{5,... | collective-permute-start | bytes 393224 | tf_op jit(solution)/shard_map/ppermute | solution.py:265
  3.9 1.0 %shard_map.55 = (bf16[4,128,128]{2,1,0:T(8,128)(2,1)S(1)}, f32[4,128,128]{2,1,0:T(8,128)S(1)}, f32[4,128]{1,0:T(4,128)S(1)}) custom-call(s32[1,4]{1,0:T(1,128)} %exps_hbm.1, s32[1,512]{1,0:T(1,128)} %degrees_hbm.1, bf16[4,128,128]{2,1,0:T(8,128)(2,1)} %bitcast.8), custom_call_target="tpu_custom_call" | custom-call | flops 65536 | bytes 262144 | tf_op jit(solution)/shard_map/pallas_call | solution.py:55
  4.9 0.1 collective-permute-start.1
  5.0 2.0 %collective-permute-start.3 = (bf16[4,128,128]{2,1,0:T(8,128)(2,1)S(1)}, bf16[4,128,128]{2,1,0:T(8,128)(2,1)S(1)}, u32[]{:S(2)}, u32[]{:S(2)}) collective-permute-start(bf16[4,128,128]{2,1,0:T(8,128)(2,1)S(1)} %get-tuple-element.32), channel_id=1, source_target_pairs={{0,16},{1,19},{2,18},{3,17},{16,0},{17,3},{18,2},{19,1},{4,20},{5,... | collective-permute-start | bytes 393224 | tf_op jit(solution)/shard_map/ppermute | solution.py:265
  6.9 0.1 pad_add_fusion.place_ref
  7.0 2.5 %shard_map.56 = (s32[8,128]{1,0:T(8,128)S(1)}, bf16[96,128,128]{2,1,0:T(8,128)(2,1)S(1)}) custom-call(s32[2]{0:T(128)S(1)} %pad_add_fusion.place_ref, s32[2,96]{1,0:T(2,128)} %bitcast.9, bf16[96,128,128]{2,1,0:T(8,128)(2,1)} %bitcast.6), custom_call_target="tpu_custom_call" | custom-call | tf_op jit(solution)/shard_map/pallas_call | solution.py:154
  9.5 0.0 collective-permute-done.1
  9.5 0.1 multiply_convert_fusion.panel.refs_0_
  9.6 0.1 collective-permute-start.2
  9.7 0.6 %shard_map.57.refs_2_ = f32[5,128,128]{2,1,0:T(8,128)S(1)} custom-call(s32[8,128]{1,0:T(8,128)S(1)} %get-tuple-element.40.order_ref, bf16[4,128,128]{2,1,0:T(8,128)(2,1)S(1)} %multiply_convert_fusion.panel.refs_0_, bf16[96,128,128]{2,1,0:T(8,128)(2,1)S(1)} %get-tuple-element.33.blocks.refs_1_.refs_2_.refs_4_), custom_call_target="tpu_custom_call" | custom-call | flops 50331648 | bytes 393216 | tf_op jit(solution)/shard_map/pallas_call | solution.py:283
  10.4 0.1 collective-permute-done.3.refs_0_.refs_1_
  10.4 0.5 %collective-permute-start.4 = (bf16[4,128,128]{2,1,0:T(8,128)(2,1)S(1)}, bf16[4,128,128]{2,1,0:T(8,128)(2,1)S(1)}, u32[]{:S(2)}, u32[]{:S(2)}) collective-permute-start(bf16[4,128,128]{2,1,0:T(8,128)(2,1)S(1)} %collective-permute-done.3.refs_0_.refs_1_), channel_id=1, source_target_pairs={{0,1},{1,0},{2,3},{3,2},{4,5},{5,4},{6,7},{7,6},{8,9},{9,8},{10,11... | collective-permute-start | bytes 393224 | tf_op jit(solution)/shard_map/ppermute | solution.py:268
  10.9 0.6 %shard_map.58.refs_3_ = f32[5,128,128]{2,1,0:T(8,128)S(1)} custom-call(s32[8,128]{1,0:T(8,128)S(1)} %get-tuple-element.40.order_ref, bf16[4,128,128]{2,1,0:T(8,128)(2,1)S(1)} %collective-permute-done.3.refs_0_.refs_1_, bf16[96,128,128]{2,1,0:T(8,128)(2,1)S(1)} %get-tuple-element.33.blocks.refs_1_.refs_2_.refs_4_, ...), custom_call_target="tpu_custom_call", output_to_operand_aliasing={{}: (3, {})} | custom-call | flops 50331648 | bytes 393216 | tf_op jit(solution)/shard_map/pallas_call | solution.py:293
  11.6 0.4 %collective-permute-done.4.refs_1_.refs_3_ = bf16[4,128,128]{2,1,0:T(8,128)(2,1)S(1)} collective-permute-done((bf16[4,128,128]{2,1,0:T(8,128)(2,1)S(1)}, bf16[4,128,128]{2,1,0:T(8,128)(2,1)S(1)}, u32[]{:S(2)}, u32[]{:S(2)}) %collective-permute-start.4) | collective-permute-done | bytes 131104 | tf_op jit(solution)/shard_map/ppermute | solution.py:268
  11.9 1.1 %shard_map.59 = bf16[4,128,128]{2,1,0:T(8,128)(2,1)S(1)} custom-call(s32[8,128]{1,0:T(8,128)S(1)} %get-tuple-element.40.order_ref, bf16[4,128,128]{2,1,0:T(8,128)(2,1)S(1)} %collective-permute-done.2.refs_0_.refs_2_, bf16[4,128,128]{2,1,0:T(8,128)(2,1)S(1)} %collective-permute-done.4.refs_1_.refs_3_, ...), custom_call_target="tpu_custom_call" | custom-call | flops 50331648 | bytes 393216 | tf_op jit(solution)/shard_map/pallas_call | solution.py:304
  13.0 1.5 %collective-permute-start.6 = (bf16[4,128,128]{2,1,0:T(8,128)(2,1)S(1)}, bf16[4,128,128]{2,1,0:T(8,128)(2,1)S(1)}, u32[]{:S(2)}, u32[]{:S(2)}) collective-permute-start(bf16[4,128,128]{2,1,0:T(8,128)(2,1)S(1)} %shard_map.59), channel_id=1, source_target_pairs={{0,4},{1,9},{2,6},{3,11},{4,0},{5,13},{6,2},{7,15},{8,12},{9,1},{1... | collective-permute-start | bytes 393224 | tf_op jit(solution)/shard_map/ppermute | solution.py:351
  14.5 1.1 %shard_map.60 = bf16[4,128,128]{2,1,0:T(8,128)(2,1)S(1)} custom-call(s32[8,128]{1,0:T(8,128)S(1)} %get-tuple-element.40.order_ref, bf16[4,128,128]{2,1,0:T(8,128)(2,1)S(1)} %multiply_convert_fusion.panel.refs_0_, bf16[4,128,128]{2,1,0:T(8,128)(2,1)S(1)} %collective-permute-done.3.refs_0_.refs_1_, ...), custom_call_target="tpu_custom_call" | custom-call | flops 100663296 | bytes 786432 | tf_op jit(solution)/shard_map/pallas_call | solution.py:315
  15.7 0.9 %collective-permute-start.5 = (bf16[4,128,128]{2,1,0:T(8,128)(2,1)S(1)}, bf16[4,128,128]{2,1,0:T(8,128)(2,1)S(1)}, u32[]{:S(2)}, u32[]{:S(2)}) collective-permute-start(bf16[4,128,128]{2,1,0:T(8,128)(2,1)S(1)} %shard_map.60), channel_id=1, source_target_pairs={{0,4},{1,9},{2,6},{3,11},{4,0},{5,13},{6,2},{7,15},{8,12},{9,1},{1... | collective-permute-start | bytes 393224 | tf_op jit(solution)/shard_map/ppermute | solution.py:351
  16.6 1.7 %shard_map.61 = (f32[4,128,128]{2,1,0:T(8,128)S(1)}, f32[4,128,128]{2,1,0:T(8,128)S(1)}) custom-call(s32[8,128]{1,0:T(8,128)S(1)} %get-tuple-element.40.order_ref, bf16[4,128,128]{2,1,0:T(8,128)(2,1)S(1)} %multiply_convert_fusion.panel.refs_0_, bf16[4,128,128]{2,1,0:T(8,128)(2,1)S(1)} %collective-permute-done.3.refs_0_.refs_1_, ...), custom_call_target="tpu_custom_call" | custom-call | flops 201326592 | bytes 1572864 | tf_op jit(solution)/shard_map/pallas_call | solution.py:328
  18.2 1.2 %collective-permute-done.6 = bf16[4,128,128]{2,1,0:T(8,128)(2,1)S(1)} collective-permute-done((bf16[4,128,128]{2,1,0:T(8,128)(2,1)S(1)}, bf16[4,128,128]{2,1,0:T(8,128)(2,1)S(1)}, u32[]{:S(2)}, u32[]{:S(2)}) %collective-permute-start.6) | collective-permute-done | bytes 131104 | tf_op jit(solution)/shard_map/ppermute | solution.py:351
  19.5 2.1 %collective-permute-start.7 = (bf16[4,128,128]{2,1,0:T(8,128)(2,1)S(1)}, bf16[4,128,128]{2,1,0:T(8,128)(2,1)S(1)}, u32[]{:S(2)}, u32[]{:S(2)}) collective-permute-start(bf16[4,128,128]{2,1,0:T(8,128)(2,1)S(1)} %add_convert_fusion), channel_id=1, source_target_pairs={{0,8},{1,5},{2,10},{3,7},{4,12},{5,1},{6,14},{7,3},{8,0},{9,13},{1... | collective-permute-start | bytes 393224 | tf_op jit(solution)/shard_map/ppermute | solution.py:351
  21.6 0.7 %collective-permute-done.5 = bf16[4,128,128]{2,1,0:T(8,128)(2,1)S(1)} collective-permute-done((bf16[4,128,128]{2,1,0:T(8,128)(2,1)S(1)}, bf16[4,128,128]{2,1,0:T(8,128)(2,1)S(1)}, u32[]{:S(2)}, u32[]{:S(2)}) %collective-permute-start.5) | collective-permute-done | bytes 131104 | tf_op jit(solution)/shard_map/ppermute | solution.py:351
  22.4 4.0 %collective-permute-done.7.refs_0_ = bf16[4,128,128]{2,1,0:T(8,128)(2,1)S(1)} collective-permute-done((bf16[4,128,128]{2,1,0:T(8,128)(2,1)S(1)}, bf16[4,128,128]{2,1,0:T(8,128)(2,1)S(1)}, u32[]{:S(2)}, u32[]{:S(2)}) %collective-permute-start.7) | collective-permute-done | bytes 131104 | tf_op jit(solution)/shard_map/ppermute | solution.py:351
  26.4 0.7 %shard_map.62 = bf16[4,128,128]{2,1,0:T(8,128)(2,1)} custom-call(f32[4,128,128]{2,1,0:T(8,128)S(1)} %get-tuple-element.26.factors, f32[4,128,128]{2,1,0:T(8,128)S(1)} %convert_add_fusion.own, bf16[4,128,128]{2,1,0:T(8,128)(2,1)S(1)} %collective-permute-done.7.refs_0_), custom_call_target="tpu_custom_call" | custom-call | tf_op jit(solution)/shard_map/pallas_call | solution.py:371
  (4 shorter events, 0.1 us)
Async XLA Ops:
  0.0 9.5 %collective-permute-start = (bf16[4,128,128]{2,1,0:T(8,128)(2,1)}, bf16[4,128,128]{2,1,0:T(8,128)(2,1)S(1)}, u32[]{:S(2)}, u32[]{:S(2)}) collective-permute-start(bf16[4,128,128]{2,1,0:T(8,128)(2,1)} %bitcast.7), channel_id=1, source_target_pairs={{0,18},{1,17},{2,16},{3,19},{16,2},{17,1},{18,0},{19,3},{4,22},{5,... | collective-permute-start | bytes 393224 | tf_op jit(solution)/shard_map/ppermute | solution.py:265
  4.9 4.6 %collective-permute-start.1 = (f32[4,128]{1,0:T(4,128)S(1)}, f32[4,128]{1,0:T(4,128)S(1)}, u32[]{:S(2)}, u32[]{:S(2)}) collective-permute-start(f32[4,128]{1,0:T(4,128)S(1)} %get-tuple-element.27), channel_id=1, source_target_pairs={{0,18},{1,17},{2,16},{3,19},{16,2},{17,1},{18,0},{19,3},{4,22},{5,... | collective-permute-start | bytes 6152 | tf_op jit(solution)/shard_map/ppermute | solution.py:265
  5.0 5.4 %collective-permute-start.3 = (bf16[4,128,128]{2,1,0:T(8,128)(2,1)S(1)}, bf16[4,128,128]{2,1,0:T(8,128)(2,1)S(1)}, u32[]{:S(2)}, u32[]{:S(2)}) collective-permute-start(bf16[4,128,128]{2,1,0:T(8,128)(2,1)S(1)} %get-tuple-element.32), channel_id=1, source_target_pairs={{0,16},{1,19},{2,18},{3,17},{16,0},{17,3},{18,2},{19,1},{4,20},{5,... | collective-permute-start | bytes 393224 | tf_op jit(solution)/shard_map/ppermute | solution.py:265
  9.6 1.9 %collective-permute-start.2 = (bf16[4,128,128]{2,1,0:T(8,128)(2,1)S(1)}, bf16[4,128,128]{2,1,0:T(8,128)(2,1)S(1)}, u32[]{:S(2)}, u32[]{:S(2)}) collective-permute-start(bf16[4,128,128]{2,1,0:T(8,128)(2,1)S(1)} %multiply_convert_fusion.panel.refs_0_), channel_id=1, source_target_pairs={{0,1},{1,0},{2,3},{3,2},{4,5},{5,4},{6,7},{7,6},{8,9},{9,8},{10,11... | collective-permute-start | bytes 393224 | tf_op jit(solution)/shard_map/ppermute | solution.py:268
  10.4 1.5 %collective-permute-start.4 = (bf16[4,128,128]{2,1,0:T(8,128)(2,1)S(1)}, bf16[4,128,128]{2,1,0:T(8,128)(2,1)S(1)}, u32[]{:S(2)}, u32[]{:S(2)}) collective-permute-start(bf16[4,128,128]{2,1,0:T(8,128)(2,1)S(1)} %collective-permute-done.3.refs_0_.refs_1_), channel_id=1, source_target_pairs={{0,1},{1,0},{2,3},{3,2},{4,5},{5,4},{6,7},{7,6},{8,9},{9,8},{10,11... | collective-permute-start | bytes 393224 | tf_op jit(solution)/shard_map/ppermute | solution.py:268
  13.0 6.4 %collective-permute-start.6 = (bf16[4,128,128]{2,1,0:T(8,128)(2,1)S(1)}, bf16[4,128,128]{2,1,0:T(8,128)(2,1)S(1)}, u32[]{:S(2)}, u32[]{:S(2)}) collective-permute-start(bf16[4,128,128]{2,1,0:T(8,128)(2,1)S(1)} %shard_map.59), channel_id=1, source_target_pairs={{0,4},{1,9},{2,6},{3,11},{4,0},{5,13},{6,2},{7,15},{8,12},{9,1},{1... | collective-permute-start | bytes 393224 | tf_op jit(solution)/shard_map/ppermute | solution.py:351
  15.7 6.6 %collective-permute-start.5 = (bf16[4,128,128]{2,1,0:T(8,128)(2,1)S(1)}, bf16[4,128,128]{2,1,0:T(8,128)(2,1)S(1)}, u32[]{:S(2)}, u32[]{:S(2)}) collective-permute-start(bf16[4,128,128]{2,1,0:T(8,128)(2,1)S(1)} %shard_map.60), channel_id=1, source_target_pairs={{0,4},{1,9},{2,6},{3,11},{4,0},{5,13},{6,2},{7,15},{8,12},{9,1},{1... | collective-permute-start | bytes 393224 | tf_op jit(solution)/shard_map/ppermute | solution.py:351
  19.5 6.9 %collective-permute-start.7 = (bf16[4,128,128]{2,1,0:T(8,128)(2,1)S(1)}, bf16[4,128,128]{2,1,0:T(8,128)(2,1)S(1)}, u32[]{:S(2)}, u32[]{:S(2)}) collective-permute-start(bf16[4,128,128]{2,1,0:T(8,128)(2,1)S(1)} %add_convert_fusion), channel_id=1, source_target_pairs={{0,8},{1,5},{2,10},{3,7},{4,12},{5,1},{6,14},{7,3},{8,0},{9,13},{1... | collective-permute-start | bytes 393224 | tf_op jit(solution)/shard_map/ppermute | solution.py:351
where the time goes:
time: 26.8 us; the launch traced here: 27.1 us
  starting transfers between devices  11 us (41%)
  Pallas kernels  9.28 us (35%)
  waiting for transfers between devices  6.41 us (24%)
  other arithmetic  0.28 us (1%)
    ppermute x3, waiting for transfers between devices, turned(): return lax.ppermute(value, ('grp', 'blk'), pairs)  5.98 us
    ppermute x3, starting transfers between devices, across(): return lax.ppermute(value, ('side', 'blk'), pairs)  5.92 us
    ppermute x3, starting transfers between devices, turned(): return lax.ppermute(value, ('grp', 'blk'), pairs)  4.52 us
    pallas_call x1, Pallas kernels, stage_blocks(): pl.pallas_call(functools.partial(stage_kernel, blks, groups, tiles_dev),...  2.46 us
    pallas_call x1, Pallas kernels, shards(): pl.pallas_call(rest_kernel, out_shape=[jax.ShapeDtypeStruct(part, jnp.flo...  1.65 us
    pallas_call x1, Pallas kernels, shards(): pl.pallas_call(first_kernel, out_shape=jax.ShapeDtypeStruct(part, jnp.bfl...  1.14 us
    pallas_call x1, Pallas kernels, shards(): pl.pallas_call(far_kernel, out_shape=jax.ShapeDtypeStruct((far_tiles, til...  1.1 us
    pallas_call x1, Pallas kernels, scale_rows(): pl.pallas_call(scale_kernel, out_shape=[jax.ShapeDtypeStruct(codes.shape,...  1 us
  transfers between devices with their start and end apart: 8, of which 5 were waited for; matrix products, arithmetic and copies ran while one was open for 1% of the time, Pallas kernels for 28%

commit v1 on v0

--- a/solution.py
+++ b/solution.py
@@ -8,7 +8,8 @@
 from jax.sharding import PartitionSpec as P
 
 UNROLL = 8
-STAGES = 5
+BATCHES = (4, 4, 4, 8, 8)
+STAGES = len(BATCHES)
 VMEM = pl.BlockSpec(memory_space=pltpu.VMEM)
 SMEM = pl.BlockSpec(memory_space=pltpu.SMEM)
 HBM = pl.BlockSpec(memory_space=pltpu.HBM)
@@ -134,7 +135,7 @@
         word = pack(listed[0:1] + (listed[1:2] << 7), listed[2:3], listed[3:4])
         count = jnp.sum((stage == at).astype(jnp.int32), axis=1, keepdims=True)
         word = jnp.where(lanes < count, word, pack(0, 0, top))
-        batches = split(count + (UNROLL - 1), UNROLL)[0]
+        batches = split(count + (BATCHES[at] - 1), BATCHES[at])[0]
         order_ref[at : at + 1, :] = jnp.where(lanes == width - UNROLL, batches, word)
     copy.wait()
 
@@ -172,8 +173,8 @@
     @pl.loop(0, order_ref[stage, order_ref.shape[1] - UNROLL])
     def _(batch):
         made = []
-        for part in range(UNROLL):
-            slot, row, target = unpack(order_ref[stage, batch * UNROLL + part])
+        for part in range(BATCHES[stage]):
+            slot, row, target = unpack(order_ref[stage, batch * BATCHES[stage] + part])
             product = jnp.dot(blocks[slot], source[row], preferred_element_type=jnp.float32)
             made.append((target, product))
         for target, product in made:

time: 26.8 us -> 27.6 us (1.030); the launches traced: 27.1 us -> 27.3 us
  transfers between devices with their start and end apart: 8 -> 8, of which waited for: 5 -> 5; matrix products, arithmetic and copies ran while one was open for 1% -> 1% of each run, Pallas kernels for 28% -> 27%
where the time goes in v1:
time: 27.6 us; the launch traced here: 27.3 us
  starting transfers between devices  11.1 us (40%)
  Pallas kernels  9.15 us (33%)
  waiting for transfers between devices  6.64 us (24%)
  other arithmetic  0.28 us (1%)
    ppermute x3, waiting for transfers between devices, turned(): return lax.ppermute(value, ('grp', 'blk'), pairs)  6.21 us
    ppermute x3, starting transfers between devices, across(): return lax.ppermute(value, ('side', 'blk'), pairs)  5.92 us
    ppermute x3, starting transfers between devices, turned(): return lax.ppermute(value, ('grp', 'blk'), pairs)  4.65 us
    pallas_call x1, Pallas kernels, stage_blocks(): pl.pallas_call(functools.partial(stage_kernel, blks, groups, tiles_dev),...  2.46 us
    pallas_call x1, Pallas kernels, shards(): pl.pallas_call(rest_kernel, out_shape=[jax.ShapeDtypeStruct(part, jnp.flo...  1.42 us
    pallas_call x1, Pallas kernels, shards(): pl.pallas_call(far_kernel, out_shape=jax.ShapeDtypeStruct((far_tiles, til...  1.19 us
    pallas_call x1, Pallas kernels, shards(): pl.pallas_call(first_kernel, out_shape=jax.ShapeDtypeStruct(part, jnp.bfl...  1.15 us
    pallas_call x1, Pallas kernels, scale_rows(): pl.pallas_call(scale_kernel, out_shape=[jax.ShapeDtypeStruct(codes.shape,...  1 us
  transfers between devices with their start and end apart: 8, of which 5 were waited for; matrix products, arithmetic and copies ran while one was open for 1% of the time, Pallas kernels for 27%

profile of v1, /device:TPU:0, one launch (start us, length us, event | category | flops | bytes accessed | tf_op | source)
XLA Modules:
  0.0 27.3 jit_solution(788298104009947937)
XLA Ops:
  0.0 3.9 %collective-permute-start = (bf16[4,128,128]{2,1,0:T(8,128)(2,1)}, bf16[4,128,128]{2,1,0:T(8,128)(2,1)S(1)}, u32[]{:S(2)}, u32[]{:S(2)}) collective-permute-start(bf16[4,128,128]{2,1,0:T(8,128)(2,1)} %bitcast.7), channel_id=1, source_target_pairs={{0,18},{1,17},{2,16},{3,19},{16,2},{17,1},{18,0},{19,3},{4,22},{5,... | collective-permute-start | bytes 393224 | tf_op jit(solution)/shard_map/ppermute | solution.py:266
  3.9 1.0 %shard_map.55 = (bf16[4,128,128]{2,1,0:T(8,128)(2,1)S(1)}, f32[4,128,128]{2,1,0:T(8,128)S(1)}, f32[4,128]{1,0:T(4,128)S(1)}) custom-call(s32[1,4]{1,0:T(1,128)} %exps_hbm.1, s32[1,512]{1,0:T(1,128)} %degrees_hbm.1, bf16[4,128,128]{2,1,0:T(8,128)(2,1)} %bitcast.8), custom_call_target="tpu_custom_call" | custom-call | flops 65536 | bytes 262144 | tf_op jit(solution)/shard_map/pallas_call | solution.py:56
  4.9 0.1 collective-permute-start.1
  5.0 2.0 %collective-permute-start.3 = (bf16[4,128,128]{2,1,0:T(8,128)(2,1)S(1)}, bf16[4,128,128]{2,1,0:T(8,128)(2,1)S(1)}, u32[]{:S(2)}, u32[]{:S(2)}) collective-permute-start(bf16[4,128,128]{2,1,0:T(8,128)(2,1)S(1)} %get-tuple-element.32), channel_id=1, source_target_pairs={{0,16},{1,19},{2,18},{3,17},{16,0},{17,3},{18,2},{19,1},{4,20},{5,... | collective-permute-start | bytes 393224 | tf_op jit(solution)/shard_map/ppermute | solution.py:266
  6.9 0.1 pad_add_fusion.place_ref
  7.0 2.5 %shard_map.56 = (s32[8,128]{1,0:T(8,128)S(1)}, bf16[96,128,128]{2,1,0:T(8,128)(2,1)S(1)}) custom-call(s32[2]{0:T(128)S(1)} %pad_add_fusion.place_ref, s32[2,96]{1,0:T(2,128)} %bitcast.9, bf16[96,128,128]{2,1,0:T(8,128)(2,1)} %bitcast.6), custom_call_target="tpu_custom_call" | custom-call | tf_op jit(solution)/shard_map/pallas_call | solution.py:155
  9.5 0.0 collective-permute-done
  9.5 0.1 multiply_convert_fusion.panel.refs_0_
  9.6 0.1 collective-permute-start.2
  9.7 0.6 %shard_map.57.refs_2_ = f32[5,128,128]{2,1,0:T(8,128)S(1)} custom-call(s32[8,128]{1,0:T(8,128)S(1)} %get-tuple-element.40.order_ref, bf16[4,128,128]{2,1,0:T(8,128)(2,1)S(1)} %multiply_convert_fusion.panel.refs_0_, bf16[96,128,128]{2,1,0:T(8,128)(2,1)S(1)} %get-tuple-element.33.blocks.refs_1_.refs_2_.refs_4_), custom_call_target="tpu_custom_call" | custom-call | flops 50331648 | bytes 393216 | tf_op jit(solution)/shard_map/pallas_call | solution.py:284
  10.4 0.1 collective-permute-done.3.refs_0_.refs_1_
  10.4 0.5 %collective-permute-start.4 = (bf16[4,128,128]{2,1,0:T(8,128)(2,1)S(1)}, bf16[4,128,128]{2,1,0:T(8,128)(2,1)S(1)}, u32[]{:S(2)}, u32[]{:S(2)}) collective-permute-start(bf16[4,128,128]{2,1,0:T(8,128)(2,1)S(1)} %collective-permute-done.3.refs_0_.refs_1_), channel_id=1, source_target_pairs={{0,1},{1,0},{2,3},{3,2},{4,5},{5,4},{6,7},{7,6},{8,9},{9,8},{10,11... | collective-permute-start | bytes 393224 | tf_op jit(solution)/shard_map/ppermute | solution.py:269
  10.9 0.6 %shard_map.58.refs_3_ = f32[5,128,128]{2,1,0:T(8,128)S(1)} custom-call(s32[8,128]{1,0:T(8,128)S(1)} %get-tuple-element.40.order_ref, bf16[4,128,128]{2,1,0:T(8,128)(2,1)S(1)} %collective-permute-done.3.refs_0_.refs_1_, bf16[96,128,128]{2,1,0:T(8,128)(2,1)S(1)} %get-tuple-element.33.blocks.refs_1_.refs_2_.refs_4_, ...), custom_call_target="tpu_custom_call", output_to_operand_aliasing={{}: (3, {})} | custom-call | flops 50331648 | bytes 393216 | tf_op jit(solution)/shard_map/pallas_call | solution.py:294
  11.6 0.4 %collective-permute-done.4.refs_1_.refs_3_ = bf16[4,128,128]{2,1,0:T(8,128)(2,1)S(1)} collective-permute-done((bf16[4,128,128]{2,1,0:T(8,128)(2,1)S(1)}, bf16[4,128,128]{2,1,0:T(8,128)(2,1)S(1)}, u32[]{:S(2)}, u32[]{:S(2)}) %collective-permute-start.4) | collective-permute-done | bytes 131104 | tf_op jit(solution)/shard_map/ppermute | solution.py:269
  11.9 1.2 %shard_map.59 = bf16[4,128,128]{2,1,0:T(8,128)(2,1)S(1)} custom-call(s32[8,128]{1,0:T(8,128)S(1)} %get-tuple-element.40.order_ref, bf16[4,128,128]{2,1,0:T(8,128)(2,1)S(1)} %collective-permute-done.2.refs_0_.refs_2_, bf16[4,128,128]{2,1,0:T(8,128)(2,1)S(1)} %collective-permute-done.4.refs_1_.refs_3_, ...), custom_call_target="tpu_custom_call" | custom-call | flops 50331648 | bytes 393216 | tf_op jit(solution)/shard_map/pallas_call | solution.py:305
  13.1 1.8 %collective-permute-start.6 = (bf16[4,128,128]{2,1,0:T(8,128)(2,1)S(1)}, bf16[4,128,128]{2,1,0:T(8,128)(2,1)S(1)}, u32[]{:S(2)}, u32[]{:S(2)}) collective-permute-start(bf16[4,128,128]{2,1,0:T(8,128)(2,1)S(1)} %shard_map.59), channel_id=1, source_target_pairs={{0,4},{1,9},{2,6},{3,11},{4,0},{5,13},{6,2},{7,15},{8,12},{9,1},{1... | collective-permute-start | bytes 393224 | tf_op jit(solution)/shard_map/ppermute | solution.py:352
  14.9 1.1 %shard_map.60 = bf16[4,128,128]{2,1,0:T(8,128)(2,1)S(1)} custom-call(s32[8,128]{1,0:T(8,128)S(1)} %get-tuple-element.40.order_ref, bf16[4,128,128]{2,1,0:T(8,128)(2,1)S(1)} %multiply_convert_fusion.panel.refs_0_, bf16[4,128,128]{2,1,0:T(8,128)(2,1)S(1)} %collective-permute-done.3.refs_0_.refs_1_, ...), custom_call_target="tpu_custom_call" | custom-call | flops 100663296 | bytes 786432 | tf_op jit(solution)/shard_map/pallas_call | solution.py:316
  16.1 0.3 %collective-permute-start.5 = (bf16[4,128,128]{2,1,0:T(8,128)(2,1)S(1)}, bf16[4,128,128]{2,1,0:T(8,128)(2,1)S(1)}, u32[]{:S(2)}, u32[]{:S(2)}) collective-permute-start(bf16[4,128,128]{2,1,0:T(8,128)(2,1)S(1)} %shard_map.60), channel_id=1, source_target_pairs={{0,4},{1,9},{2,6},{3,11},{4,0},{5,13},{6,2},{7,15},{8,12},{9,1},{1... | collective-permute-start | bytes 393224 | tf_op jit(solution)/shard_map/ppermute | solution.py:352
  16.4 1.4 %shard_map.61 = (f32[4,128,128]{2,1,0:T(8,128)S(1)}, f32[4,128,128]{2,1,0:T(8,128)S(1)}) custom-call(s32[8,128]{1,0:T(8,128)S(1)} %get-tuple-element.40.order_ref, bf16[4,128,128]{2,1,0:T(8,128)(2,1)S(1)} %multiply_convert_fusion.panel.refs_0_, bf16[4,128,128]{2,1,0:T(8,128)(2,1)S(1)} %collective-permute-done.3.refs_0_.refs_1_, ...), custom_call_target="tpu_custom_call" | custom-call | flops 201326592 | bytes 1572864 | tf_op jit(solution)/shard_map/pallas_call | solution.py:329
  17.8 1.7 %collective-permute-done.6 = bf16[4,128,128]{2,1,0:T(8,128)(2,1)S(1)} collective-permute-done((bf16[4,128,128]{2,1,0:T(8,128)(2,1)S(1)}, bf16[4,128,128]{2,1,0:T(8,128)(2,1)S(1)}, u32[]{:S(2)}, u32[]{:S(2)}) %collective-permute-start.6) | collective-permute-done | bytes 131104 | tf_op jit(solution)/shard_map/ppermute | solution.py:352
  19.6 2.5 %collective-permute-start.7 = (bf16[4,128,128]{2,1,0:T(8,128)(2,1)S(1)}, bf16[4,128,128]{2,1,0:T(8,128)(2,1)S(1)}, u32[]{:S(2)}, u32[]{:S(2)}) collective-permute-start(bf16[4,128,128]{2,1,0:T(8,128)(2,1)S(1)} %add_convert_fusion), channel_id=1, source_target_pairs={{0,8},{1,5},{2,10},{3,7},{4,12},{5,1},{6,14},{7,3},{8,0},{9,13},{1... | collective-permute-start | bytes 393224 | tf_op jit(solution)/shard_map/ppermute | solution.py:352
  22.1 0.4 %collective-permute-done.5 = bf16[4,128,128]{2,1,0:T(8,128)(2,1)S(1)} collective-permute-done((bf16[4,128,128]{2,1,0:T(8,128)(2,1)S(1)}, bf16[4,128,128]{2,1,0:T(8,128)(2,1)S(1)}, u32[]{:S(2)}, u32[]{:S(2)}) %collective-permute-start.5) | collective-permute-done | bytes 131104 | tf_op jit(solution)/shard_map/ppermute | solution.py:352
  22.5 4.1 %collective-permute-done.7.refs_0_ = bf16[4,128,128]{2,1,0:T(8,128)(2,1)S(1)} collective-permute-done((bf16[4,128,128]{2,1,0:T(8,128)(2,1)S(1)}, bf16[4,128,128]{2,1,0:T(8,128)(2,1)S(1)}, u32[]{:S(2)}, u32[]{:S(2)}) %collective-permute-start.7) | collective-permute-done | bytes 131104 | tf_op jit(solution)/shard_map/ppermute | solution.py:352
  26.6 0.7 %shard_map.62 = bf16[4,128,128]{2,1,0:T(8,128)(2,1)} custom-call(f32[4,128,128]{2,1,0:T(8,128)S(1)} %get-tuple-element.26.factors, f32[4,128,128]{2,1,0:T(8,128)S(1)} %convert_add_fusion.own, bf16[4,128,128]{2,1,0:T(8,128)(2,1)S(1)} %collective-permute-done.7.refs_0_), custom_call_target="tpu_custom_call" | custom-call | tf_op jit(solution)/shard_map/pallas_call | solution.py:372
  (4 shorter events, 0.1 us)
Async XLA Ops:
  0.0 9.5 %collective-permute-start = (bf16[4,128,128]{2,1,0:T(8,128)(2,1)}, bf16[4,128,128]{2,1,0:T(8,128)(2,1)S(1)}, u32[]{:S(2)}, u32[]{:S(2)}) collective-permute-start(bf16[4,128,128]{2,1,0:T(8,128)(2,1)} %bitcast.7), channel_id=1, source_target_pairs={{0,18},{1,17},{2,16},{3,19},{16,2},{17,1},{18,0},{19,3},{4,22},{5,... | collective-permute-start | bytes 393224 | tf_op jit(solution)/shard_map/ppermute | solution.py:266
  4.9 4.6 %collective-permute-start.1 = (f32[4,128]{1,0:T(4,128)S(1)}, f32[4,128]{1,0:T(4,128)S(1)}, u32[]{:S(2)}, u32[]{:S(2)}) collective-permute-start(f32[4,128]{1,0:T(4,128)S(1)} %get-tuple-element.27), channel_id=1, source_target_pairs={{0,18},{1,17},{2,16},{3,19},{16,2},{17,1},{18,0},{19,3},{4,22},{5,... | collective-permute-start | bytes 6152 | tf_op jit(solution)/shard_map/ppermute | solution.py:266
  5.0 5.4 %collective-permute-start.3 = (bf16[4,128,128]{2,1,0:T(8,128)(2,1)S(1)}, bf16[4,128,128]{2,1,0:T(8,128)(2,1)S(1)}, u32[]{:S(2)}, u32[]{:S(2)}) collective-permute-start(bf16[4,128,128]{2,1,0:T(8,128)(2,1)S(1)} %get-tuple-element.32), channel_id=1, source_target_pairs={{0,16},{1,19},{2,18},{3,17},{16,0},{17,3},{18,2},{19,1},{4,20},{5,... | collective-permute-start | bytes 393224 | tf_op jit(solution)/shard_map/ppermute | solution.py:266
  9.6 1.9 %collective-permute-start.2 = (bf16[4,128,128]{2,1,0:T(8,128)(2,1)S(1)}, bf16[4,128,128]{2,1,0:T(8,128)(2,1)S(1)}, u32[]{:S(2)}, u32[]{:S(2)}) collective-permute-start(bf16[4,128,128]{2,1,0:T(8,128)(2,1)S(1)} %multiply_convert_fusion.panel.refs_0_), channel_id=1, source_target_pairs={{0,1},{1,0},{2,3},{3,2},{4,5},{5,4},{6,7},{7,6},{8,9},{9,8},{10,11... | collective-permute-start | bytes 393224 | tf_op jit(solution)/shard_map/ppermute | solution.py:269
  10.4 1.5 %collective-permute-start.4 = (bf16[4,128,128]{2,1,0:T(8,128)(2,1)S(1)}, bf16[4,128,128]{2,1,0:T(8,128)(2,1)S(1)}, u32[]{:S(2)}, u32[]{:S(2)}) collective-permute-start(bf16[4,128,128]{2,1,0:T(8,128)(2,1)S(1)} %collective-permute-done.3.refs_0_.refs_1_), channel_id=1, source_target_pairs={{0,1},{1,0},{2,3},{3,2},{4,5},{5,4},{6,7},{7,6},{8,9},{9,8},{10,11... | collective-permute-start | bytes 393224 | tf_op jit(solution)/shard_map/ppermute | solution.py:269
  13.1 6.4 %collective-permute-start.6 = (bf16[4,128,128]{2,1,0:T(8,128)(2,1)S(1)}, bf16[4,128,128]{2,1,0:T(8,128)(2,1)S(1)}, u32[]{:S(2)}, u32[]{:S(2)}) collective-permute-start(bf16[4,128,128]{2,1,0:T(8,128)(2,1)S(1)} %shard_map.59), channel_id=1, source_target_pairs={{0,4},{1,9},{2,6},{3,11},{4,0},{5,13},{6,2},{7,15},{8,12},{9,1},{1... | collective-permute-start | bytes 393224 | tf_op jit(solution)/shard_map/ppermute | solution.py:352
  16.1 6.4 %collective-permute-start.5 = (bf16[4,128,128]{2,1,0:T(8,128)(2,1)S(1)}, bf16[4,128,128]{2,1,0:T(8,128)(2,1)S(1)}, u32[]{:S(2)}, u32[]{:S(2)}) collective-permute-start(bf16[4,128,128]{2,1,0:T(8,128)(2,1)S(1)} %shard_map.60), channel_id=1, source_target_pairs={{0,4},{1,9},{2,6},{3,11},{4,0},{5,13},{6,2},{7,15},{8,12},{9,1},{1... | collective-permute-start | bytes 393224 | tf_op jit(solution)/shard_map/ppermute | solution.py:352
  19.6 7.0 %collective-permute-start.7 = (bf16[4,128,128]{2,1,0:T(8,128)(2,1)S(1)}, bf16[4,128,128]{2,1,0:T(8,128)(2,1)S(1)}, u32[]{:S(2)}, u32[]{:S(2)}) collective-permute-start(bf16[4,128,128]{2,1,0:T(8,128)(2,1)S(1)} %add_convert_fusion), channel_id=1, source_target_pairs={{0,8},{1,5},{2,10},{3,7},{4,12},{5,1},{6,14},{7,3},{8,0},{9,13},{1... | collective-permute-start | bytes 393224 | tf_op jit(solution)/shard_map/ppermute | solution.py:352

commit v2 on v1

--- a/solution.py
+++ b/solution.py
@@ -8,7 +8,7 @@
 from jax.sharding import PartitionSpec as P
 
 UNROLL = 8
-BATCHES = (4, 4, 4, 8, 8)
+BATCHES = (4, 4, 4, 8, 8, 8)
 STAGES = len(BATCHES)
 VMEM = pl.BlockSpec(memory_space=pltpu.VMEM)
 SMEM = pl.BlockSpec(memory_space=pltpu.SMEM)
@@ -106,9 +106,9 @@
     far = (chunk >= 2) & ((chunk & 1) == 1)
     kept = jnp.where(chunk == 1, 1 + role * (groups // 2 - 1), (chunk >> 1) + 1 - role)
     kept = jnp.where(chunk == 0, 0, jnp.where(far, (chunk >> 1) - 1, kept))
-    stage = jnp.where(far, jnp.where(odd == 1, 2, jnp.minimum(rank, 1)), 4)
-    stage = jnp.where(far | (kept != 1), stage, 3)
-    kept = jnp.where(far, kept, jnp.where(stage == 3, 0, kept - (kept > 1).astype(jnp.int32)))
+    stage = jnp.where(far, jnp.where(odd == 1, 2, jnp.minimum(rank, 1)), 5)
+    stage = jnp.where(far | (kept != 1), stage, 4 - role)
+    kept = jnp.where(far | (kept == 0), kept, kept - 1)
     stage = jnp.where(origin < source_tiles, stage, STAGES)
     panel = jnp.where(stage == 1, rank - 1, jnp.where(stage == 2, rank, rank + odd * half))
     slot = count_up((1, capacity), 1)
@@ -124,7 +124,7 @@
         jnp.where(count_up((8, capacity), 0) == at, part, 0) for at, part in enumerate(parts)
     ).astype(jnp.bfloat16)
     far_tiles = (groups // 2 - 1) * tiles_dev
-    tops = [far_tiles] * 3 + [tiles_dev, groups // 2 * tiles_dev]
+    tops = [far_tiles] * 3 + [tiles_dev] * 2 + [groups // 2 * tiles_dev]
     lanes = count_up((1, width), 1)
     for at, top in enumerate(tops):
         where = jnp.where(stage == at, position, -1)
@@ -198,18 +198,20 @@
     add_products(1, order_ref, blocks, source, total)
 
 
-def far_kernel(order_ref, *refs):
-    *panels, blocks, total, far, source = refs
+def far_kernel(tiles_dev, order_ref, *refs):
+    *panels, blocks, _, far, first, total, source = refs
+    others = len(panels) // 2 * tiles_dev
     gather_panels(panels, source)
-    add_products(2, order_ref, blocks, source, total)
+    first[...] = jnp.zeros_like(first)
+    add_products(2, order_ref, blocks, source.at[others:], total)
+    add_products(3, order_ref, blocks, source, first)
     far[...] = total[: far.shape[0]].astype(far.dtype)
 
 
 def first_kernel(order_ref, *refs):
-    *panels, blocks, first, source, total = refs
+    *panels, blocks, _, first, total, source = refs
     gather_panels(panels, source)
-    total[...] = jnp.zeros_like(total)
-    add_products(3, order_ref, blocks, source, total)
+    add_products(4, order_ref, blocks, source, total)
     first[...] = total[: first.shape[0]].astype(first.dtype)
 
 
@@ -217,7 +219,7 @@
     *panels, blocks, own, later, source, total = refs
     gather_panels(panels, source)
     total[...] = jnp.zeros_like(total)
-    add_products(4, order_ref, blocks, source, total)
+    add_products(5, order_ref, blocks, source, total)
     tiles_dev = own.shape[0]
     own[...] = total[:tiles_dev]
     later[...] = total[tiles_dev : tiles_dev + later.shape[0]]
@@ -302,29 +304,35 @@
         cost_estimate=cost_of(capacity // 8, tile_rows, row_width),
     )(order, *middle, blocks, total)
     *others, total = lax.optimization_barrier((*others, total))
-    far = pl.pallas_call(
-        far_kernel,
-        out_shape=jax.ShapeDtypeStruct((far_tiles, tile_rows, row_width), jnp.bfloat16),
-        in_specs=[SMEM] + [VMEM] * (len(others) + 2),
-        out_specs=VMEM,
-        scratch_shapes=[held(len(others) * tiles_dev, jnp.bfloat16)],
+    panels = [early] + middle + others
+    far, first, _ = pl.pallas_call(
+        functools.partial(far_kernel, tiles_dev),
+        out_shape=[
+            jax.ShapeDtypeStruct((far_tiles, tile_rows, row_width), jnp.bfloat16),
+            jax.ShapeDtypeStruct((tiles_dev + 1, tile_rows, row_width), jnp.float32),
+            jax.ShapeDtypeStruct(total.shape, total.dtype),
+        ],
+        in_specs=[SMEM] + [VMEM] * (len(panels) + 2),
+        out_specs=[VMEM] * 3,
+        input_output_aliases={len(panels) + 2: 2},
+        scratch_shapes=[held(len(panels) * tiles_dev, jnp.bfloat16)],
         compiler_params=LIMIT,
         cost_estimate=cost_of(capacity // 8, tile_rows, row_width),
-    )(order, *others, blocks, total)
+    )(order, *panels, blocks, total)
     far, order = lax.optimization_barrier((far, order))
-    panels = [early] + middle + others
-    first = pl.pallas_call(
+    first, _ = pl.pallas_call(
         first_kernel,
-        out_shape=jax.ShapeDtypeStruct(part, jnp.bfloat16),
-        in_specs=[SMEM] + [VMEM] * (len(panels) + 1),
-        out_specs=VMEM,
-        scratch_shapes=[
-            held(len(panels) * tiles_dev, jnp.bfloat16),
-            held(tiles_dev + 1, jnp.float32),
-        ],
+        out_shape=[
+            jax.ShapeDtypeStruct(part, jnp.bfloat16),
+            jax.ShapeDtypeStruct(first.shape, first.dtype),
+        ],
+        in_specs=[SMEM] + [VMEM] * (len(panels) + 2),
+        out_specs=[VMEM] * 2,
+        input_output_aliases={len(panels) + 2: 1},
+        scratch_shapes=[held(len(panels) * tiles_dev, jnp.bfloat16)],
         compiler_params=LIMIT,
         cost_estimate=cost_of(capacity // 4, tile_rows, row_width),
-    )(order, *panels, blocks)
+    )(order, *panels, blocks, first)
     first, order = lax.optimization_barrier((first, order))
     own, later = pl.pallas_call(
         rest_kernel,

time: 27.6 us -> 28 us (1.014); the launches traced: 27.3 us -> 28.5 us
  Pallas kernels: 9.15 us -> 10.2 us
    pallas_call x2, Pallas kernels: 2.34 us -> 2.97 us  [the longest x1 1.61 us: shards(): pl.pallas_call(functools.partial(far_kernel, tiles_dev), out_shape=[jax.S...]
    pallas_call x1, Pallas kernels: 1.42 us -> 1.89 us  [shards(): pl.pallas_call(rest_kernel, out_shape=[jax.ShapeDtypeStruct(part, jnp.flo...]
    ppermute x2, starting transfers between devices: 0.58 us -> 0.94 us  [paired(): lax.ppermute(value, axis, [(at, at ^ hop) for at in range(lax.axis_size(a...]
  transfers between devices with their start and end apart: 8 -> 8, of which waited for: 5 -> 4; matrix products, arithmetic and copies ran while one was open for 1% -> 1% of each run, Pallas kernels for 27% -> 28%
where the time goes in v2:
time: 28 us; the launch traced here: 28.5 us
  starting transfers between devices  11.3 us (40%)
  Pallas kernels  10.2 us (36%)
  waiting for transfers between devices  6.51 us (23%)
    ppermute x3, waiting for transfers between devices, turned(): return lax.ppermute(value, ('grp', 'blk'), pairs)  6.08 us
    ppermute x3, starting transfers between devices, across(): return lax.ppermute(value, ('side', 'blk'), pairs)  5.92 us
    ppermute x3, starting transfers between devices, turned(): return lax.ppermute(value, ('grp', 'blk'), pairs)  4.46 us
    pallas_call x1, Pallas kernels, stage_blocks(): pl.pallas_call(functools.partial(stage_kernel, blks, groups, tiles_dev),...  2.46 us
    pallas_call x1, Pallas kernels, shards(): pl.pallas_call(rest_kernel, out_shape=[jax.ShapeDtypeStruct(part, jnp.flo...  1.89 us
    pallas_call x1, Pallas kernels, shards(): pl.pallas_call(functools.partial(far_kernel, tiles_dev), out_shape=[jax.S...  1.61 us
    pallas_call x1, Pallas kernels, shards(): pl.pallas_call(first_kernel, out_shape=[jax.ShapeDtypeStruct(part, jnp.bf...  1.36 us
    pallas_call x1, Pallas kernels, scale_rows(): pl.pallas_call(scale_kernel, out_shape=[jax.ShapeDtypeStruct(codes.shape,...  1 us
  transfers between devices with their start and end apart: 8, of which 4 were waited for; matrix products, arithmetic and copies ran while one was open for 1% of the time, Pallas kernels for 28%

profile of v2, /device:TPU:0, one launch (start us, length us, event | category | flops | bytes accessed | tf_op | source)
XLA Modules:
  0.0 28.5 jit_solution(9455887583507182470)
XLA Ops:
  0.0 3.9 %collective-permute-start = (bf16[4,128,128]{2,1,0:T(8,128)(2,1)}, bf16[4,128,128]{2,1,0:T(8,128)(2,1)S(1)}, u32[]{:S(2)}, u32[]{:S(2)}) collective-permute-start(bf16[4,128,128]{2,1,0:T(8,128)(2,1)} %bitcast.7), channel_id=1, source_target_pairs={{0,18},{1,17},{2,16},{3,19},{16,2},{17,1},{18,0},{19,3},{4,22},{5,... | collective-permute-start | bytes 393224 | tf_op jit(solution)/shard_map/ppermute | solution.py:268
  3.9 1.0 %shard_map.55 = (bf16[4,128,128]{2,1,0:T(8,128)(2,1)S(1)}, f32[4,128,128]{2,1,0:T(8,128)S(1)}, f32[4,128]{1,0:T(4,128)S(1)}) custom-call(s32[1,4]{1,0:T(1,128)} %exps_hbm.1, s32[1,512]{1,0:T(1,128)} %degrees_hbm.1, bf16[4,128,128]{2,1,0:T(8,128)(2,1)} %bitcast.8), custom_call_target="tpu_custom_call" | custom-call | flops 65536 | bytes 262144 | tf_op jit(solution)/shard_map/pallas_call | solution.py:56
  4.9 0.1 collective-permute-start.1
  5.0 2.0 %collective-permute-start.2 = (bf16[4,128,128]{2,1,0:T(8,128)(2,1)S(1)}, bf16[4,128,128]{2,1,0:T(8,128)(2,1)S(1)}, u32[]{:S(2)}, u32[]{:S(2)}) collective-permute-start(bf16[4,128,128]{2,1,0:T(8,128)(2,1)S(1)} %get-tuple-element.35), channel_id=1, source_target_pairs={{0,16},{1,19},{2,18},{3,17},{16,0},{17,3},{18,2},{19,1},{4,20},{5,... | collective-permute-start | bytes 393224 | tf_op jit(solution)/shard_map/ppermute | solution.py:268
  6.9 0.1 pad_add_fusion.place_ref
  7.0 2.5 %shard_map.56 = (s32[8,128]{1,0:T(8,128)S(1)}, bf16[96,128,128]{2,1,0:T(8,128)(2,1)S(1)}) custom-call(s32[2]{0:T(128)S(1)} %pad_add_fusion.place_ref, s32[2,96]{1,0:T(2,128)} %bitcast.9, bf16[96,128,128]{2,1,0:T(8,128)(2,1)} %bitcast.6), custom_call_target="tpu_custom_call" | custom-call | tf_op jit(solution)/shard_map/pallas_call | solution.py:155
  9.5 0.0 collective-permute-done
  9.5 0.1 multiply_convert_fusion.panel.refs_0_
  9.6 0.1 collective-permute-start.3
  9.7 0.6 %shard_map.57.refs_2_ = f32[5,128,128]{2,1,0:T(8,128)S(1)} custom-call(s32[8,128]{1,0:T(8,128)S(1)} %get-tuple-element.46.order_ref, bf16[4,128,128]{2,1,0:T(8,128)(2,1)S(1)} %multiply_convert_fusion.panel.refs_0_, bf16[96,128,128]{2,1,0:T(8,128)(2,1)S(1)} %get-tuple-element.36.blocks.refs_1_.refs_4_), custom_call_target="tpu_custom_call" | custom-call | flops 50331648 | bytes 393216 | tf_op jit(solution)/shard_map/pallas_call | solution.py:286
  10.4 0.1 collective-permute-done.2.refs_0_.refs_1_
  10.4 0.9 %collective-permute-start.4 = (bf16[4,128,128]{2,1,0:T(8,128)(2,1)S(1)}, bf16[4,128,128]{2,1,0:T(8,128)(2,1)S(1)}, u32[]{:S(2)}, u32[]{:S(2)}) collective-permute-start(bf16[4,128,128]{2,1,0:T(8,128)(2,1)S(1)} %collective-permute-done.2.refs_0_.refs_1_), channel_id=1, source_target_pairs={{0,1},{1,0},{2,3},{3,2},{4,5},{5,4},{6,7},{7,6},{8,9},{9,8},{10,11... | collective-permute-start | bytes 393224 | tf_op jit(solution)/shard_map/ppermute | solution.py:271
  11.3 0.6 %shard_map.58.refs_5_ = f32[5,128,128]{2,1,0:T(8,128)S(1)} custom-call(s32[8,128]{1,0:T(8,128)S(1)} %get-tuple-element.46.order_ref, bf16[4,128,128]{2,1,0:T(8,128)(2,1)S(1)} %collective-permute-done.2.refs_0_.refs_1_, bf16[96,128,128]{2,1,0:T(8,128)(2,1)S(1)} %get-tuple-element.36.blocks.refs_1_.refs_4_, ...), custom_call_target="tpu_custom_call", output_to_operand_aliasing={{}: (3, {})} | custom-call | flops 50331648 | bytes 393216 | tf_op jit(solution)/shard_map/pallas_call | solution.py:296
  11.9 0.0 collective-permute-done.3.refs_2_
  11.9 0.4 %collective-permute-done.4.refs_3_ = bf16[4,128,128]{2,1,0:T(8,128)(2,1)S(1)} collective-permute-done((bf16[4,128,128]{2,1,0:T(8,128)(2,1)S(1)}, bf16[4,128,128]{2,1,0:T(8,128)(2,1)S(1)}, u32[]{:S(2)}, u32[]{:S(2)}) %collective-permute-start.4) | collective-permute-done | bytes 131104 | tf_op jit(solution)/shard_map/ppermute | solution.py:271
  12.3 1.6 %shard_map.59 = (bf16[4,128,128]{2,1,0:T(8,128)(2,1)S(1)}, f32[5,128,128]{2,1,0:T(8,128)S(1)}, f32[5,128,128]{2,1,0:T(8,128)S(1)}) custom-call(s32[8,128]{1,0:T(8,128)S(1)} %get-tuple-element.46.order_ref, bf16[4,128,128]{2,1,0:T(8,128)(2,1)S(1)} %multiply_convert_fusion.panel.refs_0_, ...), custom_call_target="tpu_custom_call", output_to_operand_aliasing={{2}: (6, {})} | custom-call | flops 50331648 | bytes 393216 | tf_op jit(solution)/shard_map/pallas_call | solution.py:308
  13.9 1.3 %collective-permute-start.6 = (bf16[4,128,128]{2,1,0:T(8,128)(2,1)S(1)}, bf16[4,128,128]{2,1,0:T(8,128)(2,1)S(1)}, u32[]{:S(2)}, u32[]{:S(2)}) collective-permute-start(bf16[4,128,128]{2,1,0:T(8,128)(2,1)S(1)} %get-tuple-element.50), channel_id=1, source_target_pairs={{0,4},{1,9},{2,6},{3,11},{4,0},{5,13},{6,2},{7,15},{8,12},{9,1},{1... | collective-permute-start | bytes 393224 | tf_op jit(solution)/shard_map/ppermute | solution.py:360
  15.2 1.4 %shard_map.60 = (bf16[4,128,128]{2,1,0:T(8,128)(2,1)S(1)}, f32[5,128,128]{2,1,0:T(8,128)S(1)}) custom-call(s32[8,128]{1,0:T(8,128)S(1)} %get-tuple-element.46.order_ref, bf16[4,128,128]{2,1,0:T(8,128)(2,1)S(1)} %multiply_convert_fusion.panel.refs_0_, ...), custom_call_target="tpu_custom_call", output_to_operand_aliasing={{1}: (6, {})} | custom-call | flops 100663296 | bytes 786432 | tf_op jit(solution)/shard_map/pallas_call | solution.py:323
  16.5 0.9 %collective-permute-start.5 = (bf16[4,128,128]{2,1,0:T(8,128)(2,1)S(1)}, bf16[4,128,128]{2,1,0:T(8,128)(2,1)S(1)}, u32[]{:S(2)}, u32[]{:S(2)}) collective-permute-start(bf16[4,128,128]{2,1,0:T(8,128)(2,1)S(1)} %get-tuple-element.48), channel_id=1, source_target_pairs={{0,4},{1,9},{2,6},{3,11},{4,0},{5,13},{6,2},{7,15},{8,12},{9,1},{1... | collective-permute-start | bytes 393224 | tf_op jit(solution)/shard_map/ppermute | solution.py:360
  17.4 1.9 %shard_map.61 = (f32[4,128,128]{2,1,0:T(8,128)S(1)}, f32[4,128,128]{2,1,0:T(8,128)S(1)}) custom-call(s32[8,128]{1,0:T(8,128)S(1)} %get-tuple-element.46.order_ref, bf16[4,128,128]{2,1,0:T(8,128)(2,1)S(1)} %multiply_convert_fusion.panel.refs_0_, bf16[4,128,128]{2,1,0:T(8,128)(2,1)S(1)} %collective-permute-done.2.refs_0_.refs_1_, ...), custom_call_target="tpu_custom_call" | custom-call | flops 201326592 | bytes 1572864 | tf_op jit(solution)/shard_map/pallas_call | solution.py:337
  19.3 1.0 %collective-permute-done.6 = bf16[4,128,128]{2,1,0:T(8,128)(2,1)S(1)} collective-permute-done((bf16[4,128,128]{2,1,0:T(8,128)(2,1)S(1)}, bf16[4,128,128]{2,1,0:T(8,128)(2,1)S(1)}, u32[]{:S(2)}, u32[]{:S(2)}) %collective-permute-start.6) | collective-permute-done | bytes 131104 | tf_op jit(solution)/shard_map/ppermute | solution.py:360
  20.3 2.3 %collective-permute-start.7 = (bf16[4,128,128]{2,1,0:T(8,128)(2,1)S(1)}, bf16[4,128,128]{2,1,0:T(8,128)(2,1)S(1)}, u32[]{:S(2)}, u32[]{:S(2)}) collective-permute-start(bf16[4,128,128]{2,1,0:T(8,128)(2,1)S(1)} %add_convert_fusion), channel_id=1, source_target_pairs={{0,8},{1,5},{2,10},{3,7},{4,12},{5,1},{6,14},{7,3},{8,0},{9,13},{1... | collective-permute-start | bytes 393224 | tf_op jit(solution)/shard_map/ppermute | solution.py:360
  22.7 5.1 %collective-permute-done.7.refs_0_ = bf16[4,128,128]{2,1,0:T(8,128)(2,1)S(1)} collective-permute-done((bf16[4,128,128]{2,1,0:T(8,128)(2,1)S(1)}, bf16[4,128,128]{2,1,0:T(8,128)(2,1)S(1)}, u32[]{:S(2)}, u32[]{:S(2)}) %collective-permute-start.7) | collective-permute-done | bytes 131104 | tf_op jit(solution)/shard_map/ppermute | solution.py:360
  27.8 0.7 %shard_map.62 = bf16[4,128,128]{2,1,0:T(8,128)(2,1)} custom-call(f32[4,128,128]{2,1,0:T(8,128)S(1)} %get-tuple-element.29.factors, f32[4,128,128]{2,1,0:T(8,128)S(1)} %convert_add_fusion.own, bf16[4,128,128]{2,1,0:T(8,128)(2,1)S(1)} %collective-permute-done.7.refs_0_), custom_call_target="tpu_custom_call" | custom-call | tf_op jit(solution)/shard_map/pallas_call | solution.py:380
  (4 shorter events, 0.1 us)
Async XLA Ops:
  0.0 9.5 %collective-permute-start = (bf16[4,128,128]{2,1,0:T(8,128)(2,1)}, bf16[4,128,128]{2,1,0:T(8,128)(2,1)S(1)}, u32[]{:S(2)}, u32[]{:S(2)}) collective-permute-start(bf16[4,128,128]{2,1,0:T(8,128)(2,1)} %bitcast.7), channel_id=1, source_target_pairs={{0,18},{1,17},{2,16},{3,19},{16,2},{17,1},{18,0},{19,3},{4,22},{5,... | collective-permute-start | bytes 393224 | tf_op jit(solution)/shard_map/ppermute | solution.py:268
  4.9 4.6 %collective-permute-start.1 = (f32[4,128]{1,0:T(4,128)S(1)}, f32[4,128]{1,0:T(4,128)S(1)}, u32[]{:S(2)}, u32[]{:S(2)}) collective-permute-start(f32[4,128]{1,0:T(4,128)S(1)} %get-tuple-element.30), channel_id=1, source_target_pairs={{0,18},{1,17},{2,16},{3,19},{16,2},{17,1},{18,0},{19,3},{4,22},{5,... | collective-permute-start | bytes 6152 | tf_op jit(solution)/shard_map/ppermute | solution.py:268
  5.0 5.4 %collective-permute-start.2 = (bf16[4,128,128]{2,1,0:T(8,128)(2,1)S(1)}, bf16[4,128,128]{2,1,0:T(8,128)(2,1)S(1)}, u32[]{:S(2)}, u32[]{:S(2)}) collective-permute-start(bf16[4,128,128]{2,1,0:T(8,128)(2,1)S(1)} %get-tuple-element.35), channel_id=1, source_target_pairs={{0,16},{1,19},{2,18},{3,17},{16,0},{17,3},{18,2},{19,1},{4,20},{5,... | collective-permute-start | bytes 393224 | tf_op jit(solution)/shard_map/ppermute | solution.py:268
  9.6 2.3 %collective-permute-start.3 = (bf16[4,128,128]{2,1,0:T(8,128)(2,1)S(1)}, bf16[4,128,128]{2,1,0:T(8,128)(2,1)S(1)}, u32[]{:S(2)}, u32[]{:S(2)}) collective-permute-start(bf16[4,128,128]{2,1,0:T(8,128)(2,1)S(1)} %multiply_convert_fusion.panel.refs_0_), channel_id=1, source_target_pairs={{0,1},{1,0},{2,3},{3,2},{4,5},{5,4},{6,7},{7,6},{8,9},{9,8},{10,11... | collective-permute-start | bytes 393224 | tf_op jit(solution)/shard_map/ppermute | solution.py:271
  10.4 1.9 %collective-permute-start.4 = (bf16[4,128,128]{2,1,0:T(8,128)(2,1)S(1)}, bf16[4,128,128]{2,1,0:T(8,128)(2,1)S(1)}, u32[]{:S(2)}, u32[]{:S(2)}) collective-permute-start(bf16[4,128,128]{2,1,0:T(8,128)(2,1)S(1)} %collective-permute-done.2.refs_0_.refs_1_), channel_id=1, source_target_pairs={{0,1},{1,0},{2,3},{3,2},{4,5},{5,4},{6,7},{7,6},{8,9},{9,8},{10,11... | collective-permute-start | bytes 393224 | tf_op jit(solution)/shard_map/ppermute | solution.py:271
  13.9 6.4 %collective-permute-start.6 = (bf16[4,128,128]{2,1,0:T(8,128)(2,1)S(1)}, bf16[4,128,128]{2,1,0:T(8,128)(2,1)S(1)}, u32[]{:S(2)}, u32[]{:S(2)}) collective-permute-start(bf16[4,128,128]{2,1,0:T(8,128)(2,1)S(1)} %get-tuple-element.50), channel_id=1, source_target_pairs={{0,4},{1,9},{2,6},{3,11},{4,0},{5,13},{6,2},{7,15},{8,12},{9,1},{1... | collective-permute-start | bytes 393224 | tf_op jit(solution)/shard_map/ppermute | solution.py:360
  16.5 6.1 %collective-permute-start.5 = (bf16[4,128,128]{2,1,0:T(8,128)(2,1)S(1)}, bf16[4,128,128]{2,1,0:T(8,128)(2,1)S(1)}, u32[]{:S(2)}, u32[]{:S(2)}) collective-permute-start(bf16[4,128,128]{2,1,0:T(8,128)(2,1)S(1)} %get-tuple-element.48), channel_id=1, source_target_pairs={{0,4},{1,9},{2,6},{3,11},{4,0},{5,13},{6,2},{7,15},{8,12},{9,1},{1... | collective-permute-start | bytes 393224 | tf_op jit(solution)/shard_map/ppermute | solution.py:360
  20.3 7.4 %collective-permute-start.7 = (bf16[4,128,128]{2,1,0:T(8,128)(2,1)S(1)}, bf16[4,128,128]{2,1,0:T(8,128)(2,1)S(1)}, u32[]{:S(2)}, u32[]{:S(2)}) collective-permute-start(bf16[4,128,128]{2,1,0:T(8,128)(2,1)S(1)} %add_convert_fusion), channel_id=1, source_target_pairs={{0,8},{1,5},{2,10},{3,7},{4,12},{5,1},{6,14},{7,3},{8,0},{9,13},{1... | collective-permute-start | bytes 393224 | tf_op jit(solution)/shard_map/ppermute | solution.py:360

commit v3 on v2

--- a/solution.py
+++ b/solution.py
@@ -8,7 +8,7 @@
 from jax.sharding import PartitionSpec as P
 
 UNROLL = 8
-BATCHES = (4, 4, 4, 8, 8, 8)
+BATCHES = (4, 4, 8, 8, 8)
 STAGES = len(BATCHES)
 VMEM = pl.BlockSpec(memory_space=pltpu.VMEM)
 SMEM = pl.BlockSpec(memory_space=pltpu.SMEM)
@@ -106,11 +106,11 @@
     far = (chunk >= 2) & ((chunk & 1) == 1)
     kept = jnp.where(chunk == 1, 1 + role * (groups // 2 - 1), (chunk >> 1) + 1 - role)
     kept = jnp.where(chunk == 0, 0, jnp.where(far, (chunk >> 1) - 1, kept))
-    stage = jnp.where(far, jnp.where(odd == 1, 2, jnp.minimum(rank, 1)), 5)
-    stage = jnp.where(far | (kept != 1), stage, 4 - role)
+    stage = jnp.where(far, odd, 4)
+    stage = jnp.where(far | (kept != 1), stage, 3 - role)
     kept = jnp.where(far | (kept == 0), kept, kept - 1)
     stage = jnp.where(origin < source_tiles, stage, STAGES)
-    panel = jnp.where(stage == 1, rank - 1, jnp.where(stage == 2, rank, rank + odd * half))
+    panel = jnp.where(stage == 1, rank, rank + odd * half)
     slot = count_up((1, capacity), 1)
 
     stages = (count_up((8, capacity), 0) == stage).astype(jnp.float32)
@@ -124,7 +124,7 @@
         jnp.where(count_up((8, capacity), 0) == at, part, 0) for at, part in enumerate(parts)
     ).astype(jnp.bfloat16)
     far_tiles = (groups // 2 - 1) * tiles_dev
-    tops = [far_tiles] * 3 + [tiles_dev] * 2 + [groups // 2 * tiles_dev]
+    tops = [far_tiles] * 2 + [tiles_dev] * 2 + [groups // 2 * tiles_dev]
     lanes = count_up((1, width), 1)
     for at, top in enumerate(tops):
         where = jnp.where(stage == at, position, -1)
@@ -187,15 +187,11 @@
         source[at * rows : (at + 1) * rows] = panel[...]
 
 
-def early_kernel(order_ref, panel, blocks, total):
+def early_kernel(order_ref, *refs):
+    *panels, blocks, total, source = refs
+    gather_panels(panels, source)
     total[...] = jnp.zeros_like(total)
-    add_products(0, order_ref, blocks, panel, total)
-
-
-def middle_kernel(order_ref, *refs):
-    *panels, blocks, _, total, source = refs
-    gather_panels(panels, source)
-    add_products(1, order_ref, blocks, source, total)
+    add_products(0, order_ref, blocks, source, total)
 
 
 def far_kernel(tiles_dev, order_ref, *refs):
@@ -203,15 +199,15 @@
     others = len(panels) // 2 * tiles_dev
     gather_panels(panels, source)
     first[...] = jnp.zeros_like(first)
-    add_products(2, order_ref, blocks, source.at[others:], total)
-    add_products(3, order_ref, blocks, source, first)
+    add_products(1, order_ref, blocks, source.at[others:], total)
+    add_products(2, order_ref, blocks, source, first)
     far[...] = total[: far.shape[0]].astype(far.dtype)
 
 
 def first_kernel(order_ref, *refs):
     *panels, blocks, _, first, total, source = refs
     gather_panels(panels, source)
-    add_products(4, order_ref, blocks, source, total)
+    add_products(3, order_ref, blocks, source, total)
     first[...] = total[: first.shape[0]].astype(first.dtype)
 
 
@@ -219,7 +215,7 @@
     *panels, blocks, own, later, source, total = refs
     gather_panels(panels, source)
     total[...] = jnp.zeros_like(total)
-    add_products(5, order_ref, blocks, source, total)
+    add_products(4, order_ref, blocks, source, total)
     tiles_dev = own.shape[0]
     own[...] = total[:tiles_dev]
     later[...] = total[tiles_dev : tiles_dev + later.shape[0]]
@@ -275,9 +271,10 @@
     middle = [across(source, step) for step in range(1, blks // 2)]
     early_scales = across(scales, 0)
     order, blocks = stage_blocks(block_index[0], place, adjacency[0], blks, groups, tiles_dev)
-    early, early_scales, order = lax.optimization_barrier((early, early_scales, order))
+    *middle, early, early_scales, order = lax.optimization_barrier((*middle, early, early_scales, order))
     early = (early.astype(jnp.float32) * early_scales[:, :, None]).astype(jnp.bfloat16)
-    other = paired(early, "blk", 1)
+    panels = [early] + middle
+    others = [paired(panel, "blk", 1) for panel in panels]
     far_tiles = (groups // 2 - 1) * tiles_dev
 
     def held(count, dtype):
@@ -286,25 +283,14 @@
     total = pl.pallas_call(
         early_kernel,
         out_shape=jax.ShapeDtypeStruct((far_tiles + 1, tile_rows, row_width), jnp.float32),
-        in_specs=[SMEM] + [VMEM] * 2,
+        in_specs=[SMEM] + [VMEM] * (len(panels) + 1),
         out_specs=VMEM,
+        scratch_shapes=[held(len(panels) * tiles_dev, jnp.bfloat16)],
         compiler_params=LIMIT,
         cost_estimate=cost_of(capacity // 8, tile_rows, row_width),
-    )(order, early, blocks)
-    *middle, total = lax.optimization_barrier((*middle, total))
-    others = [other] + [paired(panel, "blk", 1) for panel in middle]
-    total = pl.pallas_call(
-        middle_kernel,
-        out_shape=jax.ShapeDtypeStruct(total.shape, total.dtype),
-        in_specs=[SMEM] + [VMEM] * (len(middle) + 2),
-        out_specs=VMEM,
-        input_output_aliases={len(middle) + 2: 0},
-        scratch_shapes=[held(len(middle) * tiles_dev, jnp.bfloat16)],
-        compiler_params=LIMIT,
-        cost_estimate=cost_of(capacity // 8, tile_rows, row_width),
-    )(order, *middle, blocks, total)
+    )(order, *panels, blocks)
     *others, total = lax.optimization_barrier((*others, total))
-    panels = [early] + middle + others
+    panels += others
     far, first, _ = pl.pallas_call(
         functools.partial(far_kernel, tiles_dev),
         out_shape=[

time: 28 us -> 27.8 us (level); the launches traced: 28.5 us -> 27.8 us
  Pallas kernels: 10.2 us -> 8.09 us
  waiting for transfers between devices: 6.51 us -> 7.38 us
  starting transfers between devices: 11.3 us -> 12 us
    ppermute x3, waiting for transfers between devices: 0.07 us -> 1.22 us  [across(): return lax.ppermute(value, ('side', 'blk'), pairs)]
    ppermute x3, starting transfers between devices: 4.46 us -> 5.47 us  [turned(): return lax.ppermute(value, ('grp', 'blk'), pairs)]
    pallas_call x1, Pallas kernels: 1.89 us -> 1.17 us  [shards(): pl.pallas_call(rest_kernel, out_shape=[jax.ShapeDtypeStruct(part, jnp.flo...]
    pallas_call x1 -> x0, Pallas kernels: 0.61 us -> none  [shards(): pl.pallas_call(middle_kernel, out_shape=jax.ShapeDtypeStruct(total.shape,...]
    pallas_call x1, Pallas kernels: 1.36 us -> 0.89 us  [shards(): pl.pallas_call(first_kernel, out_shape=[jax.ShapeDtypeStruct(part, jnp.bf...]
    ppermute x2, starting transfers between devices: 0.94 us -> 0.57 us  [paired(): lax.ppermute(value, axis, [(at, at ^ hop) for at in range(lax.axis_size(a...]
    pallas_call x1, Pallas kernels: 1.61 us -> 1.24 us  [shards(): pl.pallas_call(functools.partial(far_kernel, tiles_dev), out_shape=[jax.S...]
    ppermute x3, waiting for transfers between devices: 6.08 us -> 5.78 us  [turned(): return lax.ppermute(value, ('grp', 'blk'), pairs)]
  transfers between devices with their start and end apart: 8 -> 8, of which waited for: 4 -> 6; matrix products, arithmetic and copies ran while one was open for 1% -> 0% of each run, Pallas kernels for 28% -> 22%
where the time goes in v3:
time: 27.8 us
  starting transfers between devices  12 us (43%)
  Pallas kernels  8.09 us (29%)
  waiting for transfers between devices  7.38 us (27%)
    ppermute x3, starting transfers between devices, across(): return lax.ppermute(value, ('side', 'blk'), pairs)  5.93 us
    ppermute x3, waiting for transfers between devices, turned(): return lax.ppermute(value, ('grp', 'blk'), pairs)  5.78 us
    ppermute x3, starting transfers between devices, turned(): return lax.ppermute(value, ('grp', 'blk'), pairs)  5.47 us
    pallas_call x1, Pallas kernels, stage_blocks(): pl.pallas_call(functools.partial(stage_kernel, blks, groups, tiles_dev),...  2.46 us
    pallas_call x1, Pallas kernels, shards(): pl.pallas_call(functools.partial(far_kernel, tiles_dev), out_shape=[jax.S...  1.24 us
    ppermute x3, waiting for transfers between devices, across(): return lax.ppermute(value, ('side', 'blk'), pairs)  1.22 us
    pallas_call x1, Pallas kernels, shards(): pl.pallas_call(rest_kernel, out_shape=[jax.ShapeDtypeStruct(part, jnp.flo...  1.17 us
    pallas_call x1, Pallas kernels, scale_rows(): pl.pallas_call(scale_kernel, out_shape=[jax.ShapeDtypeStruct(codes.shape,...  1 us
  transfers between devices with their start and end apart: 8, of which 6 were waited for; matrix products, arithmetic and copies ran while one was open for 0% of the time, Pallas kernels for 22%

profile of v3, /device:TPU:0, one launch (start us, length us, event | category | flops | bytes accessed | tf_op | source)
XLA Modules:
  0.0 27.8 jit_solution(12114744058368437325)
XLA Ops:
  0.0 3.9 %collective-permute-start.1 = (bf16[4,128,128]{2,1,0:T(8,128)(2,1)}, bf16[4,128,128]{2,1,0:T(8,128)(2,1)S(1)}, u32[]{:S(2)}, u32[]{:S(2)}) collective-permute-start(bf16[4,128,128]{2,1,0:T(8,128)(2,1)} %bitcast.7), channel_id=1, source_target_pairs={{0,18},{1,17},{2,16},{3,19},{16,2},{17,1},{18,0},{19,3},{4,22},{5,... | collective-permute-start | bytes 393224 | tf_op jit(solution)/shard_map/ppermute | solution.py:264
  3.9 1.0 %shard_map.55 = (bf16[4,128,128]{2,1,0:T(8,128)(2,1)S(1)}, f32[4,128,128]{2,1,0:T(8,128)S(1)}, f32[4,128]{1,0:T(4,128)S(1)}) custom-call(s32[1,4]{1,0:T(1,128)} %exps_hbm.1, s32[1,512]{1,0:T(1,128)} %degrees_hbm.1, bf16[4,128,128]{2,1,0:T(8,128)(2,1)} %bitcast.8), custom_call_target="tpu_custom_call" | custom-call | flops 65536 | bytes 262144 | tf_op jit(solution)/shard_map/pallas_call | solution.py:56
  4.9 0.6 %collective-permute-start = (bf16[4,128,128]{2,1,0:T(8,128)(2,1)S(1)}, bf16[4,128,128]{2,1,0:T(8,128)(2,1)S(1)}, u32[]{:S(2)}, u32[]{:S(2)}) collective-permute-start(bf16[4,128,128]{2,1,0:T(8,128)(2,1)S(1)} %get-tuple-element.29), channel_id=1, source_target_pairs={{0,16},{1,19},{2,18},{3,17},{16,0},{17,3},{18,2},{19,1},{4,20},{5,... | collective-permute-start | bytes 393224 | tf_op jit(solution)/shard_map/ppermute | solution.py:264
  5.5 1.4 %collective-permute-start.2 = (f32[4,128]{1,0:T(4,128)S(1)}, f32[4,128]{1,0:T(4,128)S(1)}, u32[]{:S(2)}, u32[]{:S(2)}) collective-permute-start(f32[4,128]{1,0:T(4,128)S(1)} %get-tuple-element.30), channel_id=1, source_target_pairs={{0,18},{1,17},{2,16},{3,19},{16,2},{17,1},{18,0},{19,3},{4,22},{5,... | collective-permute-start | bytes 6152 | tf_op jit(solution)/shard_map/ppermute | solution.py:264
  6.9 0.1 pad_add_fusion.place_ref
  7.0 2.5 %shard_map.56 = (s32[8,128]{1,0:T(8,128)S(1)}, bf16[96,128,128]{2,1,0:T(8,128)(2,1)S(1)}) custom-call(s32[2]{0:T(128)S(1)} %pad_add_fusion.place_ref, s32[2,96]{1,0:T(2,128)} %bitcast.9, bf16[96,128,128]{2,1,0:T(8,128)(2,1)} %bitcast.6), custom_call_target="tpu_custom_call" | custom-call | tf_op jit(solution)/shard_map/pallas_call | solution.py:155
  9.5 1.2 %collective-permute-done.2 = f32[4,128]{1,0:T(4,128)S(1)} collective-permute-done((f32[4,128]{1,0:T(4,128)S(1)}, f32[4,128]{1,0:T(4,128)S(1)}, u32[]{:S(2)}, u32[]{:S(2)}) %collective-permute-start.2) | collective-permute-done | bytes 2080 | tf_op jit(solution)/shard_map/ppermute | solution.py:264
  10.7 0.0 collective-permute-done.1
  10.7 0.1 multiply_convert_fusion.refs_0_
  10.8 0.1 collective-permute-start.3
  10.9 0.5 %collective-permute-start.4 = (bf16[4,128,128]{2,1,0:T(8,128)(2,1)S(1)}, bf16[4,128,128]{2,1,0:T(8,128)(2,1)S(1)}, u32[]{:S(2)}, u32[]{:S(2)}) collective-permute-start(bf16[4,128,128]{2,1,0:T(8,128)(2,1)S(1)} %collective-permute-done.refs_1_), channel_id=1, source_target_pairs={{0,1},{1,0},{2,3},{3,2},{4,5},{5,4},{6,7},{7,6},{8,9},{9,8},{10,11... | collective-permute-start | bytes 393224 | tf_op jit(solution)/shard_map/ppermute | solution.py:267
  11.4 0.6 %shard_map.57.refs_5_ = f32[5,128,128]{2,1,0:T(8,128)S(1)} custom-call(s32[8,128]{1,0:T(8,128)S(1)} %get-tuple-element.44.order_ref, bf16[4,128,128]{2,1,0:T(8,128)(2,1)S(1)} %multiply_convert_fusion.refs_0_, bf16[4,128,128]{2,1,0:T(8,128)(2,1)S(1)} %collective-permute-done.refs_1_, bf16[96,128,128]{2,1,0:T(8,128)(2,1)S(1)} %get-tuple-element.36.refs_2_.refs_4_), custom_call_target="tpu_custom_call" | custom-call | flops 50331648 | bytes 393216 | tf_op jit(solution)/shard_map/pallas_call | solution.py:283
  12.1 0.2 collective-permute-done.3.refs_2_
  12.3 0.2 collective-permute-done.4.refs_3_
  12.5 1.2 %shard_map.58 = (bf16[4,128,128]{2,1,0:T(8,128)(2,1)S(1)}, f32[5,128,128]{2,1,0:T(8,128)S(1)}, f32[5,128,128]{2,1,0:T(8,128)S(1)}) custom-call(s32[8,128]{1,0:T(8,128)S(1)} %get-tuple-element.44.order_ref, bf16[4,128,128]{2,1,0:T(8,128)(2,1)S(1)} %multiply_convert_fusion.refs_0_, ...), custom_call_target="tpu_custom_call", output_to_operand_aliasing={{2}: (6, {})} | custom-call | flops 50331648 | bytes 393216 | tf_op jit(solution)/shard_map/pallas_call | solution.py:294
  13.7 1.5 %collective-permute-start.6 = (bf16[4,128,128]{2,1,0:T(8,128)(2,1)S(1)}, bf16[4,128,128]{2,1,0:T(8,128)(2,1)S(1)}, u32[]{:S(2)}, u32[]{:S(2)}) collective-permute-start(bf16[4,128,128]{2,1,0:T(8,128)(2,1)S(1)} %get-tuple-element.48), channel_id=1, source_target_pairs={{0,4},{1,9},{2,6},{3,11},{4,0},{5,13},{6,2},{7,15},{8,12},{9,1},{1... | collective-permute-start | bytes 393224 | tf_op jit(solution)/shard_map/ppermute | solution.py:346
  15.2 0.9 %shard_map.59 = (bf16[4,128,128]{2,1,0:T(8,128)(2,1)S(1)}, f32[5,128,128]{2,1,0:T(8,128)S(1)}) custom-call(s32[8,128]{1,0:T(8,128)S(1)} %get-tuple-element.44.order_ref, bf16[4,128,128]{2,1,0:T(8,128)(2,1)S(1)} %multiply_convert_fusion.refs_0_, bf16[4,128,128]{2,1,0:T(8,128)(2,1)S(1)} %collective-permute-done.refs_1_, ...), custom_call_target="tpu_custom_call", output_to_operand_aliasing={{1}: (6, {})} | custom-call | flops 100663296 | bytes 786432 | tf_op jit(solution)/shard_map/pallas_call | solution.py:309
  16.1 0.9 %collective-permute-start.5 = (bf16[4,128,128]{2,1,0:T(8,128)(2,1)S(1)}, bf16[4,128,128]{2,1,0:T(8,128)(2,1)S(1)}, u32[]{:S(2)}, u32[]{:S(2)}) collective-permute-start(bf16[4,128,128]{2,1,0:T(8,128)(2,1)S(1)} %get-tuple-element.46), channel_id=1, source_target_pairs={{0,4},{1,9},{2,6},{3,11},{4,0},{5,13},{6,2},{7,15},{8,12},{9,1},{1... | collective-permute-start | bytes 393224 | tf_op jit(solution)/shard_map/ppermute | solution.py:346
  17.0 1.2 %shard_map.60 = (f32[4,128,128]{2,1,0:T(8,128)S(1)}, f32[4,128,128]{2,1,0:T(8,128)S(1)}) custom-call(s32[8,128]{1,0:T(8,128)S(1)} %get-tuple-element.44.order_ref, bf16[4,128,128]{2,1,0:T(8,128)(2,1)S(1)} %multiply_convert_fusion.refs_0_, bf16[4,128,128]{2,1,0:T(8,128)(2,1)S(1)} %collective-permute-done.refs_1_, ...), custom_call_target="tpu_custom_call" | custom-call | flops 201326592 | bytes 1572864 | tf_op jit(solution)/shard_map/pallas_call | solution.py:323
  18.2 1.0 %collective-permute-done.6 = bf16[4,128,128]{2,1,0:T(8,128)(2,1)S(1)} collective-permute-done((bf16[4,128,128]{2,1,0:T(8,128)(2,1)S(1)}, bf16[4,128,128]{2,1,0:T(8,128)(2,1)S(1)}, u32[]{:S(2)}, u32[]{:S(2)}) %collective-permute-start.6) | collective-permute-done | bytes 131104 | tf_op jit(solution)/shard_map/ppermute | solution.py:346
  19.2 3.1 %collective-permute-start.7 = (bf16[4,128,128]{2,1,0:T(8,128)(2,1)S(1)}, bf16[4,128,128]{2,1,0:T(8,128)(2,1)S(1)}, u32[]{:S(2)}, u32[]{:S(2)}) collective-permute-start(bf16[4,128,128]{2,1,0:T(8,128)(2,1)S(1)} %add_convert_fusion), channel_id=1, source_target_pairs={{0,8},{1,5},{2,10},{3,7},{4,12},{5,1},{6,14},{7,3},{8,0},{9,13},{1... | collective-permute-start | bytes 393224 | tf_op jit(solution)/shard_map/ppermute | solution.py:346
  22.3 0.3 %collective-permute-done.5 = bf16[4,128,128]{2,1,0:T(8,128)(2,1)S(1)} collective-permute-done((bf16[4,128,128]{2,1,0:T(8,128)(2,1)S(1)}, bf16[4,128,128]{2,1,0:T(8,128)(2,1)S(1)}, u32[]{:S(2)}, u32[]{:S(2)}) %collective-permute-start.5) | collective-permute-done | bytes 131104 | tf_op jit(solution)/shard_map/ppermute | solution.py:346
  22.7 4.4 %collective-permute-done.7.refs_0_ = bf16[4,128,128]{2,1,0:T(8,128)(2,1)S(1)} collective-permute-done((bf16[4,128,128]{2,1,0:T(8,128)(2,1)S(1)}, bf16[4,128,128]{2,1,0:T(8,128)(2,1)S(1)}, u32[]{:S(2)}, u32[]{:S(2)}) %collective-permute-start.7) | collective-permute-done | bytes 131104 | tf_op jit(solution)/shard_map/ppermute | solution.py:346
  27.1 0.7 %shard_map.61 = bf16[4,128,128]{2,1,0:T(8,128)(2,1)} custom-call(f32[4,128,128]{2,1,0:T(8,128)S(1)} %get-tuple-element.28.factors, f32[4,128,128]{2,1,0:T(8,128)S(1)} %convert_add_fusion.own, bf16[4,128,128]{2,1,0:T(8,128)(2,1)S(1)} %collective-permute-done.7.refs_0_), custom_call_target="tpu_custom_call" | custom-call | tf_op jit(solution)/shard_map/pallas_call | solution.py:366
  (3 shorter events, 0.1 us)
Async XLA Ops:
  0.0 10.7 %collective-permute-start.1 = (bf16[4,128,128]{2,1,0:T(8,128)(2,1)}, bf16[4,128,128]{2,1,0:T(8,128)(2,1)S(1)}, u32[]{:S(2)}, u32[]{:S(2)}) collective-permute-start(bf16[4,128,128]{2,1,0:T(8,128)(2,1)} %bitcast.7), channel_id=1, source_target_pairs={{0,18},{1,17},{2,16},{3,19},{16,2},{17,1},{18,0},{19,3},{4,22},{5,... | collective-permute-start | bytes 393224 | tf_op jit(solution)/shard_map/ppermute | solution.py:264
  4.9 5.8 %collective-permute-start = (bf16[4,128,128]{2,1,0:T(8,128)(2,1)S(1)}, bf16[4,128,128]{2,1,0:T(8,128)(2,1)S(1)}, u32[]{:S(2)}, u32[]{:S(2)}) collective-permute-start(bf16[4,128,128]{2,1,0:T(8,128)(2,1)S(1)} %get-tuple-element.29), channel_id=1, source_target_pairs={{0,16},{1,19},{2,18},{3,17},{16,0},{17,3},{18,2},{19,1},{4,20},{5,... | collective-permute-start | bytes 393224 | tf_op jit(solution)/shard_map/ppermute | solution.py:264
  5.5 5.2 %collective-permute-start.2 = (f32[4,128]{1,0:T(4,128)S(1)}, f32[4,128]{1,0:T(4,128)S(1)}, u32[]{:S(2)}, u32[]{:S(2)}) collective-permute-start(f32[4,128]{1,0:T(4,128)S(1)} %get-tuple-element.30), channel_id=1, source_target_pairs={{0,18},{1,17},{2,16},{3,19},{16,2},{17,1},{18,0},{19,3},{4,22},{5,... | collective-permute-start | bytes 6152 | tf_op jit(solution)/shard_map/ppermute | solution.py:264
  10.8 1.4 %collective-permute-start.3 = (bf16[4,128,128]{2,1,0:T(8,128)(2,1)S(1)}, bf16[4,128,128]{2,1,0:T(8,128)(2,1)S(1)}, u32[]{:S(2)}, u32[]{:S(2)}) collective-permute-start(bf16[4,128,128]{2,1,0:T(8,128)(2,1)S(1)} %multiply_convert_fusion.refs_0_), channel_id=1, source_target_pairs={{0,1},{1,0},{2,3},{3,2},{4,5},{5,4},{6,7},{7,6},{8,9},{9,8},{10,11... | collective-permute-start | bytes 393224 | tf_op jit(solution)/shard_map/ppermute | solution.py:267
  10.9 1.5 %collective-permute-start.4 = (bf16[4,128,128]{2,1,0:T(8,128)(2,1)S(1)}, bf16[4,128,128]{2,1,0:T(8,128)(2,1)S(1)}, u32[]{:S(2)}, u32[]{:S(2)}) collective-permute-start(bf16[4,128,128]{2,1,0:T(8,128)(2,1)S(1)} %collective-permute-done.refs_1_), channel_id=1, source_target_pairs={{0,1},{1,0},{2,3},{3,2},{4,5},{5,4},{6,7},{7,6},{8,9},{9,8},{10,11... | collective-permute-start | bytes 393224 | tf_op jit(solution)/shard_map/ppermute | solution.py:267
  13.7 5.5 %collective-permute-start.6 = (bf16[4,128,128]{2,1,0:T(8,128)(2,1)S(1)}, bf16[4,128,128]{2,1,0:T(8,128)(2,1)S(1)}, u32[]{:S(2)}, u32[]{:S(2)}) collective-permute-start(bf16[4,128,128]{2,1,0:T(8,128)(2,1)S(1)} %get-tuple-element.48), channel_id=1, source_target_pairs={{0,4},{1,9},{2,6},{3,11},{4,0},{5,13},{6,2},{7,15},{8,12},{9,1},{1... | collective-permute-start | bytes 393224 | tf_op jit(solution)/shard_map/ppermute | solution.py:346
  16.1 6.6 %collective-permute-start.5 = (bf16[4,128,128]{2,1,0:T(8,128)(2,1)S(1)}, bf16[4,128,128]{2,1,0:T(8,128)(2,1)S(1)}, u32[]{:S(2)}, u32[]{:S(2)}) collective-permute-start(bf16[4,128,128]{2,1,0:T(8,128)(2,1)S(1)} %get-tuple-element.46), channel_id=1, source_target_pairs={{0,4},{1,9},{2,6},{3,11},{4,0},{5,13},{6,2},{7,15},{8,12},{9,1},{1... | collective-permute-start | bytes 393224 | tf_op jit(solution)/shard_map/ppermute | solution.py:346
  19.2 7.9 %collective-permute-start.7 = (bf16[4,128,128]{2,1,0:T(8,128)(2,1)S(1)}, bf16[4,128,128]{2,1,0:T(8,128)(2,1)S(1)}, u32[]{:S(2)}, u32[]{:S(2)}) collective-permute-start(bf16[4,128,128]{2,1,0:T(8,128)(2,1)S(1)} %add_convert_fusion), channel_id=1, source_target_pairs={{0,8},{1,5},{2,10},{3,7},{4,12},{5,1},{6,14},{7,3},{8,0},{9,13},{1... | collective-permute-start | bytes 393224 | tf_op jit(solution)/shard_map/ppermute | solution.py:346

commit v4 on v2

--- a/solution.py
+++ b/solution.py
@@ -8,7 +8,7 @@
 from jax.sharding import PartitionSpec as P
 
 UNROLL = 8
-BATCHES = (4, 4, 4, 8, 8, 8)
+BATCHES = (4, 4, 4, 8, 8, 8, 8)
 STAGES = len(BATCHES)
 VMEM = pl.BlockSpec(memory_space=pltpu.VMEM)
 SMEM = pl.BlockSpec(memory_space=pltpu.SMEM)
@@ -106,9 +106,9 @@
     far = (chunk >= 2) & ((chunk & 1) == 1)
     kept = jnp.where(chunk == 1, 1 + role * (groups // 2 - 1), (chunk >> 1) + 1 - role)
     kept = jnp.where(chunk == 0, 0, jnp.where(far, (chunk >> 1) - 1, kept))
-    stage = jnp.where(far, jnp.where(odd == 1, 2, jnp.minimum(rank, 1)), 5)
-    stage = jnp.where(far | (kept != 1), stage, 4 - role)
-    kept = jnp.where(far | (kept == 0), kept, kept - 1)
+    near = jnp.where(kept == 0, 6, jnp.where(kept == 1, 4 - role, 5))
+    stage = jnp.where(far, jnp.where(odd == 1, 2, jnp.minimum(rank, 1)), near)
+    kept = jnp.where(stage == 5, kept - 2, jnp.where(far, kept, 0))
     stage = jnp.where(origin < source_tiles, stage, STAGES)
     panel = jnp.where(stage == 1, rank - 1, jnp.where(stage == 2, rank, rank + odd * half))
     slot = count_up((1, capacity), 1)
@@ -124,7 +124,7 @@
         jnp.where(count_up((8, capacity), 0) == at, part, 0) for at, part in enumerate(parts)
     ).astype(jnp.bfloat16)
     far_tiles = (groups // 2 - 1) * tiles_dev
-    tops = [far_tiles] * 3 + [tiles_dev] * 2 + [groups // 2 * tiles_dev]
+    tops = [far_tiles] * 3 + [tiles_dev] * 2 + [far_tiles, tiles_dev]
     lanes = count_up((1, width), 1)
     for at, top in enumerate(tops):
         where = jnp.where(stage == at, position, -1)
@@ -215,14 +215,12 @@
     first[...] = total[: first.shape[0]].astype(first.dtype)
 
 
-def rest_kernel(order_ref, *refs):
-    *panels, blocks, own, later, source, total = refs
+def later_kernel(stage, order_ref, *refs):
+    *panels, blocks, later, source, total = refs
     gather_panels(panels, source)
     total[...] = jnp.zeros_like(total)
-    add_products(5, order_ref, blocks, source, total)
-    tiles_dev = own.shape[0]
-    own[...] = total[:tiles_dev]
-    later[...] = total[tiles_dev : tiles_dev + later.shape[0]]
+    add_products(stage, order_ref, blocks, source, total)
+    later[...] = total[: later.shape[0]]
 
 
 def final_kernel(factors, own, *refs):
@@ -334,21 +332,21 @@
         cost_estimate=cost_of(capacity // 4, tile_rows, row_width),
     )(order, *panels, blocks, first)
     first, order = lax.optimization_barrier((first, order))
-    own, later = pl.pallas_call(
-        rest_kernel,
-        out_shape=[
-            jax.ShapeDtypeStruct(part, jnp.float32),
-            jax.ShapeDtypeStruct((far_tiles, tile_rows, row_width), jnp.float32),
-        ],
-        in_specs=[SMEM] + [VMEM] * (len(panels) + 1),
-        out_specs=[VMEM] * 2,
-        scratch_shapes=[
-            held(len(panels) * tiles_dev, jnp.bfloat16),
-            held(groups // 2 * tiles_dev + 1, jnp.float32),
-        ],
-        compiler_params=LIMIT,
-        cost_estimate=cost_of(capacity // 2, tile_rows, row_width),
-    )(order, *panels, blocks)
+    def multiplied(stage, count, ready):
+        return pl.pallas_call(
+            functools.partial(later_kernel, stage),
+            out_shape=jax.ShapeDtypeStruct((count, tile_rows, row_width), jnp.float32),
+            in_specs=[SMEM] + [VMEM] * (len(panels) + 1),
+            out_specs=VMEM,
+            scratch_shapes=[
+                held(len(panels) * tiles_dev, jnp.bfloat16),
+                held(count + 1, jnp.float32),
+            ],
+            compiler_params=LIMIT,
+            cost_estimate=cost_of(capacity // 4, tile_rows, row_width),
+        )(ready, *panels, blocks)
+
+    later = multiplied(5, far_tiles, order)
 
     def turned(value, even_hop, odd_hop):
         hops = (even_hop, odd_hop)
@@ -374,8 +372,9 @@
             elif at == steps - 1:
                 value = value + jnp.where(even_core, 0.0, extra)
         odd_hop = 1 if at == steps - 1 else 2 * at + 4
-        arrived.append(turned(value.astype(jnp.bfloat16), 2 * at + 2, odd_hop))
-    own = own + arrived[0].astype(jnp.float32)
+        value, order = lax.optimization_barrier((value.astype(jnp.bfloat16), order))
+        arrived.append(turned(value, 2 * at + 2, odd_hop))
+    own = multiplied(6, tiles_dev, order) + arrived[0].astype(jnp.float32)
     own, *sums = lax.optimization_barrier((own, *arrived[1:]))
     out = pl.pallas_call(
         final_kernel,

time: 28 us -> 27.8 us (level)
  waiting for transfers between devices: 6.51 us -> 4.58 us
  starting transfers between devices: 11.3 us -> 13.1 us
    ppermute x3, starting transfers between devices: 4.46 us -> 6.61 us  [turned(): return lax.ppermute(value, ('grp', 'blk'), pairs)]
    ppermute x3, waiting for transfers between devices: 6.08 us -> 4.15 us  [turned(): return lax.ppermute(value, ('grp', 'blk'), pairs)]
    pallas_call x1 -> x2, Pallas kernels: 1.89 us -> 2.3 us  [multiplied(): pl.pallas_call(functools.partial(later_kernel, stage), out_shape=jax.Shap...]
    pallas_call x1, Pallas kernels: 1.61 us -> 1.24 us  [shards(): pl.pallas_call(functools.partial(far_kernel, tiles_dev), out_shape=[jax.S...]
    ppermute x2, starting transfers between devices: 0.94 us -> 0.58 us  [paired(): lax.ppermute(value, axis, [(at, at ^ hop) for at in range(lax.axis_size(a...]
  transfers between devices with their start and end apart: 8 -> 8, of which waited for: 4 -> 4; matrix products, arithmetic and copies ran while one was open for 1% -> 1% of each run, Pallas kernels for 28% -> 29%
where the time goes in v4:
time: 27.8 us; the launch traced here: 28.1 us
  starting transfers between devices  13.1 us (47%)
  Pallas kernels  10 us (36%)
  waiting for transfers between devices  4.58 us (16%)
  other arithmetic  0.28 us (1%)
    ppermute x3, starting transfers between devices, turned(): return lax.ppermute(value, ('grp', 'blk'), pairs)  6.61 us
    ppermute x3, starting transfers between devices, across(): return lax.ppermute(value, ('side', 'blk'), pairs)  5.92 us
    ppermute x3, waiting for transfers between devices, turned(): return lax.ppermute(value, ('grp', 'blk'), pairs)  4.15 us
    pallas_call x1, Pallas kernels, stage_blocks(): pl.pallas_call(functools.partial(stage_kernel, blks, groups, tiles_dev),...  2.46 us
    pallas_call x2, Pallas kernels, multiplied(): pl.pallas_call(functools.partial(later_kernel, stage), out_shape=jax.Shap...  2.3 us
    pallas_call x1, Pallas kernels, shards(): pl.pallas_call(functools.partial(far_kernel, tiles_dev), out_shape=[jax.S...  1.24 us
    pallas_call x1, Pallas kernels, shards(): pl.pallas_call(first_kernel, out_shape=[jax.ShapeDtypeStruct(part, jnp.bf...  1.12 us
    pallas_call x1, Pallas kernels, scale_rows(): pl.pallas_call(scale_kernel, out_shape=[jax.ShapeDtypeStruct(codes.shape,...  1 us
  transfers between devices with their start and end apart: 8, of which 4 were waited for; matrix products, arithmetic and copies ran while one was open for 1% of the time, Pallas kernels for 29%

profile of v4, /device:TPU:0, one launch (start us, length us, event | category | flops | bytes accessed | tf_op | source)
XLA Modules:
  0.0 28.1 jit_solution(12525468326496503733)
XLA Ops:
  0.0 3.9 %collective-permute-start = (bf16[4,128,128]{2,1,0:T(8,128)(2,1)}, bf16[4,128,128]{2,1,0:T(8,128)(2,1)S(1)}, u32[]{:S(2)}, u32[]{:S(2)}) collective-permute-start(bf16[4,128,128]{2,1,0:T(8,128)(2,1)} %bitcast.7), channel_id=1, source_target_pairs={{0,18},{1,17},{2,16},{3,19},{16,2},{17,1},{18,0},{19,3},{4,22},{5,... | collective-permute-start | bytes 393224 | tf_op jit(solution)/shard_map/ppermute | solution.py:266
  3.9 1.0 %shard_map.55 = (bf16[4,128,128]{2,1,0:T(8,128)(2,1)S(1)}, f32[4,128,128]{2,1,0:T(8,128)S(1)}, f32[4,128]{1,0:T(4,128)S(1)}) custom-call(s32[1,4]{1,0:T(1,128)} %exps_hbm.1, s32[1,512]{1,0:T(1,128)} %degrees_hbm.1, bf16[4,128,128]{2,1,0:T(8,128)(2,1)} %bitcast.8), custom_call_target="tpu_custom_call" | custom-call | flops 65536 | bytes 262144 | tf_op jit(solution)/shard_map/pallas_call | solution.py:56
  4.9 0.1 collective-permute-start.1
  5.0 2.0 %collective-permute-start.2 = (bf16[4,128,128]{2,1,0:T(8,128)(2,1)S(1)}, bf16[4,128,128]{2,1,0:T(8,128)(2,1)S(1)}, u32[]{:S(2)}, u32[]{:S(2)}) collective-permute-start(bf16[4,128,128]{2,1,0:T(8,128)(2,1)S(1)} %get-tuple-element.35), channel_id=1, source_target_pairs={{0,16},{1,19},{2,18},{3,17},{16,0},{17,3},{18,2},{19,1},{4,20},{5,... | collective-permute-start | bytes 393224 | tf_op jit(solution)/shard_map/ppermute | solution.py:266
  6.9 0.1 pad_add_fusion.place_ref
  7.0 2.5 %shard_map.56 = (s32[8,128]{1,0:T(8,128)S(1)}, bf16[96,128,128]{2,1,0:T(8,128)(2,1)S(1)}) custom-call(s32[2]{0:T(128)S(1)} %pad_add_fusion.place_ref, s32[2,96]{1,0:T(2,128)} %bitcast.9, bf16[96,128,128]{2,1,0:T(8,128)(2,1)} %bitcast.6), custom_call_target="tpu_custom_call" | custom-call | tf_op jit(solution)/shard_map/pallas_call | solution.py:155
  9.5 0.0 collective-permute-done.1
  9.5 0.1 multiply_convert_fusion.panel.refs_0_
  9.6 0.1 collective-permute-start.3
  9.7 0.6 %shard_map.57.refs_2_ = f32[5,128,128]{2,1,0:T(8,128)S(1)} custom-call(s32[8,128]{1,0:T(8,128)S(1)} %get-tuple-element.48.order_ref, bf16[4,128,128]{2,1,0:T(8,128)(2,1)S(1)} %multiply_convert_fusion.panel.refs_0_, bf16[96,128,128]{2,1,0:T(8,128)(2,1)S(1)} %get-tuple-element.36.blocks.refs_1_.refs_4_), custom_call_target="tpu_custom_call" | custom-call | flops 50331648 | bytes 393216 | tf_op jit(solution)/shard_map/pallas_call | solution.py:284
  10.4 0.1 collective-permute-done.2.refs_0_.refs_1_
  10.4 0.5 %collective-permute-start.4 = (bf16[4,128,128]{2,1,0:T(8,128)(2,1)S(1)}, bf16[4,128,128]{2,1,0:T(8,128)(2,1)S(1)}, u32[]{:S(2)}, u32[]{:S(2)}) collective-permute-start(bf16[4,128,128]{2,1,0:T(8,128)(2,1)S(1)} %collective-permute-done.2.refs_0_.refs_1_), channel_id=1, source_target_pairs={{0,1},{1,0},{2,3},{3,2},{4,5},{5,4},{6,7},{7,6},{8,9},{9,8},{10,11... | collective-permute-start | bytes 393224 | tf_op jit(solution)/shard_map/ppermute | solution.py:269
  10.9 0.6 %shard_map.58.refs_5_ = f32[5,128,128]{2,1,0:T(8,128)S(1)} custom-call(s32[8,128]{1,0:T(8,128)S(1)} %get-tuple-element.48.order_ref, bf16[4,128,128]{2,1,0:T(8,128)(2,1)S(1)} %collective-permute-done.2.refs_0_.refs_1_, bf16[96,128,128]{2,1,0:T(8,128)(2,1)S(1)} %get-tuple-element.36.blocks.refs_1_.refs_4_, ...), custom_call_target="tpu_custom_call", output_to_operand_aliasing={{}: (3, {})} | custom-call | flops 50331648 | bytes 393216 | tf_op jit(solution)/shard_map/pallas_call | solution.py:294
  11.6 0.4 %collective-permute-done.4.refs_3_ = bf16[4,128,128]{2,1,0:T(8,128)(2,1)S(1)} collective-permute-done((bf16[4,128,128]{2,1,0:T(8,128)(2,1)S(1)}, bf16[4,128,128]{2,1,0:T(8,128)(2,1)S(1)}, u32[]{:S(2)}, u32[]{:S(2)}) %collective-permute-start.4) | collective-permute-done | bytes 131104 | tf_op jit(solution)/shard_map/ppermute | solution.py:269
  11.9 1.2 %shard_map.59 = (bf16[4,128,128]{2,1,0:T(8,128)(2,1)S(1)}, f32[5,128,128]{2,1,0:T(8,128)S(1)}, f32[5,128,128]{2,1,0:T(8,128)S(1)}) custom-call(s32[8,128]{1,0:T(8,128)S(1)} %get-tuple-element.48.order_ref, bf16[4,128,128]{2,1,0:T(8,128)(2,1)S(1)} %multiply_convert_fusion.panel.refs_0_, ...), custom_call_target="tpu_custom_call", output_to_operand_aliasing={{2}: (6, {})} | custom-call | flops 50331648 | bytes 393216 | tf_op jit(solution)/shard_map/pallas_call | solution.py:306
  13.2 2.1 %collective-permute-start.5 = (bf16[4,128,128]{2,1,0:T(8,128)(2,1)S(1)}, bf16[4,128,128]{2,1,0:T(8,128)(2,1)S(1)}, u32[]{:S(2)}, u32[]{:S(2)}) collective-permute-start(bf16[4,128,128]{2,1,0:T(8,128)(2,1)S(1)} %get-tuple-element.47), channel_id=1, source_target_pairs={{0,4},{1,9},{2,6},{3,11},{4,0},{5,13},{6,2},{7,15},{8,12},{9,1},{1... | collective-permute-start | bytes 393224 | tf_op jit(solution)/shard_map/ppermute | solution.py:358
  15.2 1.1 %shard_map.60 = (bf16[4,128,128]{2,1,0:T(8,128)(2,1)S(1)}, f32[5,128,128]{2,1,0:T(8,128)S(1)}) custom-call(s32[8,128]{1,0:T(8,128)S(1)} %get-tuple-element.48.order_ref, bf16[4,128,128]{2,1,0:T(8,128)(2,1)S(1)} %multiply_convert_fusion.panel.refs_0_, ...), custom_call_target="tpu_custom_call", output_to_operand_aliasing={{1}: (6, {})} | custom-call | flops 100663296 | bytes 786432 | tf_op jit(solution)/shard_map/pallas_call | solution.py:321
  16.3 0.6 %collective-permute-start.6 = (bf16[4,128,128]{2,1,0:T(8,128)(2,1)S(1)}, bf16[4,128,128]{2,1,0:T(8,128)(2,1)S(1)}, u32[]{:S(2)}, u32[]{:S(2)}) collective-permute-start(bf16[4,128,128]{2,1,0:T(8,128)(2,1)S(1)} %get-tuple-element.49), channel_id=1, source_target_pairs={{0,4},{1,9},{2,6},{3,11},{4,0},{5,13},{6,2},{7,15},{8,12},{9,1},{1... | collective-permute-start | bytes 393224 | tf_op jit(solution)/shard_map/ppermute | solution.py:358
  16.9 1.1 %shard_map.61 = f32[4,128,128]{2,1,0:T(8,128)S(1)} custom-call(s32[8,128]{1,0:T(8,128)S(1)} %get-tuple-element.48.order_ref, bf16[4,128,128]{2,1,0:T(8,128)(2,1)S(1)} %multiply_convert_fusion.panel.refs_0_, bf16[4,128,128]{2,1,0:T(8,128)(2,1)S(1)} %collective-permute-done.2.refs_0_.refs_1_, bf16[4,128,128]{2,1,0:T(8,128)(2,1)S(1)} %collective-permute-done.3.refs_2_, ...), custom_call_target="tpu_custom_call" | custom-call | flops 100663296 | bytes 786432 | tf_op jit(solution)/shard_map/pallas_call | solution.py:336
  18.1 0.1 collective-permute-done.5
  18.2 4.0 %collective-permute-start.7 = (bf16[4,128,128]{2,1,0:T(8,128)(2,1)S(1)}, bf16[4,128,128]{2,1,0:T(8,128)(2,1)S(1)}, u32[]{:S(2)}, u32[]{:S(2)}) collective-permute-start(bf16[4,128,128]{2,1,0:T(8,128)(2,1)S(1)} %add_convert_fusion), channel_id=1, source_target_pairs={{0,8},{1,5},{2,10},{3,7},{4,12},{5,1},{6,14},{7,3},{8,0},{9,13},{1... | collective-permute-start | bytes 393224 | tf_op jit(solution)/shard_map/ppermute | solution.py:358
  22.2 1.1 %shard_map.62 = f32[4,128,128]{2,1,0:T(8,128)S(1)} custom-call(s32[8,128]{1,0:T(8,128)S(1)} %get-tuple-element.48.order_ref, bf16[4,128,128]{2,1,0:T(8,128)(2,1)S(1)} %multiply_convert_fusion.panel.refs_0_, bf16[4,128,128]{2,1,0:T(8,128)(2,1)S(1)} %collective-permute-done.2.refs_0_.refs_1_, bf16[4,128,128]{2,1,0:T(8,128)(2,1)S(1)} %collective-permute-done.3.refs_2_, ...), custom_call_target="tpu_custom_call" | custom-call | flops 100663296 | bytes 786432 | tf_op jit(solution)/shard_map/pallas_call | solution.py:336
  23.4 4.0 %collective-permute-done.7.refs_0_ = bf16[4,128,128]{2,1,0:T(8,128)(2,1)S(1)} collective-permute-done((bf16[4,128,128]{2,1,0:T(8,128)(2,1)S(1)}, bf16[4,128,128]{2,1,0:T(8,128)(2,1)S(1)}, u32[]{:S(2)}, u32[]{:S(2)}) %collective-permute-start.7) | collective-permute-done | bytes 131104 | tf_op jit(solution)/shard_map/ppermute | solution.py:358
  27.4 0.7 %shard_map.63 = bf16[4,128,128]{2,1,0:T(8,128)(2,1)} custom-call(f32[4,128,128]{2,1,0:T(8,128)S(1)} %get-tuple-element.29.factors, f32[4,128,128]{2,1,0:T(8,128)S(1)} %convert_add_fusion.own, bf16[4,128,128]{2,1,0:T(8,128)(2,1)S(1)} %collective-permute-done.7.refs_0_), custom_call_target="tpu_custom_call" | custom-call | tf_op jit(solution)/shard_map/pallas_call | solution.py:379
  (5 shorter events, 0.1 us)
Async XLA Ops:
  0.0 9.5 %collective-permute-start = (bf16[4,128,128]{2,1,0:T(8,128)(2,1)}, bf16[4,128,128]{2,1,0:T(8,128)(2,1)S(1)}, u32[]{:S(2)}, u32[]{:S(2)}) collective-permute-start(bf16[4,128,128]{2,1,0:T(8,128)(2,1)} %bitcast.7), channel_id=1, source_target_pairs={{0,18},{1,17},{2,16},{3,19},{16,2},{17,1},{18,0},{19,3},{4,22},{5,... | collective-permute-start | bytes 393224 | tf_op jit(solution)/shard_map/ppermute | solution.py:266
  4.9 4.6 %collective-permute-start.1 = (f32[4,128]{1,0:T(4,128)S(1)}, f32[4,128]{1,0:T(4,128)S(1)}, u32[]{:S(2)}, u32[]{:S(2)}) collective-permute-start(f32[4,128]{1,0:T(4,128)S(1)} %get-tuple-element.30), channel_id=1, source_target_pairs={{0,18},{1,17},{2,16},{3,19},{16,2},{17,1},{18,0},{19,3},{4,22},{5,... | collective-permute-start | bytes 6152 | tf_op jit(solution)/shard_map/ppermute | solution.py:266
  5.0 5.4 %collective-permute-start.2 = (bf16[4,128,128]{2,1,0:T(8,128)(2,1)S(1)}, bf16[4,128,128]{2,1,0:T(8,128)(2,1)S(1)}, u32[]{:S(2)}, u32[]{:S(2)}) collective-permute-start(bf16[4,128,128]{2,1,0:T(8,128)(2,1)S(1)} %get-tuple-element.35), channel_id=1, source_target_pairs={{0,16},{1,19},{2,18},{3,17},{16,0},{17,3},{18,2},{19,1},{4,20},{5,... | collective-permute-start | bytes 393224 | tf_op jit(solution)/shard_map/ppermute | solution.py:266
  9.6 1.9 %collective-permute-start.3 = (bf16[4,128,128]{2,1,0:T(8,128)(2,1)S(1)}, bf16[4,128,128]{2,1,0:T(8,128)(2,1)S(1)}, u32[]{:S(2)}, u32[]{:S(2)}) collective-permute-start(bf16[4,128,128]{2,1,0:T(8,128)(2,1)S(1)} %multiply_convert_fusion.panel.refs_0_), channel_id=1, source_target_pairs={{0,1},{1,0},{2,3},{3,2},{4,5},{5,4},{6,7},{7,6},{8,9},{9,8},{10,11... | collective-permute-start | bytes 393224 | tf_op jit(solution)/shard_map/ppermute | solution.py:269
  10.4 1.5 %collective-permute-start.4 = (bf16[4,128,128]{2,1,0:T(8,128)(2,1)S(1)}, bf16[4,128,128]{2,1,0:T(8,128)(2,1)S(1)}, u32[]{:S(2)}, u32[]{:S(2)}) collective-permute-start(bf16[4,128,128]{2,1,0:T(8,128)(2,1)S(1)} %collective-permute-done.2.refs_0_.refs_1_), channel_id=1, source_target_pairs={{0,1},{1,0},{2,3},{3,2},{4,5},{5,4},{6,7},{7,6},{8,9},{9,8},{10,11... | collective-permute-start | bytes 393224 | tf_op jit(solution)/shard_map/ppermute | solution.py:269
  13.2 5.0 %collective-permute-start.5 = (bf16[4,128,128]{2,1,0:T(8,128)(2,1)S(1)}, bf16[4,128,128]{2,1,0:T(8,128)(2,1)S(1)}, u32[]{:S(2)}, u32[]{:S(2)}) collective-permute-start(bf16[4,128,128]{2,1,0:T(8,128)(2,1)S(1)} %get-tuple-element.47), channel_id=1, source_target_pairs={{0,4},{1,9},{2,6},{3,11},{4,0},{5,13},{6,2},{7,15},{8,12},{9,1},{1... | collective-permute-start | bytes 393224 | tf_op jit(solution)/shard_map/ppermute | solution.py:358
  16.3 7.0 %collective-permute-start.6 = (bf16[4,128,128]{2,1,0:T(8,128)(2,1)S(1)}, bf16[4,128,128]{2,1,0:T(8,128)(2,1)S(1)}, u32[]{:S(2)}, u32[]{:S(2)}) collective-permute-start(bf16[4,128,128]{2,1,0:T(8,128)(2,1)S(1)} %get-tuple-element.49), channel_id=1, source_target_pairs={{0,4},{1,9},{2,6},{3,11},{4,0},{5,13},{6,2},{7,15},{8,12},{9,1},{1... | collective-permute-start | bytes 393224 | tf_op jit(solution)/shard_map/ppermute | solution.py:358
  18.2 9.2 %collective-permute-start.7 = (bf16[4,128,128]{2,1,0:T(8,128)(2,1)S(1)}, bf16[4,128,128]{2,1,0:T(8,128)(2,1)S(1)}, u32[]{:S(2)}, u32[]{:S(2)}) collective-permute-start(bf16[4,128,128]{2,1,0:T(8,128)(2,1)S(1)} %add_convert_fusion), channel_id=1, source_target_pairs={{0,8},{1,5},{2,10},{3,7},{4,12},{5,1},{6,14},{7,3},{8,0},{9,13},{1... | collective-permute-start | bytes 393224 | tf_op jit(solution)/shard_map/ppermute | solution.py:358

commit v5 on v4

--- a/solution.py
+++ b/solution.py
@@ -347,6 +347,7 @@
         )(ready, *panels, blocks)
 
     later = multiplied(5, far_tiles, order)
+    later, first = lax.optimization_barrier((later, first))
 
     def turned(value, even_hop, odd_hop):
         hops = (even_hop, odd_hop)

time: 27.8 us -> 28.7 us (1.032); the launches traced: 28.1 us -> 28.3 us
  Pallas kernels: 10 us -> 9.38 us
  starting transfers between devices: 13.1 us -> 13.7 us
    ppermute x3, starting transfers between devices: 6.61 us -> 7.21 us  [turned(): return lax.ppermute(value, ('grp', 'blk'), pairs)]
    pallas_call x2, Pallas kernels: 2.3 us -> 1.82 us  [multiplied(): pl.pallas_call(functools.partial(later_kernel, stage), out_shape=jax.Shap...]
  transfers between devices with their start and end apart: 8 -> 8, of which waited for: 4 -> 4; matrix products, arithmetic and copies ran while one was open for 1% -> 1% of each run, Pallas kernels for 29% -> 27%
where the time goes in v5:
time: 28.7 us; the launch traced here: 28.3 us
  starting transfers between devices  13.7 us (48%)
  Pallas kernels  9.38 us (33%)
  waiting for transfers between devices  4.82 us (17%)
    ppermute x3, starting transfers between devices, turned(): return lax.ppermute(value, ('grp', 'blk'), pairs)  7.21 us
    ppermute x3, starting transfers between devices, across(): return lax.ppermute(value, ('side', 'blk'), pairs)  5.92 us
    ppermute x3, waiting for transfers between devices, turned(): return lax.ppermute(value, ('grp', 'blk'), pairs)  4.39 us
    pallas_call x1, Pallas kernels, stage_blocks(): pl.pallas_call(functools.partial(stage_kernel, blks, groups, tiles_dev),...  2.46 us
    pallas_call x2, Pallas kernels, multiplied(): pl.pallas_call(functools.partial(later_kernel, stage), out_shape=jax.Shap...  1.82 us
    pallas_call x1, Pallas kernels, shards(): pl.pallas_call(first_kernel, out_shape=[jax.ShapeDtypeStruct(part, jnp.bf...  1.12 us
    pallas_call x1, Pallas kernels, shards(): pl.pallas_call(functools.partial(far_kernel, tiles_dev), out_shape=[jax.S...  1.05 us
    pallas_call x1, Pallas kernels, scale_rows(): pl.pallas_call(scale_kernel, out_shape=[jax.ShapeDtypeStruct(codes.shape,...  1 us
  transfers between devices with their start and end apart: 8, of which 4 were waited for; matrix products, arithmetic and copies ran while one was open for 1% of the time, Pallas kernels for 27%

profile of v5, /device:TPU:0, one launch (start us, length us, event | category | flops | bytes accessed | tf_op | source)
XLA Modules:
  0.0 28.3 jit_solution(6972478462694140344)
XLA Ops:
  0.0 3.9 %collective-permute-start = (bf16[4,128,128]{2,1,0:T(8,128)(2,1)}, bf16[4,128,128]{2,1,0:T(8,128)(2,1)S(1)}, u32[]{:S(2)}, u32[]{:S(2)}) collective-permute-start(bf16[4,128,128]{2,1,0:T(8,128)(2,1)} %bitcast.7), channel_id=1, source_target_pairs={{0,18},{1,17},{2,16},{3,19},{16,2},{17,1},{18,0},{19,3},{4,22},{5,... | collective-permute-start | bytes 393224 | tf_op jit(solution)/shard_map/ppermute | solution.py:266
  3.9 1.0 %shard_map.55 = (bf16[4,128,128]{2,1,0:T(8,128)(2,1)S(1)}, f32[4,128,128]{2,1,0:T(8,128)S(1)}, f32[4,128]{1,0:T(4,128)S(1)}) custom-call(s32[1,4]{1,0:T(1,128)} %exps_hbm.1, s32[1,512]{1,0:T(1,128)} %degrees_hbm.1, bf16[4,128,128]{2,1,0:T(8,128)(2,1)} %bitcast.8), custom_call_target="tpu_custom_call" | custom-call | flops 65536 | bytes 262144 | tf_op jit(solution)/shard_map/pallas_call | solution.py:56
  4.9 0.1 collective-permute-start.1
  5.0 2.0 %collective-permute-start.2 = (bf16[4,128,128]{2,1,0:T(8,128)(2,1)S(1)}, bf16[4,128,128]{2,1,0:T(8,128)(2,1)S(1)}, u32[]{:S(2)}, u32[]{:S(2)}) collective-permute-start(bf16[4,128,128]{2,1,0:T(8,128)(2,1)S(1)} %get-tuple-element.37), channel_id=1, source_target_pairs={{0,16},{1,19},{2,18},{3,17},{16,0},{17,3},{18,2},{19,1},{4,20},{5,... | collective-permute-start | bytes 393224 | tf_op jit(solution)/shard_map/ppermute | solution.py:266
  6.9 0.1 pad_add_fusion.place_ref
  7.0 2.5 %shard_map.56 = (s32[8,128]{1,0:T(8,128)S(1)}, bf16[96,128,128]{2,1,0:T(8,128)(2,1)S(1)}) custom-call(s32[2]{0:T(128)S(1)} %pad_add_fusion.place_ref, s32[2,96]{1,0:T(2,128)} %bitcast.9, bf16[96,128,128]{2,1,0:T(8,128)(2,1)} %bitcast.6), custom_call_target="tpu_custom_call" | custom-call | tf_op jit(solution)/shard_map/pallas_call | solution.py:155
  9.5 0.0 collective-permute-done.1
  9.5 0.1 multiply_convert_fusion.panel.refs_0_
  9.6 0.1 collective-permute-start.3
  9.7 0.6 %shard_map.57.refs_2_ = f32[5,128,128]{2,1,0:T(8,128)S(1)} custom-call(s32[8,128]{1,0:T(8,128)S(1)} %get-tuple-element.52.order_ref, bf16[4,128,128]{2,1,0:T(8,128)(2,1)S(1)} %multiply_convert_fusion.panel.refs_0_, bf16[96,128,128]{2,1,0:T(8,128)(2,1)S(1)} %get-tuple-element.38.blocks.refs_1_.refs_4_), custom_call_target="tpu_custom_call" | custom-call | flops 50331648 | bytes 393216 | tf_op jit(solution)/shard_map/pallas_call | solution.py:284
  10.4 0.1 collective-permute-done.2.refs_0_.refs_1_
  10.4 0.5 %collective-permute-start.4 = (bf16[4,128,128]{2,1,0:T(8,128)(2,1)S(1)}, bf16[4,128,128]{2,1,0:T(8,128)(2,1)S(1)}, u32[]{:S(2)}, u32[]{:S(2)}) collective-permute-start(bf16[4,128,128]{2,1,0:T(8,128)(2,1)S(1)} %collective-permute-done.2.refs_0_.refs_1_), channel_id=1, source_target_pairs={{0,1},{1,0},{2,3},{3,2},{4,5},{5,4},{6,7},{7,6},{8,9},{9,8},{10,11... | collective-permute-start | bytes 393224 | tf_op jit(solution)/shard_map/ppermute | solution.py:269
  10.9 0.6 %shard_map.58.refs_5_ = f32[5,128,128]{2,1,0:T(8,128)S(1)} custom-call(s32[8,128]{1,0:T(8,128)S(1)} %get-tuple-element.52.order_ref, bf16[4,128,128]{2,1,0:T(8,128)(2,1)S(1)} %collective-permute-done.2.refs_0_.refs_1_, bf16[96,128,128]{2,1,0:T(8,128)(2,1)S(1)} %get-tuple-element.38.blocks.refs_1_.refs_4_, ...), custom_call_target="tpu_custom_call", output_to_operand_aliasing={{}: (3, {})} | custom-call | flops 50331648 | bytes 393216 | tf_op jit(solution)/shard_map/pallas_call | solution.py:294
  11.6 0.4 %collective-permute-done.4.refs_3_ = bf16[4,128,128]{2,1,0:T(8,128)(2,1)S(1)} collective-permute-done((bf16[4,128,128]{2,1,0:T(8,128)(2,1)S(1)}, bf16[4,128,128]{2,1,0:T(8,128)(2,1)S(1)}, u32[]{:S(2)}, u32[]{:S(2)}) %collective-permute-start.4) | collective-permute-done | bytes 131104 | tf_op jit(solution)/shard_map/ppermute | solution.py:269
  11.9 1.1 %shard_map.59 = (bf16[4,128,128]{2,1,0:T(8,128)(2,1)S(1)}, f32[5,128,128]{2,1,0:T(8,128)S(1)}, f32[5,128,128]{2,1,0:T(8,128)S(1)}) custom-call(s32[8,128]{1,0:T(8,128)S(1)} %get-tuple-element.52.order_ref, bf16[4,128,128]{2,1,0:T(8,128)(2,1)S(1)} %multiply_convert_fusion.panel.refs_0_, ...), custom_call_target="tpu_custom_call", output_to_operand_aliasing={{2}: (6, {})} | custom-call | flops 50331648 | bytes 393216 | tf_op jit(solution)/shard_map/pallas_call | solution.py:306
  13.0 2.1 %collective-permute-start.5 = (bf16[4,128,128]{2,1,0:T(8,128)(2,1)S(1)}, bf16[4,128,128]{2,1,0:T(8,128)(2,1)S(1)}, u32[]{:S(2)}, u32[]{:S(2)}) collective-permute-start(bf16[4,128,128]{2,1,0:T(8,128)(2,1)S(1)} %get-tuple-element.51), channel_id=1, source_target_pairs={{0,4},{1,9},{2,6},{3,11},{4,0},{5,13},{6,2},{7,15},{8,12},{9,1},{1... | collective-permute-start | bytes 393224 | tf_op jit(solution)/shard_map/ppermute | solution.py:359
  15.0 1.1 %shard_map.60 = (bf16[4,128,128]{2,1,0:T(8,128)(2,1)S(1)}, f32[5,128,128]{2,1,0:T(8,128)S(1)}) custom-call(s32[8,128]{1,0:T(8,128)S(1)} %get-tuple-element.52.order_ref, bf16[4,128,128]{2,1,0:T(8,128)(2,1)S(1)} %multiply_convert_fusion.panel.refs_0_, ...), custom_call_target="tpu_custom_call", output_to_operand_aliasing={{1}: (6, {})} | custom-call | flops 100663296 | bytes 786432 | tf_op jit(solution)/shard_map/pallas_call | solution.py:321
  16.2 0.9 %shard_map.61 = f32[4,128,128]{2,1,0:T(8,128)S(1)} custom-call(s32[8,128]{1,0:T(8,128)S(1)} %get-tuple-element.52.order_ref, bf16[4,128,128]{2,1,0:T(8,128)(2,1)S(1)} %multiply_convert_fusion.panel.refs_0_, bf16[4,128,128]{2,1,0:T(8,128)(2,1)S(1)} %collective-permute-done.2.refs_0_.refs_1_, bf16[4,128,128]{2,1,0:T(8,128)(2,1)S(1)} %collective-permute-done.3.refs_2_, ...), custom_call_target="tpu_custom_call" | custom-call | flops 100663296 | bytes 786432 | tf_op jit(solution)/shard_map/pallas_call | solution.py:336
  17.1 0.6 %collective-permute-start.6 = (bf16[4,128,128]{2,1,0:T(8,128)(2,1)S(1)}, bf16[4,128,128]{2,1,0:T(8,128)(2,1)S(1)}, u32[]{:S(2)}, u32[]{:S(2)}) collective-permute-start(bf16[4,128,128]{2,1,0:T(8,128)(2,1)S(1)} %get-tuple-element.53), channel_id=1, source_target_pairs={{0,4},{1,9},{2,6},{3,11},{4,0},{5,13},{6,2},{7,15},{8,12},{9,1},{1... | collective-permute-start | bytes 393224 | tf_op jit(solution)/shard_map/ppermute | solution.py:359
  17.7 0.4 %collective-permute-done.5 = bf16[4,128,128]{2,1,0:T(8,128)(2,1)S(1)} collective-permute-done((bf16[4,128,128]{2,1,0:T(8,128)(2,1)S(1)}, bf16[4,128,128]{2,1,0:T(8,128)(2,1)S(1)}, u32[]{:S(2)}, u32[]{:S(2)}) %collective-permute-start.5) | collective-permute-done | bytes 131104 | tf_op jit(solution)/shard_map/ppermute | solution.py:359
  18.0 4.6 %collective-permute-start.7 = (bf16[4,128,128]{2,1,0:T(8,128)(2,1)S(1)}, bf16[4,128,128]{2,1,0:T(8,128)(2,1)S(1)}, u32[]{:S(2)}, u32[]{:S(2)}) collective-permute-start(bf16[4,128,128]{2,1,0:T(8,128)(2,1)S(1)} %add_convert_fusion), channel_id=1, source_target_pairs={{0,8},{1,5},{2,10},{3,7},{4,12},{5,1},{6,14},{7,3},{8,0},{9,13},{1... | collective-permute-start | bytes 393224 | tf_op jit(solution)/shard_map/ppermute | solution.py:359
  22.6 0.9 %shard_map.62 = f32[4,128,128]{2,1,0:T(8,128)S(1)} custom-call(s32[8,128]{1,0:T(8,128)S(1)} %get-tuple-element.52.order_ref, bf16[4,128,128]{2,1,0:T(8,128)(2,1)S(1)} %multiply_convert_fusion.panel.refs_0_, bf16[4,128,128]{2,1,0:T(8,128)(2,1)S(1)} %collective-permute-done.2.refs_0_.refs_1_, bf16[4,128,128]{2,1,0:T(8,128)(2,1)S(1)} %collective-permute-done.3.refs_2_, ...), custom_call_target="tpu_custom_call" | custom-call | flops 100663296 | bytes 786432 | tf_op jit(solution)/shard_map/pallas_call | solution.py:336
  23.6 4.0 %collective-permute-done.7.refs_0_ = bf16[4,128,128]{2,1,0:T(8,128)(2,1)S(1)} collective-permute-done((bf16[4,128,128]{2,1,0:T(8,128)(2,1)S(1)}, bf16[4,128,128]{2,1,0:T(8,128)(2,1)S(1)}, u32[]{:S(2)}, u32[]{:S(2)}) %collective-permute-start.7) | collective-permute-done | bytes 131104 | tf_op jit(solution)/shard_map/ppermute | solution.py:359
  27.6 0.7 %shard_map.63 = bf16[4,128,128]{2,1,0:T(8,128)(2,1)} custom-call(f32[4,128,128]{2,1,0:T(8,128)S(1)} %get-tuple-element.31.factors, f32[4,128,128]{2,1,0:T(8,128)S(1)} %convert_add_fusion.own, bf16[4,128,128]{2,1,0:T(8,128)(2,1)S(1)} %collective-permute-done.7.refs_0_), custom_call_target="tpu_custom_call" | custom-call | tf_op jit(solution)/shard_map/pallas_call | solution.py:380
  (5 shorter events, 0.1 us)
Async XLA Ops:
  0.0 9.5 %collective-permute-start = (bf16[4,128,128]{2,1,0:T(8,128)(2,1)}, bf16[4,128,128]{2,1,0:T(8,128)(2,1)S(1)}, u32[]{:S(2)}, u32[]{:S(2)}) collective-permute-start(bf16[4,128,128]{2,1,0:T(8,128)(2,1)} %bitcast.7), channel_id=1, source_target_pairs={{0,18},{1,17},{2,16},{3,19},{16,2},{17,1},{18,0},{19,3},{4,22},{5,... | collective-permute-start | bytes 393224 | tf_op jit(solution)/shard_map/ppermute | solution.py:266
  4.9 4.6 %collective-permute-start.1 = (f32[4,128]{1,0:T(4,128)S(1)}, f32[4,128]{1,0:T(4,128)S(1)}, u32[]{:S(2)}, u32[]{:S(2)}) collective-permute-start(f32[4,128]{1,0:T(4,128)S(1)} %get-tuple-element.32), channel_id=1, source_target_pairs={{0,18},{1,17},{2,16},{3,19},{16,2},{17,1},{18,0},{19,3},{4,22},{5,... | collective-permute-start | bytes 6152 | tf_op jit(solution)/shard_map/ppermute | solution.py:266
  5.0 5.4 %collective-permute-start.2 = (bf16[4,128,128]{2,1,0:T(8,128)(2,1)S(1)}, bf16[4,128,128]{2,1,0:T(8,128)(2,1)S(1)}, u32[]{:S(2)}, u32[]{:S(2)}) collective-permute-start(bf16[4,128,128]{2,1,0:T(8,128)(2,1)S(1)} %get-tuple-element.37), channel_id=1, source_target_pairs={{0,16},{1,19},{2,18},{3,17},{16,0},{17,3},{18,2},{19,1},{4,20},{5,... | collective-permute-start | bytes 393224 | tf_op jit(solution)/shard_map/ppermute | solution.py:266
  9.6 1.9 %collective-permute-start.3 = (bf16[4,128,128]{2,1,0:T(8,128)(2,1)S(1)}, bf16[4,128,128]{2,1,0:T(8,128)(2,1)S(1)}, u32[]{:S(2)}, u32[]{:S(2)}) collective-permute-start(bf16[4,128,128]{2,1,0:T(8,128)(2,1)S(1)} %multiply_convert_fusion.panel.refs_0_), channel_id=1, source_target_pairs={{0,1},{1,0},{2,3},{3,2},{4,5},{5,4},{6,7},{7,6},{8,9},{9,8},{10,11... | collective-permute-start | bytes 393224 | tf_op jit(solution)/shard_map/ppermute | solution.py:269
  10.4 1.5 %collective-permute-start.4 = (bf16[4,128,128]{2,1,0:T(8,128)(2,1)S(1)}, bf16[4,128,128]{2,1,0:T(8,128)(2,1)S(1)}, u32[]{:S(2)}, u32[]{:S(2)}) collective-permute-start(bf16[4,128,128]{2,1,0:T(8,128)(2,1)S(1)} %collective-permute-done.2.refs_0_.refs_1_), channel_id=1, source_target_pairs={{0,1},{1,0},{2,3},{3,2},{4,5},{5,4},{6,7},{7,6},{8,9},{9,8},{10,11... | collective-permute-start | bytes 393224 | tf_op jit(solution)/shard_map/ppermute | solution.py:269
  13.0 5.0 %collective-permute-start.5 = (bf16[4,128,128]{2,1,0:T(8,128)(2,1)S(1)}, bf16[4,128,128]{2,1,0:T(8,128)(2,1)S(1)}, u32[]{:S(2)}, u32[]{:S(2)}) collective-permute-start(bf16[4,128,128]{2,1,0:T(8,128)(2,1)S(1)} %get-tuple-element.51), channel_id=1, source_target_pairs={{0,4},{1,9},{2,6},{3,11},{4,0},{5,13},{6,2},{7,15},{8,12},{9,1},{1... | collective-permute-start | bytes 393224 | tf_op jit(solution)/shard_map/ppermute | solution.py:359
  17.1 6.5 %collective-permute-start.6 = (bf16[4,128,128]{2,1,0:T(8,128)(2,1)S(1)}, bf16[4,128,128]{2,1,0:T(8,128)(2,1)S(1)}, u32[]{:S(2)}, u32[]{:S(2)}) collective-permute-start(bf16[4,128,128]{2,1,0:T(8,128)(2,1)S(1)} %get-tuple-element.53), channel_id=1, source_target_pairs={{0,4},{1,9},{2,6},{3,11},{4,0},{5,13},{6,2},{7,15},{8,12},{9,1},{1... | collective-permute-start | bytes 393224 | tf_op jit(solution)/shard_map/ppermute | solution.py:359
  18.0 9.6 %collective-permute-start.7 = (bf16[4,128,128]{2,1,0:T(8,128)(2,1)S(1)}, bf16[4,128,128]{2,1,0:T(8,128)(2,1)S(1)}, u32[]{:S(2)}, u32[]{:S(2)}) collective-permute-start(bf16[4,128,128]{2,1,0:T(8,128)(2,1)S(1)} %add_convert_fusion), channel_id=1, source_target_pairs={{0,8},{1,5},{2,10},{3,7},{4,12},{5,1},{6,14},{7,3},{8,0},{9,13},{1... | collective-permute-start | bytes 393224 | tf_op jit(solution)/shard_map/ppermute | solution.py:359

commit v6 on v2

--- a/solution.py
+++ b/solution.py
@@ -102,7 +102,7 @@
     hop = hop ^ my_blk
     chunk = chunk ^ my_grp
     odd = hop & 1
-    rank = jnp.where(odd == role, half - 1 - (hop >> 1), hop >> 1)
+    rank = jnp.where(odd == role, hop >> 1, half - 1 - (hop >> 1))
     far = (chunk >= 2) & ((chunk & 1) == 1)
     kept = jnp.where(chunk == 1, 1 + role * (groups // 2 - 1), (chunk >> 1) + 1 - role)
     kept = jnp.where(chunk == 0, 0, jnp.where(far, (chunk >> 1) - 1, kept))
@@ -261,7 +261,7 @@
 
     def across(value, step):
         pairs = [
-            (side * blks + at, (1 - side) * blks + (at ^ (2 * step if at & 1 else blks - 2 - 2 * step)))
+            (side * blks + at, (1 - side) * blks + (at ^ (blks - 2 - 2 * step if at & 1 else 2 * step)))
             for side in range(2)
             for at in range(blks)
         ]

time: 28 us -> 27.2 us (0.971); the launches traced: 28.5 us -> 27.1 us
  waiting for transfers between devices: 6.51 us -> 4.72 us
  starting transfers between devices: 11.3 us -> 12.3 us
  Pallas kernels: 10.2 us -> 9.77 us
    ppermute x3, waiting for transfers between devices: 6.08 us -> 3.85 us  [turned(): return lax.ppermute(value, ('grp', 'blk'), pairs)]
    ppermute x3, starting transfers between devices: 4.46 us -> 6.22 us  [turned(): return lax.ppermute(value, ('grp', 'blk'), pairs)]
    ppermute x2, starting transfers between devices: 0.94 us -> 0.07 us  [paired(): lax.ppermute(value, axis, [(at, at ^ hop) for at in range(lax.axis_size(a...]
    pallas_call x1, Pallas kernels: 1.61 us -> 1.05 us  [shards(): pl.pallas_call(functools.partial(far_kernel, tiles_dev), out_shape=[jax.S...]
    pallas_call x1, Pallas kernels: 0.62 us -> 1.18 us  [shards(): pl.pallas_call(early_kernel, out_shape=jax.ShapeDtypeStruct((far_tiles +...]
    ppermute x2, waiting for transfers between devices: 0.36 us -> 0.72 us  [paired(): lax.ppermute(value, axis, [(at, at ^ hop) for at in range(lax.axis_size(a...]
  transfers between devices with their start and end apart: 8 -> 8, of which waited for: 4 -> 4; matrix products, arithmetic and copies ran while one was open for 1% -> 1% of each run, Pallas kernels for 28% -> 30%
where the time goes in v6:
time: 27.2 us; the launch traced here: 27.1 us
  starting transfers between devices  12.3 us (45%)
  Pallas kernels  9.77 us (36%)
  waiting for transfers between devices  4.72 us (17%)
    ppermute x3, starting transfers between devices, turned(): return lax.ppermute(value, ('grp', 'blk'), pairs)  6.22 us
    ppermute x3, starting transfers between devices, across(): return lax.ppermute(value, ('side', 'blk'), pairs)  5.98 us
    ppermute x3, waiting for transfers between devices, turned(): return lax.ppermute(value, ('grp', 'blk'), pairs)  3.85 us
    pallas_call x1, Pallas kernels, stage_blocks(): pl.pallas_call(functools.partial(stage_kernel, blks, groups, tiles_dev),...  2.46 us
    pallas_call x1, Pallas kernels, shards(): pl.pallas_call(rest_kernel, out_shape=[jax.ShapeDtypeStruct(part, jnp.flo...  1.65 us
    pallas_call x1, Pallas kernels, shards(): pl.pallas_call(early_kernel, out_shape=jax.ShapeDtypeStruct((far_tiles +...  1.18 us
    pallas_call x1, Pallas kernels, shards(): pl.pallas_call(first_kernel, out_shape=[jax.ShapeDtypeStruct(part, jnp.bf...  1.12 us
    pallas_call x1, Pallas kernels, shards(): pl.pallas_call(functools.partial(far_kernel, tiles_dev), out_shape=[jax.S...  1.05 us
  transfers between devices with their start and end apart: 8, of which 4 were waited for; matrix products, arithmetic and copies ran while one was open for 1% of the time, Pallas kernels for 30%

profile of v6, /device:TPU:0, one launch (start us, length us, event | category | flops | bytes accessed | tf_op | source)
XLA Modules:
  0.0 27.1 jit_solution(12159609621801619374)
XLA Ops:
  0.0 2.9 %collective-permute-start = (bf16[4,128,128]{2,1,0:T(8,128)(2,1)}, bf16[4,128,128]{2,1,0:T(8,128)(2,1)S(1)}, u32[]{:S(2)}, u32[]{:S(2)}) collective-permute-start(bf16[4,128,128]{2,1,0:T(8,128)(2,1)} %bitcast.7), channel_id=1, source_target_pairs={{0,16},{1,19},{2,18},{3,17},{16,0},{17,3},{18,2},{19,1},{4,20},{5,... | collective-permute-start | bytes 393224 | tf_op jit(solution)/shard_map/ppermute | solution.py:268
  2.9 1.0 %shard_map.55 = (bf16[4,128,128]{2,1,0:T(8,128)(2,1)S(1)}, f32[4,128,128]{2,1,0:T(8,128)S(1)}, f32[4,128]{1,0:T(4,128)S(1)}) custom-call(s32[1,4]{1,0:T(1,128)} %exps_hbm.1, s32[1,512]{1,0:T(1,128)} %degrees_hbm.1, bf16[4,128,128]{2,1,0:T(8,128)(2,1)} %bitcast.8), custom_call_target="tpu_custom_call" | custom-call | flops 65536 | bytes 262144 | tf_op jit(solution)/shard_map/pallas_call | solution.py:56
  4.0 0.1 collective-permute-start.1
  4.0 3.0 %collective-permute-start.2 = (bf16[4,128,128]{2,1,0:T(8,128)(2,1)S(1)}, bf16[4,128,128]{2,1,0:T(8,128)(2,1)S(1)}, u32[]{:S(2)}, u32[]{:S(2)}) collective-permute-start(bf16[4,128,128]{2,1,0:T(8,128)(2,1)S(1)} %get-tuple-element.35), channel_id=1, source_target_pairs={{0,18},{1,17},{2,16},{3,19},{16,2},{17,1},{18,0},{19,3},{4,22},{5,... | collective-permute-start | bytes 393224 | tf_op jit(solution)/shard_map/ppermute | solution.py:268
  7.0 0.1 pad_add_fusion.place_ref
  7.1 2.5 %shard_map.56 = (s32[8,128]{1,0:T(8,128)S(1)}, bf16[96,128,128]{2,1,0:T(8,128)(2,1)S(1)}) custom-call(s32[2]{0:T(128)S(1)} %pad_add_fusion.place_ref, s32[2,96]{1,0:T(2,128)} %bitcast.9, bf16[96,128,128]{2,1,0:T(8,128)(2,1)} %bitcast.6), custom_call_target="tpu_custom_call" | custom-call | tf_op jit(solution)/shard_map/pallas_call | solution.py:155
  9.5 0.0 collective-permute-done.1
  9.6 0.0 collective-permute-done
  9.6 0.1 multiply_convert_fusion.panel.refs_0_
  9.7 0.1 collective-permute-start.3
  9.8 1.2 %shard_map.57.refs_2_ = f32[5,128,128]{2,1,0:T(8,128)S(1)} custom-call(s32[8,128]{1,0:T(8,128)S(1)} %get-tuple-element.46.order_ref, bf16[4,128,128]{2,1,0:T(8,128)(2,1)S(1)} %multiply_convert_fusion.panel.refs_0_, bf16[96,128,128]{2,1,0:T(8,128)(2,1)S(1)} %get-tuple-element.36.blocks.refs_1_.refs_4_), custom_call_target="tpu_custom_call" | custom-call | flops 50331648 | bytes 393216 | tf_op jit(solution)/shard_map/pallas_call | solution.py:286
  11.0 0.1 collective-permute-done.2.refs_0_.refs_1_
  11.1 0.6 %shard_map.58.refs_5_ = f32[5,128,128]{2,1,0:T(8,128)S(1)} custom-call(s32[8,128]{1,0:T(8,128)S(1)} %get-tuple-element.46.order_ref, bf16[4,128,128]{2,1,0:T(8,128)(2,1)S(1)} %collective-permute-done.2.refs_0_.refs_1_, bf16[96,128,128]{2,1,0:T(8,128)(2,1)S(1)} %get-tuple-element.36.blocks.refs_1_.refs_4_, ...), custom_call_target="tpu_custom_call", output_to_operand_aliasing={{}: (3, {})} | custom-call | flops 50331648 | bytes 393216 | tf_op jit(solution)/shard_map/pallas_call | solution.py:296
  11.7 0.7 %collective-permute-done.4.refs_3_ = bf16[4,128,128]{2,1,0:T(8,128)(2,1)S(1)} collective-permute-done((bf16[4,128,128]{2,1,0:T(8,128)(2,1)S(1)}, bf16[4,128,128]{2,1,0:T(8,128)(2,1)S(1)}, u32[]{:S(2)}, u32[]{:S(2)}) %collective-permute-start.4) | collective-permute-done | bytes 131104 | tf_op jit(solution)/shard_map/ppermute | solution.py:271
  12.5 1.1 %shard_map.59 = (bf16[4,128,128]{2,1,0:T(8,128)(2,1)S(1)}, f32[5,128,128]{2,1,0:T(8,128)S(1)}, f32[5,128,128]{2,1,0:T(8,128)S(1)}) custom-call(s32[8,128]{1,0:T(8,128)S(1)} %get-tuple-element.46.order_ref, bf16[4,128,128]{2,1,0:T(8,128)(2,1)S(1)} %multiply_convert_fusion.panel.refs_0_, ...), custom_call_target="tpu_custom_call", output_to_operand_aliasing={{2}: (6, {})} | custom-call | flops 50331648 | bytes 393216 | tf_op jit(solution)/shard_map/pallas_call | solution.py:308
  13.5 1.5 %collective-permute-start.6 = (bf16[4,128,128]{2,1,0:T(8,128)(2,1)S(1)}, bf16[4,128,128]{2,1,0:T(8,128)(2,1)S(1)}, u32[]{:S(2)}, u32[]{:S(2)}) collective-permute-start(bf16[4,128,128]{2,1,0:T(8,128)(2,1)S(1)} %get-tuple-element.50), channel_id=1, source_target_pairs={{0,4},{1,9},{2,6},{3,11},{4,0},{5,13},{6,2},{7,15},{8,12},{9,1},{1... | collective-permute-start | bytes 393224 | tf_op jit(solution)/shard_map/ppermute | solution.py:360
  15.0 1.1 %shard_map.60 = (bf16[4,128,128]{2,1,0:T(8,128)(2,1)S(1)}, f32[5,128,128]{2,1,0:T(8,128)S(1)}) custom-call(s32[8,128]{1,0:T(8,128)S(1)} %get-tuple-element.46.order_ref, bf16[4,128,128]{2,1,0:T(8,128)(2,1)S(1)} %multiply_convert_fusion.panel.refs_0_, ...), custom_call_target="tpu_custom_call", output_to_operand_aliasing={{1}: (6, {})} | custom-call | flops 100663296 | bytes 786432 | tf_op jit(solution)/shard_map/pallas_call | solution.py:323
  16.1 0.7 %collective-permute-start.5 = (bf16[4,128,128]{2,1,0:T(8,128)(2,1)S(1)}, bf16[4,128,128]{2,1,0:T(8,128)(2,1)S(1)}, u32[]{:S(2)}, u32[]{:S(2)}) collective-permute-start(bf16[4,128,128]{2,1,0:T(8,128)(2,1)S(1)} %get-tuple-element.48), channel_id=1, source_target_pairs={{0,4},{1,9},{2,6},{3,11},{4,0},{5,13},{6,2},{7,15},{8,12},{9,1},{1... | collective-permute-start | bytes 393224 | tf_op jit(solution)/shard_map/ppermute | solution.py:360
  16.8 1.7 %shard_map.61 = (f32[4,128,128]{2,1,0:T(8,128)S(1)}, f32[4,128,128]{2,1,0:T(8,128)S(1)}) custom-call(s32[8,128]{1,0:T(8,128)S(1)} %get-tuple-element.46.order_ref, bf16[4,128,128]{2,1,0:T(8,128)(2,1)S(1)} %multiply_convert_fusion.panel.refs_0_, bf16[4,128,128]{2,1,0:T(8,128)(2,1)S(1)} %collective-permute-done.2.refs_0_.refs_1_, ...), custom_call_target="tpu_custom_call" | custom-call | flops 201326592 | bytes 1572864 | tf_op jit(solution)/shard_map/pallas_call | solution.py:337
  18.5 0.1 collective-permute-done.6
  18.6 4.1 %collective-permute-start.7 = (bf16[4,128,128]{2,1,0:T(8,128)(2,1)S(1)}, bf16[4,128,128]{2,1,0:T(8,128)(2,1)S(1)}, u32[]{:S(2)}, u32[]{:S(2)}) collective-permute-start(bf16[4,128,128]{2,1,0:T(8,128)(2,1)S(1)} %add_convert_fusion), channel_id=1, source_target_pairs={{0,8},{1,5},{2,10},{3,7},{4,12},{5,1},{6,14},{7,3},{8,0},{9,13},{1... | collective-permute-start | bytes 393224 | tf_op jit(solution)/shard_map/ppermute | solution.py:360
  22.7 0.0 collective-permute-done.5
  22.7 3.8 %collective-permute-done.7.refs_0_ = bf16[4,128,128]{2,1,0:T(8,128)(2,1)S(1)} collective-permute-done((bf16[4,128,128]{2,1,0:T(8,128)(2,1)S(1)}, bf16[4,128,128]{2,1,0:T(8,128)(2,1)S(1)}, u32[]{:S(2)}, u32[]{:S(2)}) %collective-permute-start.7) | collective-permute-done | bytes 131104 | tf_op jit(solution)/shard_map/ppermute | solution.py:360
  26.4 0.7 %shard_map.62 = bf16[4,128,128]{2,1,0:T(8,128)(2,1)} custom-call(f32[4,128,128]{2,1,0:T(8,128)S(1)} %get-tuple-element.29.factors, f32[4,128,128]{2,1,0:T(8,128)S(1)} %convert_add_fusion.own, bf16[4,128,128]{2,1,0:T(8,128)(2,1)S(1)} %collective-permute-done.7.refs_0_), custom_call_target="tpu_custom_call" | custom-call | tf_op jit(solution)/shard_map/pallas_call | solution.py:380
  (4 shorter events, 0.1 us)
Async XLA Ops:
  0.0 9.6 %collective-permute-start = (bf16[4,128,128]{2,1,0:T(8,128)(2,1)}, bf16[4,128,128]{2,1,0:T(8,128)(2,1)S(1)}, u32[]{:S(2)}, u32[]{:S(2)}) collective-permute-start(bf16[4,128,128]{2,1,0:T(8,128)(2,1)} %bitcast.7), channel_id=1, source_target_pairs={{0,16},{1,19},{2,18},{3,17},{16,0},{17,3},{18,2},{19,1},{4,20},{5,... | collective-permute-start | bytes 393224 | tf_op jit(solution)/shard_map/ppermute | solution.py:268
  4.0 5.6 %collective-permute-start.1 = (f32[4,128]{1,0:T(4,128)S(1)}, f32[4,128]{1,0:T(4,128)S(1)}, u32[]{:S(2)}, u32[]{:S(2)}) collective-permute-start(f32[4,128]{1,0:T(4,128)S(1)} %get-tuple-element.30), channel_id=1, source_target_pairs={{0,16},{1,19},{2,18},{3,17},{16,0},{17,3},{18,2},{19,1},{4,20},{5,... | collective-permute-start | bytes 6152 | tf_op jit(solution)/shard_map/ppermute | solution.py:268
  4.0 7.1 %collective-permute-start.2 = (bf16[4,128,128]{2,1,0:T(8,128)(2,1)S(1)}, bf16[4,128,128]{2,1,0:T(8,128)(2,1)S(1)}, u32[]{:S(2)}, u32[]{:S(2)}) collective-permute-start(bf16[4,128,128]{2,1,0:T(8,128)(2,1)S(1)} %get-tuple-element.35), channel_id=1, source_target_pairs={{0,18},{1,17},{2,16},{3,19},{16,2},{17,1},{18,0},{19,3},{4,22},{5,... | collective-permute-start | bytes 393224 | tf_op jit(solution)/shard_map/ppermute | solution.py:268
  9.7 2.0 %collective-permute-start.3 = (bf16[4,128,128]{2,1,0:T(8,128)(2,1)S(1)}, bf16[4,128,128]{2,1,0:T(8,128)(2,1)S(1)}, u32[]{:S(2)}, u32[]{:S(2)}) collective-permute-start(bf16[4,128,128]{2,1,0:T(8,128)(2,1)S(1)} %multiply_convert_fusion.panel.refs_0_), channel_id=1, source_target_pairs={{0,1},{1,0},{2,3},{3,2},{4,5},{5,4},{6,7},{7,6},{8,9},{9,8},{10,11... | collective-permute-start | bytes 393224 | tf_op jit(solution)/shard_map/ppermute | solution.py:271
  11.1 1.3 %collective-permute-start.4 = (bf16[4,128,128]{2,1,0:T(8,128)(2,1)S(1)}, bf16[4,128,128]{2,1,0:T(8,128)(2,1)S(1)}, u32[]{:S(2)}, u32[]{:S(2)}) collective-permute-start(bf16[4,128,128]{2,1,0:T(8,128)(2,1)S(1)} %collective-permute-done.2.refs_0_.refs_1_), channel_id=1, source_target_pairs={{0,1},{1,0},{2,3},{3,2},{4,5},{5,4},{6,7},{7,6},{8,9},{9,8},{10,11... | collective-permute-start | bytes 393224 | tf_op jit(solution)/shard_map/ppermute | solution.py:271
  13.5 5.0 %collective-permute-start.6 = (bf16[4,128,128]{2,1,0:T(8,128)(2,1)S(1)}, bf16[4,128,128]{2,1,0:T(8,128)(2,1)S(1)}, u32[]{:S(2)}, u32[]{:S(2)}) collective-permute-start(bf16[4,128,128]{2,1,0:T(8,128)(2,1)S(1)} %get-tuple-element.50), channel_id=1, source_target_pairs={{0,4},{1,9},{2,6},{3,11},{4,0},{5,13},{6,2},{7,15},{8,12},{9,1},{1... | collective-permute-start | bytes 393224 | tf_op jit(solution)/shard_map/ppermute | solution.py:360
  16.1 6.6 %collective-permute-start.5 = (bf16[4,128,128]{2,1,0:T(8,128)(2,1)S(1)}, bf16[4,128,128]{2,1,0:T(8,128)(2,1)S(1)}, u32[]{:S(2)}, u32[]{:S(2)}) collective-permute-start(bf16[4,128,128]{2,1,0:T(8,128)(2,1)S(1)} %get-tuple-element.48), channel_id=1, source_target_pairs={{0,4},{1,9},{2,6},{3,11},{4,0},{5,13},{6,2},{7,15},{8,12},{9,1},{1... | collective-permute-start | bytes 393224 | tf_op jit(solution)/shard_map/ppermute | solution.py:360
  18.6 7.9 %collective-permute-start.7 = (bf16[4,128,128]{2,1,0:T(8,128)(2,1)S(1)}, bf16[4,128,128]{2,1,0:T(8,128)(2,1)S(1)}, u32[]{:S(2)}, u32[]{:S(2)}) collective-permute-start(bf16[4,128,128]{2,1,0:T(8,128)(2,1)S(1)} %add_convert_fusion), channel_id=1, source_target_pairs={{0,8},{1,5},{2,10},{3,7},{4,12},{5,1},{6,14},{7,3},{8,0},{9,13},{1... | collective-permute-start | bytes 393224 | tf_op jit(solution)/shard_map/ppermute | solution.py:360

commit v7 on v2

--- a/solution.py
+++ b/solution.py
@@ -169,8 +169,12 @@
     )(place, *in_hbm(index, blocks))
 
 
+def batches_of(stage, order_ref):
+    return order_ref[stage, order_ref.shape[1] - UNROLL]
+
+
 def add_products(stage, order_ref, blocks, source, total):
-    @pl.loop(0, order_ref[stage, order_ref.shape[1] - UNROLL])
+    @pl.loop(0, batches_of(stage, order_ref))
     def _(batch):
         made = []
         for part in range(BATCHES[stage]):
@@ -200,18 +204,28 @@
 
 def far_kernel(tiles_dev, order_ref, *refs):
     *panels, blocks, _, far, first, total, source = refs
-    others = len(panels) // 2 * tiles_dev
-    gather_panels(panels, source)
-    first[...] = jnp.zeros_like(first)
-    add_products(2, order_ref, blocks, source.at[others:], total)
-    add_products(3, order_ref, blocks, source, first)
+    half = len(panels) // 2
+    others = source.at[half * tiles_dev :]
+    gather_panels(panels[half:], others)
+    add_products(2, order_ref, blocks, others, total)
     far[...] = total[: far.shape[0]].astype(far.dtype)
+
+    @pl.when(batches_of(3, order_ref) > 0)
+    def _():
+        gather_panels(panels[:half], source)
+        first[...] = jnp.zeros_like(first)
+        add_products(3, order_ref, blocks, source, first)
 
 
 def first_kernel(order_ref, *refs):
     *panels, blocks, _, first, total, source = refs
-    gather_panels(panels, source)
-    add_products(4, order_ref, blocks, source, total)
+
+    @pl.when(batches_of(3, order_ref) == 0)
+    def _():
+        gather_panels(panels, source)
+        total[...] = jnp.zeros_like(total)
+        add_products(4, order_ref, blocks, source, total)
+
     first[...] = total[: first.shape[0]].astype(first.dtype)
 
 

time: 28 us -> 27.5 us (0.982)
  starting transfers between devices: 11.3 us -> 10.4 us
  Pallas kernels: 10.2 us -> 10.8 us
  waiting for transfers between devices: 6.51 us -> 6.21 us
    ppermute x2, starting transfers between devices: 0.94 us -> 0.14 us  [paired(): lax.ppermute(value, axis, [(at, at ^ hop) for at in range(lax.axis_size(a...]
    pallas_call x1, Pallas kernels: 0.62 us -> 1.36 us  [shards(): pl.pallas_call(early_kernel, out_shape=jax.ShapeDtypeStruct((far_tiles +...]
    ppermute x3, waiting for transfers between devices: 6.08 us -> 5.49 us  [turned(): return lax.ppermute(value, ('grp', 'blk'), pairs)]
    pallas_call x1, Pallas kernels: 1.61 us -> 1.2 us  [shards(): pl.pallas_call(functools.partial(far_kernel, tiles_dev), out_shape=[jax.S...]
    ppermute x2, waiting for transfers between devices: 0.36 us -> 0.71 us  [paired(): lax.ppermute(value, axis, [(at, at ^ hop) for at in range(lax.axis_size(a...]
  transfers between devices with their start and end apart: 8 -> 8, of which waited for: 4 -> 4; matrix products, arithmetic and copies ran while one was open for 1% -> 1% of each run, Pallas kernels for 28% -> 32%
where the time goes in v7:
time: 27.5 us; the launch traced here: 27.8 us
  Pallas kernels  10.8 us (39%)
  starting transfers between devices  10.4 us (38%)
  waiting for transfers between devices  6.21 us (23%)
    ppermute x3, starting transfers between devices, across(): return lax.ppermute(value, ('side', 'blk'), pairs)  5.92 us
    ppermute x3, waiting for transfers between devices, turned(): return lax.ppermute(value, ('grp', 'blk'), pairs)  5.49 us
    ppermute x3, starting transfers between devices, turned(): return lax.ppermute(value, ('grp', 'blk'), pairs)  4.32 us
    pallas_call x1, Pallas kernels, stage_blocks(): pl.pallas_call(functools.partial(stage_kernel, blks, groups, tiles_dev),...  2.46 us
    pallas_call x1, Pallas kernels, shards(): pl.pallas_call(rest_kernel, out_shape=[jax.ShapeDtypeStruct(part, jnp.flo...  2.12 us
    pallas_call x1, Pallas kernels, shards(): pl.pallas_call(first_kernel, out_shape=[jax.ShapeDtypeStruct(part, jnp.bf...  1.39 us
    pallas_call x1, Pallas kernels, shards(): pl.pallas_call(early_kernel, out_shape=jax.ShapeDtypeStruct((far_tiles +...  1.36 us
    pallas_call x1, Pallas kernels, shards(): pl.pallas_call(functools.partial(far_kernel, tiles_dev), out_shape=[jax.S...  1.2 us
  transfers between devices with their start and end apart: 8, of which 4 were waited for; matrix products, arithmetic and copies ran while one was open for 1% of the time, Pallas kernels for 32%

profile of v7, /device:TPU:0, one launch (start us, length us, event | category | flops | bytes accessed | tf_op | source)
XLA Modules:
  0.0 27.8 jit_solution(17219592599961762802)
XLA Ops:
  0.0 3.9 %collective-permute-start = (bf16[4,128,128]{2,1,0:T(8,128)(2,1)}, bf16[4,128,128]{2,1,0:T(8,128)(2,1)S(1)}, u32[]{:S(2)}, u32[]{:S(2)}) collective-permute-start(bf16[4,128,128]{2,1,0:T(8,128)(2,1)} %bitcast.7), channel_id=1, source_target_pairs={{0,18},{1,17},{2,16},{3,19},{16,2},{17,1},{18,0},{19,3},{4,22},{5,... | collective-permute-start | bytes 393224 | tf_op jit(solution)/shard_map/ppermute | solution.py:282
  3.9 1.0 %shard_map.55 = (bf16[4,128,128]{2,1,0:T(8,128)(2,1)S(1)}, f32[4,128,128]{2,1,0:T(8,128)S(1)}, f32[4,128]{1,0:T(4,128)S(1)}) custom-call(s32[1,4]{1,0:T(1,128)} %exps_hbm.1, s32[1,512]{1,0:T(1,128)} %degrees_hbm.1, bf16[4,128,128]{2,1,0:T(8,128)(2,1)} %bitcast.8), custom_call_target="tpu_custom_call" | custom-call | flops 65536 | bytes 262144 | tf_op jit(solution)/shard_map/pallas_call | solution.py:56
  4.9 0.1 collective-permute-start.1
  5.0 2.0 %collective-permute-start.2 = (bf16[4,128,128]{2,1,0:T(8,128)(2,1)S(1)}, bf16[4,128,128]{2,1,0:T(8,128)(2,1)S(1)}, u32[]{:S(2)}, u32[]{:S(2)}) collective-permute-start(bf16[4,128,128]{2,1,0:T(8,128)(2,1)S(1)} %get-tuple-element.35), channel_id=1, source_target_pairs={{0,16},{1,19},{2,18},{3,17},{16,0},{17,3},{18,2},{19,1},{4,20},{5,... | collective-permute-start | bytes 393224 | tf_op jit(solution)/shard_map/ppermute | solution.py:282
  6.9 0.1 pad_add_fusion.place_ref
  7.0 2.5 %shard_map.56 = (s32[8,128]{1,0:T(8,128)S(1)}, bf16[96,128,128]{2,1,0:T(8,128)(2,1)S(1)}) custom-call(s32[2]{0:T(128)S(1)} %pad_add_fusion.place_ref, s32[2,96]{1,0:T(2,128)} %bitcast.9, bf16[96,128,128]{2,1,0:T(8,128)(2,1)} %bitcast.6), custom_call_target="tpu_custom_call" | custom-call | tf_op jit(solution)/shard_map/pallas_call | solution.py:155
  9.5 0.0 collective-permute-done.1
  9.5 0.0 collective-permute-done
  9.5 0.1 multiply_convert_fusion.panel.refs_0_
  9.6 0.1 collective-permute-start.3
  9.7 1.4 %shard_map.57.refs_2_ = f32[5,128,128]{2,1,0:T(8,128)S(1)} custom-call(s32[8,128]{1,0:T(8,128)S(1)} %get-tuple-element.46.order_ref, bf16[4,128,128]{2,1,0:T(8,128)(2,1)S(1)} %multiply_convert_fusion.panel.refs_0_, bf16[96,128,128]{2,1,0:T(8,128)(2,1)S(1)} %get-tuple-element.36.blocks.refs_1_.refs_4_), custom_call_target="tpu_custom_call" | custom-call | flops 50331648 | bytes 393216 | tf_op jit(solution)/shard_map/pallas_call | solution.py:300
  11.1 0.1 collective-permute-start.4
  11.2 0.6 %shard_map.58.refs_5_ = f32[5,128,128]{2,1,0:T(8,128)S(1)} custom-call(s32[8,128]{1,0:T(8,128)S(1)} %get-tuple-element.46.order_ref, bf16[4,128,128]{2,1,0:T(8,128)(2,1)S(1)} %collective-permute-done.2.refs_0_.refs_1_, bf16[96,128,128]{2,1,0:T(8,128)(2,1)S(1)} %get-tuple-element.36.blocks.refs_1_.refs_4_, ...), custom_call_target="tpu_custom_call", output_to_operand_aliasing={{}: (3, {})} | custom-call | flops 50331648 | bytes 393216 | tf_op jit(solution)/shard_map/pallas_call | solution.py:310
  11.8 0.7 %collective-permute-done.4.refs_3_ = bf16[4,128,128]{2,1,0:T(8,128)(2,1)S(1)} collective-permute-done((bf16[4,128,128]{2,1,0:T(8,128)(2,1)S(1)}, bf16[4,128,128]{2,1,0:T(8,128)(2,1)S(1)}, u32[]{:S(2)}, u32[]{:S(2)}) %collective-permute-start.4) | collective-permute-done | bytes 131104 | tf_op jit(solution)/shard_map/ppermute | solution.py:285
  12.5 1.2 %shard_map.59 = (bf16[4,128,128]{2,1,0:T(8,128)(2,1)S(1)}, f32[5,128,128]{2,1,0:T(8,128)S(1)}, f32[5,128,128]{2,1,0:T(8,128)S(1)}) custom-call(s32[8,128]{1,0:T(8,128)S(1)} %get-tuple-element.46.order_ref, bf16[4,128,128]{2,1,0:T(8,128)(2,1)S(1)} %multiply_convert_fusion.panel.refs_0_, ...), custom_call_target="tpu_custom_call", output_to_operand_aliasing={{2}: (6, {})} | custom-call | flops 50331648 | bytes 393216 | tf_op jit(solution)/shard_map/pallas_call | solution.py:322
  13.7 1.3 %collective-permute-start.6 = (bf16[4,128,128]{2,1,0:T(8,128)(2,1)S(1)}, bf16[4,128,128]{2,1,0:T(8,128)(2,1)S(1)}, u32[]{:S(2)}, u32[]{:S(2)}) collective-permute-start(bf16[4,128,128]{2,1,0:T(8,128)(2,1)S(1)} %get-tuple-element.50), channel_id=1, source_target_pairs={{0,4},{1,9},{2,6},{3,11},{4,0},{5,13},{6,2},{7,15},{8,12},{9,1},{1... | collective-permute-start | bytes 393224 | tf_op jit(solution)/shard_map/ppermute | solution.py:374
  15.0 1.4 %shard_map.60 = (bf16[4,128,128]{2,1,0:T(8,128)(2,1)S(1)}, f32[5,128,128]{2,1,0:T(8,128)S(1)}) custom-call(s32[8,128]{1,0:T(8,128)S(1)} %get-tuple-element.46.order_ref, bf16[4,128,128]{2,1,0:T(8,128)(2,1)S(1)} %multiply_convert_fusion.panel.refs_0_, ...), custom_call_target="tpu_custom_call", output_to_operand_aliasing={{1}: (6, {})} | custom-call | flops 100663296 | bytes 786432 | tf_op jit(solution)/shard_map/pallas_call | solution.py:337
  16.4 0.7 %collective-permute-start.5 = (bf16[4,128,128]{2,1,0:T(8,128)(2,1)S(1)}, bf16[4,128,128]{2,1,0:T(8,128)(2,1)S(1)}, u32[]{:S(2)}, u32[]{:S(2)}) collective-permute-start(bf16[4,128,128]{2,1,0:T(8,128)(2,1)S(1)} %get-tuple-element.48), channel_id=1, source_target_pairs={{0,4},{1,9},{2,6},{3,11},{4,0},{5,13},{6,2},{7,15},{8,12},{9,1},{1... | collective-permute-start | bytes 393224 | tf_op jit(solution)/shard_map/ppermute | solution.py:374
  17.0 2.1 %shard_map.61 = (f32[4,128,128]{2,1,0:T(8,128)S(1)}, f32[4,128,128]{2,1,0:T(8,128)S(1)}) custom-call(s32[8,128]{1,0:T(8,128)S(1)} %get-tuple-element.46.order_ref, bf16[4,128,128]{2,1,0:T(8,128)(2,1)S(1)} %multiply_convert_fusion.panel.refs_0_, bf16[4,128,128]{2,1,0:T(8,128)(2,1)S(1)} %collective-permute-done.2.refs_0_.refs_1_, ...), custom_call_target="tpu_custom_call" | custom-call | flops 201326592 | bytes 1572864 | tf_op jit(solution)/shard_map/pallas_call | solution.py:351
  19.2 0.6 %collective-permute-done.6 = bf16[4,128,128]{2,1,0:T(8,128)(2,1)S(1)} collective-permute-done((bf16[4,128,128]{2,1,0:T(8,128)(2,1)S(1)}, bf16[4,128,128]{2,1,0:T(8,128)(2,1)S(1)}, u32[]{:S(2)}, u32[]{:S(2)}) %collective-permute-start.6) | collective-permute-done | bytes 131104 | tf_op jit(solution)/shard_map/ppermute | solution.py:374
  19.8 2.4 %collective-permute-start.7 = (bf16[4,128,128]{2,1,0:T(8,128)(2,1)S(1)}, bf16[4,128,128]{2,1,0:T(8,128)(2,1)S(1)}, u32[]{:S(2)}, u32[]{:S(2)}) collective-permute-start(bf16[4,128,128]{2,1,0:T(8,128)(2,1)S(1)} %add_convert_fusion), channel_id=1, source_target_pairs={{0,8},{1,5},{2,10},{3,7},{4,12},{5,1},{6,14},{7,3},{8,0},{9,13},{1... | collective-permute-start | bytes 393224 | tf_op jit(solution)/shard_map/ppermute | solution.py:374
  22.2 0.9 %collective-permute-done.5 = bf16[4,128,128]{2,1,0:T(8,128)(2,1)S(1)} collective-permute-done((bf16[4,128,128]{2,1,0:T(8,128)(2,1)S(1)}, bf16[4,128,128]{2,1,0:T(8,128)(2,1)S(1)}, u32[]{:S(2)}, u32[]{:S(2)}) %collective-permute-start.5) | collective-permute-done | bytes 131104 | tf_op jit(solution)/shard_map/ppermute | solution.py:374
  23.1 4.0 %collective-permute-done.7.refs_0_ = bf16[4,128,128]{2,1,0:T(8,128)(2,1)S(1)} collective-permute-done((bf16[4,128,128]{2,1,0:T(8,128)(2,1)S(1)}, bf16[4,128,128]{2,1,0:T(8,128)(2,1)S(1)}, u32[]{:S(2)}, u32[]{:S(2)}) %collective-permute-start.7) | collective-permute-done | bytes 131104 | tf_op jit(solution)/shard_map/ppermute | solution.py:374
  27.1 0.7 %shard_map.62 = bf16[4,128,128]{2,1,0:T(8,128)(2,1)} custom-call(f32[4,128,128]{2,1,0:T(8,128)S(1)} %get-tuple-element.29.factors, f32[4,128,128]{2,1,0:T(8,128)S(1)} %convert_add_fusion.own, bf16[4,128,128]{2,1,0:T(8,128)(2,1)S(1)} %collective-permute-done.7.refs_0_), custom_call_target="tpu_custom_call" | custom-call | tf_op jit(solution)/shard_map/pallas_call | solution.py:394
  (4 shorter events, 0.1 us)
Async XLA Ops:
  0.0 9.5 %collective-permute-start = (bf16[4,128,128]{2,1,0:T(8,128)(2,1)}, bf16[4,128,128]{2,1,0:T(8,128)(2,1)S(1)}, u32[]{:S(2)}, u32[]{:S(2)}) collective-permute-start(bf16[4,128,128]{2,1,0:T(8,128)(2,1)} %bitcast.7), channel_id=1, source_target_pairs={{0,18},{1,17},{2,16},{3,19},{16,2},{17,1},{18,0},{19,3},{4,22},{5,... | collective-permute-start | bytes 393224 | tf_op jit(solution)/shard_map/ppermute | solution.py:282
  4.9 4.6 %collective-permute-start.1 = (f32[4,128]{1,0:T(4,128)S(1)}, f32[4,128]{1,0:T(4,128)S(1)}, u32[]{:S(2)}, u32[]{:S(2)}) collective-permute-start(f32[4,128]{1,0:T(4,128)S(1)} %get-tuple-element.30), channel_id=1, source_target_pairs={{0,18},{1,17},{2,16},{3,19},{16,2},{17,1},{18,0},{19,3},{4,22},{5,... | collective-permute-start | bytes 6152 | tf_op jit(solution)/shard_map/ppermute | solution.py:282
  5.0 6.1 %collective-permute-start.2 = (bf16[4,128,128]{2,1,0:T(8,128)(2,1)S(1)}, bf16[4,128,128]{2,1,0:T(8,128)(2,1)S(1)}, u32[]{:S(2)}, u32[]{:S(2)}) collective-permute-start(bf16[4,128,128]{2,1,0:T(8,128)(2,1)S(1)} %get-tuple-element.35), channel_id=1, source_target_pairs={{0,16},{1,19},{2,18},{3,17},{16,0},{17,3},{18,2},{19,1},{4,20},{5,... | collective-permute-start | bytes 393224 | tf_op jit(solution)/shard_map/ppermute | solution.py:282
  9.6 2.2 %collective-permute-start.3 = (bf16[4,128,128]{2,1,0:T(8,128)(2,1)S(1)}, bf16[4,128,128]{2,1,0:T(8,128)(2,1)S(1)}, u32[]{:S(2)}, u32[]{:S(2)}) collective-permute-start(bf16[4,128,128]{2,1,0:T(8,128)(2,1)S(1)} %multiply_convert_fusion.panel.refs_0_), channel_id=1, source_target_pairs={{0,1},{1,0},{2,3},{3,2},{4,5},{5,4},{6,7},{7,6},{8,9},{9,8},{10,11... | collective-permute-start | bytes 393224 | tf_op jit(solution)/shard_map/ppermute | solution.py:285
  11.1 1.4 %collective-permute-start.4 = (bf16[4,128,128]{2,1,0:T(8,128)(2,1)S(1)}, bf16[4,128,128]{2,1,0:T(8,128)(2,1)S(1)}, u32[]{:S(2)}, u32[]{:S(2)}) collective-permute-start(bf16[4,128,128]{2,1,0:T(8,128)(2,1)S(1)} %collective-permute-done.2.refs_0_.refs_1_), channel_id=1, source_target_pairs={{0,1},{1,0},{2,3},{3,2},{4,5},{5,4},{6,7},{7,6},{8,9},{9,8},{10,11... | collective-permute-start | bytes 393224 | tf_op jit(solution)/shard_map/ppermute | solution.py:285
  13.7 6.0 %collective-permute-start.6 = (bf16[4,128,128]{2,1,0:T(8,128)(2,1)S(1)}, bf16[4,128,128]{2,1,0:T(8,128)(2,1)S(1)}, u32[]{:S(2)}, u32[]{:S(2)}) collective-permute-start(bf16[4,128,128]{2,1,0:T(8,128)(2,1)S(1)} %get-tuple-element.50), channel_id=1, source_target_pairs={{0,4},{1,9},{2,6},{3,11},{4,0},{5,13},{6,2},{7,15},{8,12},{9,1},{1... | collective-permute-start | bytes 393224 | tf_op jit(solution)/shard_map/ppermute | solution.py:374
  16.4 6.7 %collective-permute-start.5 = (bf16[4,128,128]{2,1,0:T(8,128)(2,1)S(1)}, bf16[4,128,128]{2,1,0:T(8,128)(2,1)S(1)}, u32[]{:S(2)}, u32[]{:S(2)}) collective-permute-start(bf16[4,128,128]{2,1,0:T(8,128)(2,1)S(1)} %get-tuple-element.48), channel_id=1, source_target_pairs={{0,4},{1,9},{2,6},{3,11},{4,0},{5,13},{6,2},{7,15},{8,12},{9,1},{1... | collective-permute-start | bytes 393224 | tf_op jit(solution)/shard_map/ppermute | solution.py:374
  19.8 7.4 %collective-permute-start.7 = (bf16[4,128,128]{2,1,0:T(8,128)(2,1)S(1)}, bf16[4,128,128]{2,1,0:T(8,128)(2,1)S(1)}, u32[]{:S(2)}, u32[]{:S(2)}) collective-permute-start(bf16[4,128,128]{2,1,0:T(8,128)(2,1)S(1)} %add_convert_fusion), channel_id=1, source_target_pairs={{0,8},{1,5},{2,10},{3,7},{4,12},{5,1},{6,14},{7,3},{8,0},{9,13},{1... | collective-permute-start | bytes 393224 | tf_op jit(solution)/shard_map/ppermute | solution.py:374

commit v8 on v0

--- a/solution.py
+++ b/solution.py
@@ -198,7 +198,7 @@
 
 
 def far_kernel(order_ref, *refs):
-    *panels, blocks, total, far, source = refs
+    *panels, blocks, _, far, total, source = refs
     gather_panels(panels, source)
     add_products(2, order_ref, blocks, source, total)
     far[...] = total[: far.shape[0]].astype(far.dtype)
@@ -301,11 +301,15 @@
         cost_estimate=cost_of(capacity // 8, tile_rows, row_width),
     )(order, *middle, blocks, total)
     *others, total = lax.optimization_barrier((*others, total))
-    far = pl.pallas_call(
+    far, _ = pl.pallas_call(
         far_kernel,
-        out_shape=jax.ShapeDtypeStruct((far_tiles, tile_rows, row_width), jnp.bfloat16),
+        out_shape=[
+            jax.ShapeDtypeStruct((far_tiles, tile_rows, row_width), jnp.bfloat16),
+            jax.ShapeDtypeStruct(total.shape, total.dtype),
+        ],
         in_specs=[SMEM] + [VMEM] * (len(others) + 2),
-        out_specs=VMEM,
+        out_specs=[VMEM] * 2,
+        input_output_aliases={len(others) + 2: 1},
         scratch_shapes=[held(len(others) * tiles_dev, jnp.bfloat16)],
         compiler_params=LIMIT,
         cost_estimate=cost_of(capacity // 8, tile_rows, row_width),

time: 26.8 us -> 27.2 us (1.015)
  starting transfers between devices: 11 us -> 12.2 us
  Pallas kernels: 9.28 us -> 8.58 us
    ppermute x3, starting transfers between devices: 4.52 us -> 5.27 us  [turned(): return lax.ppermute(value, ('grp', 'blk'), pairs)]
    ppermute x2, starting transfers between devices: 0.58 us -> 1.04 us  [paired(): lax.ppermute(value, axis, [(at, at ^ hop) for at in range(lax.axis_size(a...]
  transfers between devices with their start and end apart: 8 -> 8, of which waited for: 5 -> 4; matrix products, arithmetic and copies ran while one was open for 1% -> 1% of each run, Pallas kernels for 28% -> 25%
where the time goes in v8:
time: 27.2 us; the launch traced here: 27.6 us
  starting transfers between devices  12.2 us (45%)
  Pallas kernels  8.58 us (32%)
  waiting for transfers between devices  6.35 us (23%)
  other arithmetic  0.28 us (1%)
    ppermute x3, starting transfers between devices, across(): return lax.ppermute(value, ('side', 'blk'), pairs)  5.92 us
    ppermute x3, waiting for transfers between devices, turned(): return lax.ppermute(value, ('grp', 'blk'), pairs)  5.91 us
    ppermute x3, starting transfers between devices, turned(): return lax.ppermute(value, ('grp', 'blk'), pairs)  5.27 us
    pallas_call x1, Pallas kernels, stage_blocks(): pl.pallas_call(functools.partial(stage_kernel, blks, groups, tiles_dev),...  2.46 us
    pallas_call x1, Pallas kernels, shards(): pl.pallas_call(rest_kernel, out_shape=[jax.ShapeDtypeStruct(part, jnp.flo...  1.42 us
    ppermute x2, starting transfers between devices, paired(): lax.ppermute(value, axis, [(at, at ^ hop) for at in range(lax.axis_size(a...  1.04 us
    pallas_call x1, Pallas kernels, scale_rows(): pl.pallas_call(scale_kernel, out_shape=[jax.ShapeDtypeStruct(codes.shape,...  1 us
    pallas_call x1, Pallas kernels, shards(): pl.pallas_call(first_kernel, out_shape=jax.ShapeDtypeStruct(part, jnp.bfl...  0.91 us
  transfers between devices with their start and end apart: 8, of which 4 were waited for; matrix products, arithmetic and copies ran while one was open for 1% of the time, Pallas kernels for 25%

profile of v8, /device:TPU:0, one launch (start us, length us, event | category | flops | bytes accessed | tf_op | source)
XLA Modules:
  0.0 27.6 jit_solution(15406372399567507160)
XLA Ops:
  0.0 3.9 %collective-permute-start = (bf16[4,128,128]{2,1,0:T(8,128)(2,1)}, bf16[4,128,128]{2,1,0:T(8,128)(2,1)S(1)}, u32[]{:S(2)}, u32[]{:S(2)}) collective-permute-start(bf16[4,128,128]{2,1,0:T(8,128)(2,1)} %bitcast.7), channel_id=1, source_target_pairs={{0,18},{1,17},{2,16},{3,19},{16,2},{17,1},{18,0},{19,3},{4,22},{5,... | collective-permute-start | bytes 393224 | tf_op jit(solution)/shard_map/ppermute | solution.py:265
  3.9 1.0 %shard_map.55 = (bf16[4,128,128]{2,1,0:T(8,128)(2,1)S(1)}, f32[4,128,128]{2,1,0:T(8,128)S(1)}, f32[4,128]{1,0:T(4,128)S(1)}) custom-call(s32[1,4]{1,0:T(1,128)} %exps_hbm.1, s32[1,512]{1,0:T(1,128)} %degrees_hbm.1, bf16[4,128,128]{2,1,0:T(8,128)(2,1)} %bitcast.8), custom_call_target="tpu_custom_call" | custom-call | flops 65536 | bytes 262144 | tf_op jit(solution)/shard_map/pallas_call | solution.py:55
  4.9 0.1 collective-permute-start.1
  5.0 2.0 %collective-permute-start.3 = (bf16[4,128,128]{2,1,0:T(8,128)(2,1)S(1)}, bf16[4,128,128]{2,1,0:T(8,128)(2,1)S(1)}, u32[]{:S(2)}, u32[]{:S(2)}) collective-permute-start(bf16[4,128,128]{2,1,0:T(8,128)(2,1)S(1)} %get-tuple-element.33), channel_id=1, source_target_pairs={{0,16},{1,19},{2,18},{3,17},{16,0},{17,3},{18,2},{19,1},{4,20},{5,... | collective-permute-start | bytes 393224 | tf_op jit(solution)/shard_map/ppermute | solution.py:265
  6.9 0.1 pad_add_fusion.place_ref
  7.0 2.5 %shard_map.56 = (s32[8,128]{1,0:T(8,128)S(1)}, bf16[96,128,128]{2,1,0:T(8,128)(2,1)S(1)}) custom-call(s32[2]{0:T(128)S(1)} %pad_add_fusion.place_ref, s32[2,96]{1,0:T(2,128)} %bitcast.9, bf16[96,128,128]{2,1,0:T(8,128)(2,1)} %bitcast.6), custom_call_target="tpu_custom_call" | custom-call | tf_op jit(solution)/shard_map/pallas_call | solution.py:154
  9.5 0.0 collective-permute-done.1
  9.5 0.0 collective-permute-done
  9.5 0.1 multiply_convert_fusion.panel.refs_0_
  9.6 0.1 collective-permute-start.2
  9.7 0.6 %shard_map.57.refs_2_ = f32[5,128,128]{2,1,0:T(8,128)S(1)} custom-call(s32[8,128]{1,0:T(8,128)S(1)} %get-tuple-element.42.order_ref, bf16[4,128,128]{2,1,0:T(8,128)(2,1)S(1)} %multiply_convert_fusion.panel.refs_0_, bf16[96,128,128]{2,1,0:T(8,128)(2,1)S(1)} %get-tuple-element.34.blocks.refs_1_.refs_2_.refs_4_), custom_call_target="tpu_custom_call" | custom-call | flops 50331648 | bytes 393216 | tf_op jit(solution)/shard_map/pallas_call | solution.py:283
  10.4 0.1 collective-permute-done.3.refs_0_.refs_1_
  10.4 1.0 %collective-permute-start.4 = (bf16[4,128,128]{2,1,0:T(8,128)(2,1)S(1)}, bf16[4,128,128]{2,1,0:T(8,128)(2,1)S(1)}, u32[]{:S(2)}, u32[]{:S(2)}) collective-permute-start(bf16[4,128,128]{2,1,0:T(8,128)(2,1)S(1)} %collective-permute-done.3.refs_0_.refs_1_), channel_id=1, source_target_pairs={{0,1},{1,0},{2,3},{3,2},{4,5},{5,4},{6,7},{7,6},{8,9},{9,8},{10,11... | collective-permute-start | bytes 393224 | tf_op jit(solution)/shard_map/ppermute | solution.py:268
  11.4 0.6 %shard_map.58.refs_3_ = f32[5,128,128]{2,1,0:T(8,128)S(1)} custom-call(s32[8,128]{1,0:T(8,128)S(1)} %get-tuple-element.42.order_ref, bf16[4,128,128]{2,1,0:T(8,128)(2,1)S(1)} %collective-permute-done.3.refs_0_.refs_1_, bf16[96,128,128]{2,1,0:T(8,128)(2,1)S(1)} %get-tuple-element.34.blocks.refs_1_.refs_2_.refs_4_, ...), custom_call_target="tpu_custom_call", output_to_operand_aliasing={{}: (3, {})} | custom-call | flops 50331648 | bytes 393216 | tf_op jit(solution)/shard_map/pallas_call | solution.py:293
  12.0 0.4 %collective-permute-done.4.refs_1_.refs_3_ = bf16[4,128,128]{2,1,0:T(8,128)(2,1)S(1)} collective-permute-done((bf16[4,128,128]{2,1,0:T(8,128)(2,1)S(1)}, bf16[4,128,128]{2,1,0:T(8,128)(2,1)S(1)}, u32[]{:S(2)}, u32[]{:S(2)}) %collective-permute-start.4) | collective-permute-done | bytes 131104 | tf_op jit(solution)/shard_map/ppermute | solution.py:268
  12.4 0.9 %shard_map.59 = (bf16[4,128,128]{2,1,0:T(8,128)(2,1)S(1)}, f32[5,128,128]{2,1,0:T(8,128)S(1)}) custom-call(s32[8,128]{1,0:T(8,128)S(1)} %get-tuple-element.42.order_ref, bf16[4,128,128]{2,1,0:T(8,128)(2,1)S(1)} %collective-permute-done.2.refs_0_.refs_2_, ...), custom_call_target="tpu_custom_call", output_to_operand_aliasing={{1}: (4, {})} | custom-call | flops 50331648 | bytes 393216 | tf_op jit(solution)/shard_map/pallas_call | solution.py:304
  13.3 1.3 %collective-permute-start.6 = (bf16[4,128,128]{2,1,0:T(8,128)(2,1)S(1)}, bf16[4,128,128]{2,1,0:T(8,128)(2,1)S(1)}, u32[]{:S(2)}, u32[]{:S(2)}) collective-permute-start(bf16[4,128,128]{2,1,0:T(8,128)(2,1)S(1)} %get-tuple-element.46), channel_id=1, source_target_pairs={{0,4},{1,9},{2,6},{3,11},{4,0},{5,13},{6,2},{7,15},{8,12},{9,1},{1... | collective-permute-start | bytes 393224 | tf_op jit(solution)/shard_map/ppermute | solution.py:355
  14.5 0.9 %shard_map.60 = bf16[4,128,128]{2,1,0:T(8,128)(2,1)S(1)} custom-call(s32[8,128]{1,0:T(8,128)S(1)} %get-tuple-element.42.order_ref, bf16[4,128,128]{2,1,0:T(8,128)(2,1)S(1)} %multiply_convert_fusion.panel.refs_0_, bf16[4,128,128]{2,1,0:T(8,128)(2,1)S(1)} %collective-permute-done.3.refs_0_.refs_1_, ...), custom_call_target="tpu_custom_call" | custom-call | flops 100663296 | bytes 786432 | tf_op jit(solution)/shard_map/pallas_call | solution.py:319
  15.5 1.1 %collective-permute-start.5 = (bf16[4,128,128]{2,1,0:T(8,128)(2,1)S(1)}, bf16[4,128,128]{2,1,0:T(8,128)(2,1)S(1)}, u32[]{:S(2)}, u32[]{:S(2)}) collective-permute-start(bf16[4,128,128]{2,1,0:T(8,128)(2,1)S(1)} %shard_map.60), channel_id=1, source_target_pairs={{0,4},{1,9},{2,6},{3,11},{4,0},{5,13},{6,2},{7,15},{8,12},{9,1},{1... | collective-permute-start | bytes 393224 | tf_op jit(solution)/shard_map/ppermute | solution.py:355
  16.6 1.4 %shard_map.61 = (f32[4,128,128]{2,1,0:T(8,128)S(1)}, f32[4,128,128]{2,1,0:T(8,128)S(1)}) custom-call(s32[8,128]{1,0:T(8,128)S(1)} %get-tuple-element.42.order_ref, bf16[4,128,128]{2,1,0:T(8,128)(2,1)S(1)} %multiply_convert_fusion.panel.refs_0_, bf16[4,128,128]{2,1,0:T(8,128)(2,1)S(1)} %collective-permute-done.3.refs_0_.refs_1_, ...), custom_call_target="tpu_custom_call" | custom-call | flops 201326592 | bytes 1572864 | tf_op jit(solution)/shard_map/pallas_call | solution.py:332
  18.0 0.8 %collective-permute-done.6 = bf16[4,128,128]{2,1,0:T(8,128)(2,1)S(1)} collective-permute-done((bf16[4,128,128]{2,1,0:T(8,128)(2,1)S(1)}, bf16[4,128,128]{2,1,0:T(8,128)(2,1)S(1)}, u32[]{:S(2)}, u32[]{:S(2)}) %collective-permute-start.6) | collective-permute-done | bytes 131104 | tf_op jit(solution)/shard_map/ppermute | solution.py:355
  18.9 2.9 %collective-permute-start.7 = (bf16[4,128,128]{2,1,0:T(8,128)(2,1)S(1)}, bf16[4,128,128]{2,1,0:T(8,128)(2,1)S(1)}, u32[]{:S(2)}, u32[]{:S(2)}) collective-permute-start(bf16[4,128,128]{2,1,0:T(8,128)(2,1)S(1)} %add_convert_fusion), channel_id=1, source_target_pairs={{0,8},{1,5},{2,10},{3,7},{4,12},{5,1},{6,14},{7,3},{8,0},{9,13},{1... | collective-permute-start | bytes 393224 | tf_op jit(solution)/shard_map/ppermute | solution.py:355
  21.8 5.1 %collective-permute-done.7.refs_0_ = bf16[4,128,128]{2,1,0:T(8,128)(2,1)S(1)} collective-permute-done((bf16[4,128,128]{2,1,0:T(8,128)(2,1)S(1)}, bf16[4,128,128]{2,1,0:T(8,128)(2,1)S(1)}, u32[]{:S(2)}, u32[]{:S(2)}) %collective-permute-start.7) | collective-permute-done | bytes 131104 | tf_op jit(solution)/shard_map/ppermute | solution.py:355
  26.9 0.7 %shard_map.62 = bf16[4,128,128]{2,1,0:T(8,128)(2,1)} custom-call(f32[4,128,128]{2,1,0:T(8,128)S(1)} %get-tuple-element.27.factors, f32[4,128,128]{2,1,0:T(8,128)S(1)} %convert_add_fusion.own, bf16[4,128,128]{2,1,0:T(8,128)(2,1)S(1)} %collective-permute-done.7.refs_0_), custom_call_target="tpu_custom_call" | custom-call | tf_op jit(solution)/shard_map/pallas_call | solution.py:375
  (4 shorter events, 0.1 us)
Async XLA Ops:
  0.0 9.5 %collective-permute-start = (bf16[4,128,128]{2,1,0:T(8,128)(2,1)}, bf16[4,128,128]{2,1,0:T(8,128)(2,1)S(1)}, u32[]{:S(2)}, u32[]{:S(2)}) collective-permute-start(bf16[4,128,128]{2,1,0:T(8,128)(2,1)} %bitcast.7), channel_id=1, source_target_pairs={{0,18},{1,17},{2,16},{3,19},{16,2},{17,1},{18,0},{19,3},{4,22},{5,... | collective-permute-start | bytes 393224 | tf_op jit(solution)/shard_map/ppermute | solution.py:265
  4.9 4.6 %collective-permute-start.1 = (f32[4,128]{1,0:T(4,128)S(1)}, f32[4,128]{1,0:T(4,128)S(1)}, u32[]{:S(2)}, u32[]{:S(2)}) collective-permute-start(f32[4,128]{1,0:T(4,128)S(1)} %get-tuple-element.28), channel_id=1, source_target_pairs={{0,18},{1,17},{2,16},{3,19},{16,2},{17,1},{18,0},{19,3},{4,22},{5,... | collective-permute-start | bytes 6152 | tf_op jit(solution)/shard_map/ppermute | solution.py:265
  5.0 5.4 %collective-permute-start.3 = (bf16[4,128,128]{2,1,0:T(8,128)(2,1)S(1)}, bf16[4,128,128]{2,1,0:T(8,128)(2,1)S(1)}, u32[]{:S(2)}, u32[]{:S(2)}) collective-permute-start(bf16[4,128,128]{2,1,0:T(8,128)(2,1)S(1)} %get-tuple-element.33), channel_id=1, source_target_pairs={{0,16},{1,19},{2,18},{3,17},{16,0},{17,3},{18,2},{19,1},{4,20},{5,... | collective-permute-start | bytes 393224 | tf_op jit(solution)/shard_map/ppermute | solution.py:265
  9.6 2.4 %collective-permute-start.2 = (bf16[4,128,128]{2,1,0:T(8,128)(2,1)S(1)}, bf16[4,128,128]{2,1,0:T(8,128)(2,1)S(1)}, u32[]{:S(2)}, u32[]{:S(2)}) collective-permute-start(bf16[4,128,128]{2,1,0:T(8,128)(2,1)S(1)} %multiply_convert_fusion.panel.refs_0_), channel_id=1, source_target_pairs={{0,1},{1,0},{2,3},{3,2},{4,5},{5,4},{6,7},{7,6},{8,9},{9,8},{10,11... | collective-permute-start | bytes 393224 | tf_op jit(solution)/shard_map/ppermute | solution.py:268
  10.4 2.0 %collective-permute-start.4 = (bf16[4,128,128]{2,1,0:T(8,128)(2,1)S(1)}, bf16[4,128,128]{2,1,0:T(8,128)(2,1)S(1)}, u32[]{:S(2)}, u32[]{:S(2)}) collective-permute-start(bf16[4,128,128]{2,1,0:T(8,128)(2,1)S(1)} %collective-permute-done.3.refs_0_.refs_1_), channel_id=1, source_target_pairs={{0,1},{1,0},{2,3},{3,2},{4,5},{5,4},{6,7},{7,6},{8,9},{9,8},{10,11... | collective-permute-start | bytes 393224 | tf_op jit(solution)/shard_map/ppermute | solution.py:268
  13.3 5.6 %collective-permute-start.6 = (bf16[4,128,128]{2,1,0:T(8,128)(2,1)S(1)}, bf16[4,128,128]{2,1,0:T(8,128)(2,1)S(1)}, u32[]{:S(2)}, u32[]{:S(2)}) collective-permute-start(bf16[4,128,128]{2,1,0:T(8,128)(2,1)S(1)} %get-tuple-element.46), channel_id=1, source_target_pairs={{0,4},{1,9},{2,6},{3,11},{4,0},{5,13},{6,2},{7,15},{8,12},{9,1},{1... | collective-permute-start | bytes 393224 | tf_op jit(solution)/shard_map/ppermute | solution.py:355
  15.5 6.3 %collective-permute-start.5 = (bf16[4,128,128]{2,1,0:T(8,128)(2,1)S(1)}, bf16[4,128,128]{2,1,0:T(8,128)(2,1)S(1)}, u32[]{:S(2)}, u32[]{:S(2)}) collective-permute-start(bf16[4,128,128]{2,1,0:T(8,128)(2,1)S(1)} %shard_map.60), channel_id=1, source_target_pairs={{0,4},{1,9},{2,6},{3,11},{4,0},{5,13},{6,2},{7,15},{8,12},{9,1},{1... | collective-permute-start | bytes 393224 | tf_op jit(solution)/shard_map/ppermute | solution.py:355
  18.9 8.0 %collective-permute-start.7 = (bf16[4,128,128]{2,1,0:T(8,128)(2,1)S(1)}, bf16[4,128,128]{2,1,0:T(8,128)(2,1)S(1)}, u32[]{:S(2)}, u32[]{:S(2)}) collective-permute-start(bf16[4,128,128]{2,1,0:T(8,128)(2,1)S(1)} %add_convert_fusion), channel_id=1, source_target_pairs={{0,8},{1,5},{2,10},{3,7},{4,12},{5,1},{6,14},{7,3},{8,0},{9,13},{1... | collective-permute-start | bytes 393224 | tf_op jit(solution)/shard_map/ppermute | solution.py:355

commit v9 on v8

--- a/solution.py
+++ b/solution.py
@@ -106,8 +106,10 @@
     kept = jnp.where(chunk == 1, 1 + role * (groups // 2 - 1), (chunk >> 1) + 1 - role)
     kept = jnp.where(chunk == 0, 0, jnp.where(far, (chunk >> 1) - 1, kept))
     stage = jnp.where(far, jnp.where(odd == 1, 2, jnp.minimum(rank, 1)), 4)
-    stage = jnp.where(far | (kept != 1), stage, 3)
-    kept = jnp.where(far, kept, jnp.where(stage == 3, 0, kept - (kept > 1).astype(jnp.int32)))
+    drawn = (kept == 0) & (role == 0)
+    stage = jnp.where(far | ((kept != 1) & ~drawn), stage, 3)
+    near = jnp.where(stage == 3, 1 - kept, kept - (kept > 1).astype(jnp.int32))
+    kept = jnp.where(far, kept, near)
     stage = jnp.where(origin < source_tiles, stage, STAGES)
     panel = jnp.where(stage == 1, rank - 1, jnp.where(stage == 2, rank, rank + odd * half))
     slot = count_up((1, capacity), 1)
@@ -123,7 +125,7 @@
         jnp.where(count_up((8, capacity), 0) == at, part, 0) for at, part in enumerate(parts)
     ).astype(jnp.bfloat16)
     far_tiles = (groups // 2 - 1) * tiles_dev
-    tops = [far_tiles] * 3 + [tiles_dev, groups // 2 * tiles_dev]
+    tops = [far_tiles] * 3 + [2 * tiles_dev, groups // 2 * tiles_dev]
     lanes = count_up((1, width), 1)
     for at, top in enumerate(tops):
         where = jnp.where(stage == at, position, -1)
@@ -205,11 +207,13 @@
 
 
 def first_kernel(order_ref, *refs):
-    *panels, blocks, first, source, total = refs
+    *panels, blocks, first, own, source, total = refs
     gather_panels(panels, source)
     total[...] = jnp.zeros_like(total)
     add_products(3, order_ref, blocks, source, total)
-    first[...] = total[: first.shape[0]].astype(first.dtype)
+    tiles_dev = first.shape[0]
+    first[...] = total[:tiles_dev].astype(first.dtype)
+    own[...] = total[tiles_dev : 2 * tiles_dev]
 
 
 def rest_kernel(order_ref, *refs):
@@ -316,14 +320,17 @@
     )(order, *others, blocks, total)
     far, order = lax.optimization_barrier((far, order))
     panels = [early] + middle + others
-    first = pl.pallas_call(
+    first, even_own = pl.pallas_call(
         first_kernel,
-        out_shape=jax.ShapeDtypeStruct(part, jnp.bfloat16),
+        out_shape=[
+            jax.ShapeDtypeStruct(part, jnp.bfloat16),
+            jax.ShapeDtypeStruct(part, jnp.float32),
+        ],
         in_specs=[SMEM] + [VMEM] * (len(panels) + 1),
-        out_specs=VMEM,
+        out_specs=[VMEM] * 2,
         scratch_shapes=[
             held(len(panels) * tiles_dev, jnp.bfloat16),
-            held(tiles_dev + 1, jnp.float32),
+            held(2 * tiles_dev + 1, jnp.float32),
         ],
         compiler_params=LIMIT,
         cost_estimate=cost_of(capacity // 4, tile_rows, row_width),
@@ -370,7 +377,7 @@
                 value = value + jnp.where(even_core, 0.0, extra)
         odd_hop = 1 if at == steps - 1 else 2 * at + 4
         arrived.append(turned(value.astype(jnp.bfloat16), 2 * at + 2, odd_hop))
-    own = own + arrived[0].astype(jnp.float32)
+    own = own + even_own + arrived[0].astype(jnp.float32)
     own, *sums = lax.optimization_barrier((own, *arrived[1:]))
     out = pl.pallas_call(
         final_kernel,

time: 27.2 us -> 27.2 us (level)
  Pallas kernels: 8.58 us -> 9.1 us
  starting transfers between devices: 12.2 us -> 11.8 us
    pallas_call x1, Pallas kernels: 0.91 us -> 1.41 us  [shards(): pl.pallas_call(first_kernel, out_shape=[jax.ShapeDtypeStruct(part, jnp.bf...]
    pallas_call x1, Pallas kernels: 0.61 us -> 1.09 us  [shards(): pl.pallas_call(middle_kernel, out_shape=jax.ShapeDtypeStruct(total.shape,...]
    ppermute x3, starting transfers between devices: 5.27 us -> 4.86 us  [turned(): return lax.ppermute(value, ('grp', 'blk'), pairs)]
    ppermute x2, waiting for transfers between devices: 0.36 us -> 0.01 us  [paired(): lax.ppermute(value, axis, [(at, at ^ hop) for at in range(lax.axis_size(a...]
  transfers between devices with their start and end apart: 8 -> 8, of which waited for: 4 -> 4; matrix products, arithmetic and copies ran while one was open for 1% -> 1% of each run, Pallas kernels for 25% -> 28%
where the time goes in v9:
time: 27.2 us; the launch traced here: 27.5 us
  starting transfers between devices  11.8 us (43%)
  Pallas kernels  9.1 us (33%)
  waiting for transfers between devices  6.14 us (23%)
  other arithmetic  0.29 us (1%)
    ppermute x3, waiting for transfers between devices, turned(): return lax.ppermute(value, ('grp', 'blk'), pairs)  6.07 us
    ppermute x3, starting transfers between devices, across(): return lax.ppermute(value, ('side', 'blk'), pairs)  5.92 us
    ppermute x3, starting transfers between devices, turned(): return lax.ppermute(value, ('grp', 'blk'), pairs)  4.86 us
    pallas_call x1, Pallas kernels, stage_blocks(): pl.pallas_call(functools.partial(stage_kernel, blks, groups, tiles_dev),...  2.46 us
    pallas_call x1, Pallas kernels, shards(): pl.pallas_call(first_kernel, out_shape=[jax.ShapeDtypeStruct(part, jnp.bf...  1.41 us
    pallas_call x1, Pallas kernels, shards(): pl.pallas_call(rest_kernel, out_shape=[jax.ShapeDtypeStruct(part, jnp.flo...  1.18 us
    pallas_call x1, Pallas kernels, shards(): pl.pallas_call(middle_kernel, out_shape=jax.ShapeDtypeStruct(total.shape,...  1.09 us
    ppermute x2, starting transfers between devices, paired(): lax.ppermute(value, axis, [(at, at ^ hop) for at in range(lax.axis_size(a...  1.04 us
  transfers between devices with their start and end apart: 8, of which 4 were waited for; matrix products, arithmetic and copies ran while one was open for 1% of the time, Pallas kernels for 28%

profile of v9, /device:TPU:0, one launch (start us, length us, event | category | flops | bytes accessed | tf_op | source)
XLA Modules:
  0.0 27.5 jit_solution(11767689982549321610)
XLA Ops:
  0.0 3.9 %collective-permute-start = (bf16[4,128,128]{2,1,0:T(8,128)(2,1)}, bf16[4,128,128]{2,1,0:T(8,128)(2,1)S(1)}, u32[]{:S(2)}, u32[]{:S(2)}) collective-permute-start(bf16[4,128,128]{2,1,0:T(8,128)(2,1)} %bitcast.7), channel_id=1, source_target_pairs={{0,18},{1,17},{2,16},{3,19},{16,2},{17,1},{18,0},{19,3},{4,22},{5,... | collective-permute-start | bytes 393224 | tf_op jit(solution)/shard_map/ppermute | solution.py:269
  3.9 1.0 %shard_map.55 = (bf16[4,128,128]{2,1,0:T(8,128)(2,1)S(1)}, f32[4,128,128]{2,1,0:T(8,128)S(1)}, f32[4,128]{1,0:T(4,128)S(1)}) custom-call(s32[1,4]{1,0:T(1,128)} %exps_hbm.1, s32[1,512]{1,0:T(1,128)} %degrees_hbm.1, bf16[4,128,128]{2,1,0:T(8,128)(2,1)} %bitcast.8), custom_call_target="tpu_custom_call" | custom-call | flops 65536 | bytes 262144 | tf_op jit(solution)/shard_map/pallas_call | solution.py:55
  4.9 0.1 collective-permute-start.1
  5.0 2.0 %collective-permute-start.3 = (bf16[4,128,128]{2,1,0:T(8,128)(2,1)S(1)}, bf16[4,128,128]{2,1,0:T(8,128)(2,1)S(1)}, u32[]{:S(2)}, u32[]{:S(2)}) collective-permute-start(bf16[4,128,128]{2,1,0:T(8,128)(2,1)S(1)} %get-tuple-element.35), channel_id=1, source_target_pairs={{0,16},{1,19},{2,18},{3,17},{16,0},{17,3},{18,2},{19,1},{4,20},{5,... | collective-permute-start | bytes 393224 | tf_op jit(solution)/shard_map/ppermute | solution.py:269
  6.9 0.1 pad_add_fusion.place_ref
  7.0 2.5 %shard_map.56 = (s32[8,128]{1,0:T(8,128)S(1)}, bf16[96,128,128]{2,1,0:T(8,128)(2,1)S(1)}) custom-call(s32[2]{0:T(128)S(1)} %pad_add_fusion.place_ref, s32[2,96]{1,0:T(2,128)} %bitcast.9, bf16[96,128,128]{2,1,0:T(8,128)(2,1)} %bitcast.6), custom_call_target="tpu_custom_call" | custom-call | tf_op jit(solution)/shard_map/pallas_call | solution.py:156
  9.5 0.0 collective-permute-done
  9.5 0.1 multiply_convert_fusion.panel.refs_0_
  9.6 0.1 collective-permute-start.2
  9.7 0.6 %shard_map.57.refs_2_ = f32[5,128,128]{2,1,0:T(8,128)S(1)} custom-call(s32[8,128]{1,0:T(8,128)S(1)} %get-tuple-element.45.order_ref, bf16[4,128,128]{2,1,0:T(8,128)(2,1)S(1)} %multiply_convert_fusion.panel.refs_0_, bf16[96,128,128]{2,1,0:T(8,128)(2,1)S(1)} %get-tuple-element.36.blocks.refs_1_.refs_2_.refs_4_), custom_call_target="tpu_custom_call" | custom-call | flops 50331648 | bytes 393216 | tf_op jit(solution)/shard_map/pallas_call | solution.py:287
  10.4 0.1 collective-permute-done.3.refs_0_.refs_1_
  10.4 1.0 %collective-permute-start.4 = (bf16[4,128,128]{2,1,0:T(8,128)(2,1)S(1)}, bf16[4,128,128]{2,1,0:T(8,128)(2,1)S(1)}, u32[]{:S(2)}, u32[]{:S(2)}) collective-permute-start(bf16[4,128,128]{2,1,0:T(8,128)(2,1)S(1)} %collective-permute-done.3.refs_0_.refs_1_), channel_id=1, source_target_pairs={{0,1},{1,0},{2,3},{3,2},{4,5},{5,4},{6,7},{7,6},{8,9},{9,8},{10,11... | collective-permute-start | bytes 393224 | tf_op jit(solution)/shard_map/ppermute | solution.py:272
  11.4 1.1 %shard_map.58.refs_3_ = f32[5,128,128]{2,1,0:T(8,128)S(1)} custom-call(s32[8,128]{1,0:T(8,128)S(1)} %get-tuple-element.45.order_ref, bf16[4,128,128]{2,1,0:T(8,128)(2,1)S(1)} %collective-permute-done.3.refs_0_.refs_1_, bf16[96,128,128]{2,1,0:T(8,128)(2,1)S(1)} %get-tuple-element.36.blocks.refs_1_.refs_2_.refs_4_, ...), custom_call_target="tpu_custom_call", output_to_operand_aliasing={{}: (3, {})} | custom-call | flops 50331648 | bytes 393216 | tf_op jit(solution)/shard_map/pallas_call | solution.py:297
  12.5 0.0 collective-permute-done.2.refs_0_.refs_2_
  12.5 0.6 %shard_map.59 = (bf16[4,128,128]{2,1,0:T(8,128)(2,1)S(1)}, f32[5,128,128]{2,1,0:T(8,128)S(1)}) custom-call(s32[8,128]{1,0:T(8,128)S(1)} %get-tuple-element.45.order_ref, bf16[4,128,128]{2,1,0:T(8,128)(2,1)S(1)} %collective-permute-done.2.refs_0_.refs_2_, ...), custom_call_target="tpu_custom_call", output_to_operand_aliasing={{1}: (4, {})} | custom-call | flops 50331648 | bytes 393216 | tf_op jit(solution)/shard_map/pallas_call | solution.py:308
  13.2 1.6 %collective-permute-start.6 = (bf16[4,128,128]{2,1,0:T(8,128)(2,1)S(1)}, bf16[4,128,128]{2,1,0:T(8,128)(2,1)S(1)}, u32[]{:S(2)}, u32[]{:S(2)}) collective-permute-start(bf16[4,128,128]{2,1,0:T(8,128)(2,1)S(1)} %get-tuple-element.50), channel_id=1, source_target_pairs={{0,4},{1,9},{2,6},{3,11},{4,0},{5,13},{6,2},{7,15},{8,12},{9,1},{1... | collective-permute-start | bytes 393224 | tf_op jit(solution)/shard_map/ppermute | solution.py:362
  14.8 1.4 %shard_map.60 = (bf16[4,128,128]{2,1,0:T(8,128)(2,1)S(1)}, f32[4,128,128]{2,1,0:T(8,128)S(1)}) custom-call(s32[8,128]{1,0:T(8,128)S(1)} %get-tuple-element.45.order_ref, bf16[4,128,128]{2,1,0:T(8,128)(2,1)S(1)} %multiply_convert_fusion.panel.refs_0_, bf16[4,128,128]{2,1,0:T(8,128)(2,1)S(1)} %collective-permute-done.3.refs_0_.refs_1_, ...), custom_call_target="tpu_custom_call" | custom-call | flops 100663296 | bytes 786432 | tf_op jit(solution)/shard_map/pallas_call | solution.py:323
  16.2 1.0 %collective-permute-start.5 = (bf16[4,128,128]{2,1,0:T(8,128)(2,1)S(1)}, bf16[4,128,128]{2,1,0:T(8,128)(2,1)S(1)}, u32[]{:S(2)}, u32[]{:S(2)}) collective-permute-start(bf16[4,128,128]{2,1,0:T(8,128)(2,1)S(1)} %get-tuple-element.48), channel_id=1, source_target_pairs={{0,4},{1,9},{2,6},{3,11},{4,0},{5,13},{6,2},{7,15},{8,12},{9,1},{1... | collective-permute-start | bytes 393224 | tf_op jit(solution)/shard_map/ppermute | solution.py:362
  17.2 1.2 %shard_map.61 = (f32[4,128,128]{2,1,0:T(8,128)S(1)}, f32[4,128,128]{2,1,0:T(8,128)S(1)}) custom-call(s32[8,128]{1,0:T(8,128)S(1)} %get-tuple-element.45.order_ref, bf16[4,128,128]{2,1,0:T(8,128)(2,1)S(1)} %multiply_convert_fusion.panel.refs_0_, bf16[4,128,128]{2,1,0:T(8,128)(2,1)S(1)} %collective-permute-done.3.refs_0_.refs_1_, ...), custom_call_target="tpu_custom_call" | custom-call | flops 201326592 | bytes 1572864 | tf_op jit(solution)/shard_map/pallas_call | solution.py:339
  18.4 1.2 %collective-permute-done.6 = bf16[4,128,128]{2,1,0:T(8,128)(2,1)S(1)} collective-permute-done((bf16[4,128,128]{2,1,0:T(8,128)(2,1)S(1)}, bf16[4,128,128]{2,1,0:T(8,128)(2,1)S(1)}, u32[]{:S(2)}, u32[]{:S(2)}) %collective-permute-start.6) | collective-permute-done | bytes 131104 | tf_op jit(solution)/shard_map/ppermute | solution.py:362
  19.6 2.2 %collective-permute-start.7 = (bf16[4,128,128]{2,1,0:T(8,128)(2,1)S(1)}, bf16[4,128,128]{2,1,0:T(8,128)(2,1)S(1)}, u32[]{:S(2)}, u32[]{:S(2)}) collective-permute-start(bf16[4,128,128]{2,1,0:T(8,128)(2,1)S(1)} %add_convert_fusion), channel_id=1, source_target_pairs={{0,8},{1,5},{2,10},{3,7},{4,12},{5,1},{6,14},{7,3},{8,0},{9,13},{1... | collective-permute-start | bytes 393224 | tf_op jit(solution)/shard_map/ppermute | solution.py:362
  21.9 0.4 %collective-permute-done.5 = bf16[4,128,128]{2,1,0:T(8,128)(2,1)S(1)} collective-permute-done((bf16[4,128,128]{2,1,0:T(8,128)(2,1)S(1)}, bf16[4,128,128]{2,1,0:T(8,128)(2,1)S(1)}, u32[]{:S(2)}, u32[]{:S(2)}) %collective-permute-start.5) | collective-permute-done | bytes 131104 | tf_op jit(solution)/shard_map/ppermute | solution.py:362
  22.4 4.4 %collective-permute-done.7.refs_0_ = bf16[4,128,128]{2,1,0:T(8,128)(2,1)S(1)} collective-permute-done((bf16[4,128,128]{2,1,0:T(8,128)(2,1)S(1)}, bf16[4,128,128]{2,1,0:T(8,128)(2,1)S(1)}, u32[]{:S(2)}, u32[]{:S(2)}) %collective-permute-start.7) | collective-permute-done | bytes 131104 | tf_op jit(solution)/shard_map/ppermute | solution.py:362
  26.8 0.7 %shard_map.62 = bf16[4,128,128]{2,1,0:T(8,128)(2,1)} custom-call(f32[4,128,128]{2,1,0:T(8,128)S(1)} %get-tuple-element.29.factors, f32[4,128,128]{2,1,0:T(8,128)S(1)} %convert_add_fusion.own, bf16[4,128,128]{2,1,0:T(8,128)(2,1)S(1)} %collective-permute-done.7.refs_0_), custom_call_target="tpu_custom_call" | custom-call | tf_op jit(solution)/shard_map/pallas_call | solution.py:382
  (4 shorter events, 0.1 us)
Async XLA Ops:
  0.0 9.5 %collective-permute-start = (bf16[4,128,128]{2,1,0:T(8,128)(2,1)}, bf16[4,128,128]{2,1,0:T(8,128)(2,1)S(1)}, u32[]{:S(2)}, u32[]{:S(2)}) collective-permute-start(bf16[4,128,128]{2,1,0:T(8,128)(2,1)} %bitcast.7), channel_id=1, source_target_pairs={{0,18},{1,17},{2,16},{3,19},{16,2},{17,1},{18,0},{19,3},{4,22},{5,... | collective-permute-start | bytes 393224 | tf_op jit(solution)/shard_map/ppermute | solution.py:269
  4.9 4.6 %collective-permute-start.1 = (f32[4,128]{1,0:T(4,128)S(1)}, f32[4,128]{1,0:T(4,128)S(1)}, u32[]{:S(2)}, u32[]{:S(2)}) collective-permute-start(f32[4,128]{1,0:T(4,128)S(1)} %get-tuple-element.30), channel_id=1, source_target_pairs={{0,18},{1,17},{2,16},{3,19},{16,2},{17,1},{18,0},{19,3},{4,22},{5,... | collective-permute-start | bytes 6152 | tf_op jit(solution)/shard_map/ppermute | solution.py:269
  5.0 5.4 %collective-permute-start.3 = (bf16[4,128,128]{2,1,0:T(8,128)(2,1)S(1)}, bf16[4,128,128]{2,1,0:T(8,128)(2,1)S(1)}, u32[]{:S(2)}, u32[]{:S(2)}) collective-permute-start(bf16[4,128,128]{2,1,0:T(8,128)(2,1)S(1)} %get-tuple-element.35), channel_id=1, source_target_pairs={{0,16},{1,19},{2,18},{3,17},{16,0},{17,3},{18,2},{19,1},{4,20},{5,... | collective-permute-start | bytes 393224 | tf_op jit(solution)/shard_map/ppermute | solution.py:269
  9.6 2.8 %collective-permute-start.2 = (bf16[4,128,128]{2,1,0:T(8,128)(2,1)S(1)}, bf16[4,128,128]{2,1,0:T(8,128)(2,1)S(1)}, u32[]{:S(2)}, u32[]{:S(2)}) collective-permute-start(bf16[4,128,128]{2,1,0:T(8,128)(2,1)S(1)} %multiply_convert_fusion.panel.refs_0_), channel_id=1, source_target_pairs={{0,1},{1,0},{2,3},{3,2},{4,5},{5,4},{6,7},{7,6},{8,9},{9,8},{10,11... | collective-permute-start | bytes 393224 | tf_op jit(solution)/shard_map/ppermute | solution.py:272
  10.4 2.1 %collective-permute-start.4 = (bf16[4,128,128]{2,1,0:T(8,128)(2,1)S(1)}, bf16[4,128,128]{2,1,0:T(8,128)(2,1)S(1)}, u32[]{:S(2)}, u32[]{:S(2)}) collective-permute-start(bf16[4,128,128]{2,1,0:T(8,128)(2,1)S(1)} %collective-permute-done.3.refs_0_.refs_1_), channel_id=1, source_target_pairs={{0,1},{1,0},{2,3},{3,2},{4,5},{5,4},{6,7},{7,6},{8,9},{9,8},{10,11... | collective-permute-start | bytes 393224 | tf_op jit(solution)/shard_map/ppermute | solution.py:272
  13.2 6.4 %collective-permute-start.6 = (bf16[4,128,128]{2,1,0:T(8,128)(2,1)S(1)}, bf16[4,128,128]{2,1,0:T(8,128)(2,1)S(1)}, u32[]{:S(2)}, u32[]{:S(2)}) collective-permute-start(bf16[4,128,128]{2,1,0:T(8,128)(2,1)S(1)} %get-tuple-element.50), channel_id=1, source_target_pairs={{0,4},{1,9},{2,6},{3,11},{4,0},{5,13},{6,2},{7,15},{8,12},{9,1},{1... | collective-permute-start | bytes 393224 | tf_op jit(solution)/shard_map/ppermute | solution.py:362
  16.2 6.1 %collective-permute-start.5 = (bf16[4,128,128]{2,1,0:T(8,128)(2,1)S(1)}, bf16[4,128,128]{2,1,0:T(8,128)(2,1)S(1)}, u32[]{:S(2)}, u32[]{:S(2)}) collective-permute-start(bf16[4,128,128]{2,1,0:T(8,128)(2,1)S(1)} %get-tuple-element.48), channel_id=1, source_target_pairs={{0,4},{1,9},{2,6},{3,11},{4,0},{5,13},{6,2},{7,15},{8,12},{9,1},{1... | collective-permute-start | bytes 393224 | tf_op jit(solution)/shard_map/ppermute | solution.py:362
  19.6 7.1 %collective-permute-start.7 = (bf16[4,128,128]{2,1,0:T(8,128)(2,1)S(1)}, bf16[4,128,128]{2,1,0:T(8,128)(2,1)S(1)}, u32[]{:S(2)}, u32[]{:S(2)}) collective-permute-start(bf16[4,128,128]{2,1,0:T(8,128)(2,1)S(1)} %add_convert_fusion), channel_id=1, source_target_pairs={{0,8},{1,5},{2,10},{3,7},{4,12},{5,1},{6,14},{7,3},{8,0},{9,13},{1... | collective-permute-start | bytes 393224 | tf_op jit(solution)/shard_map/ppermute | solution.py:362

commit v10 on v9

--- a/solution.py
+++ b/solution.py
@@ -8,7 +8,8 @@
 from jax.sharding import PartitionSpec as P
 
 UNROLL = 8
-STAGES = 5
+BATCHES = (8, 8, 4, 8, 8)
+STAGES = len(BATCHES)
 VMEM = pl.BlockSpec(memory_space=pltpu.VMEM)
 SMEM = pl.BlockSpec(memory_space=pltpu.SMEM)
 HBM = pl.BlockSpec(memory_space=pltpu.HBM)
@@ -136,7 +137,7 @@
         word = pack(listed[0:1] + (listed[1:2] << 7), listed[2:3], listed[3:4])
         count = jnp.sum((stage == at).astype(jnp.int32), axis=1, keepdims=True)
         word = jnp.where(lanes < count, word, pack(0, 0, top))
-        batches = split(count + (UNROLL - 1), UNROLL)[0]
+        batches = split(count + (BATCHES[at] - 1), BATCHES[at])[0]
         order_ref[at : at + 1, :] = jnp.where(lanes == width - UNROLL, batches, word)
     copy.wait()
 
@@ -174,8 +175,8 @@
     @pl.loop(0, order_ref[stage, order_ref.shape[1] - UNROLL])
     def _(batch):
         made = []
-        for part in range(UNROLL):
-            slot, row, target = unpack(order_ref[stage, batch * UNROLL + part])
+        for part in range(BATCHES[stage]):
+            slot, row, target = unpack(order_ref[stage, batch * BATCHES[stage] + part])
             product = jnp.dot(blocks[slot], source[row], preferred_element_type=jnp.float32)
             made.append((target, product))
         for target, product in made:

time: 27.2 us -> 26.5 us (0.974); the launches traced: 27.5 us -> 26.3 us
  waiting for transfers between devices: 6.14 us -> 4.76 us
  Pallas kernels: 9.1 us -> 10 us
  starting transfers between devices: 11.8 us -> 11.1 us
    ppermute x3, waiting for transfers between devices: 6.07 us -> 4.54 us  [turned(): return lax.ppermute(value, ('grp', 'blk'), pairs)]
    ppermute x2, starting transfers between devices: 1.04 us -> 0.41 us  [paired(): lax.ppermute(value, axis, [(at, at ^ hop) for at in range(lax.axis_size(a...]
    pallas_call x1, Pallas kernels: 1.41 us -> 1.88 us  [shards(): pl.pallas_call(first_kernel, out_shape=[jax.ShapeDtypeStruct(part, jnp.bf...]
    pallas_call x1, Pallas kernels: 0.62 us -> 1.08 us  [shards(): pl.pallas_call(early_kernel, out_shape=jax.ShapeDtypeStruct((far_tiles +...]
  transfers between devices with their start and end apart: 8 -> 8, of which waited for: 4 -> 4; matrix products, arithmetic and copies ran while one was open for 1% -> 1% of each run, Pallas kernels for 28% -> 33%
where the time goes in v10:
time: 26.5 us; the launch traced here: 26.3 us
  starting transfers between devices  11.1 us (42%)
  Pallas kernels  10 us (38%)
  waiting for transfers between devices  4.76 us (18%)
  other arithmetic  0.29 us (1%)
    ppermute x3, starting transfers between devices, across(): return lax.ppermute(value, ('side', 'blk'), pairs)  5.92 us
    ppermute x3, starting transfers between devices, turned(): return lax.ppermute(value, ('grp', 'blk'), pairs)  4.76 us
    ppermute x3, waiting for transfers between devices, turned(): return lax.ppermute(value, ('grp', 'blk'), pairs)  4.54 us
    pallas_call x1, Pallas kernels, stage_blocks(): pl.pallas_call(functools.partial(stage_kernel, blks, groups, tiles_dev),...  2.46 us
    pallas_call x1, Pallas kernels, shards(): pl.pallas_call(first_kernel, out_shape=[jax.ShapeDtypeStruct(part, jnp.bf...  1.88 us
    pallas_call x1, Pallas kernels, shards(): pl.pallas_call(rest_kernel, out_shape=[jax.ShapeDtypeStruct(part, jnp.flo...  1.42 us
    pallas_call x1, Pallas kernels, shards(): pl.pallas_call(early_kernel, out_shape=jax.ShapeDtypeStruct((far_tiles +...  1.08 us
    pallas_call x1, Pallas kernels, scale_rows(): pl.pallas_call(scale_kernel, out_shape=[jax.ShapeDtypeStruct(codes.shape,...  1 us
  transfers between devices with their start and end apart: 8, of which 4 were waited for; matrix products, arithmetic and copies ran while one was open for 1% of the time, Pallas kernels for 33%

profile of v10, /device:TPU:0, one launch (start us, length us, event | category | flops | bytes accessed | tf_op | source)
XLA Modules:
  0.0 26.3 jit_solution(15926587432009704004)
XLA Ops:
  0.0 3.9 %collective-permute-start = (bf16[4,128,128]{2,1,0:T(8,128)(2,1)}, bf16[4,128,128]{2,1,0:T(8,128)(2,1)S(1)}, u32[]{:S(2)}, u32[]{:S(2)}) collective-permute-start(bf16[4,128,128]{2,1,0:T(8,128)(2,1)} %bitcast.7), channel_id=1, source_target_pairs={{0,18},{1,17},{2,16},{3,19},{16,2},{17,1},{18,0},{19,3},{4,22},{5,... | collective-permute-start | bytes 393224 | tf_op jit(solution)/shard_map/ppermute | solution.py:270
  3.9 1.0 %shard_map.55 = (bf16[4,128,128]{2,1,0:T(8,128)(2,1)S(1)}, f32[4,128,128]{2,1,0:T(8,128)S(1)}, f32[4,128]{1,0:T(4,128)S(1)}) custom-call(s32[1,4]{1,0:T(1,128)} %exps_hbm.1, s32[1,512]{1,0:T(1,128)} %degrees_hbm.1, bf16[4,128,128]{2,1,0:T(8,128)(2,1)} %bitcast.8), custom_call_target="tpu_custom_call" | custom-call | flops 65536 | bytes 262144 | tf_op jit(solution)/shard_map/pallas_call | solution.py:56
  4.9 0.1 collective-permute-start.1
  5.0 2.0 %collective-permute-start.3 = (bf16[4,128,128]{2,1,0:T(8,128)(2,1)S(1)}, bf16[4,128,128]{2,1,0:T(8,128)(2,1)S(1)}, u32[]{:S(2)}, u32[]{:S(2)}) collective-permute-start(bf16[4,128,128]{2,1,0:T(8,128)(2,1)S(1)} %get-tuple-element.35), channel_id=1, source_target_pairs={{0,16},{1,19},{2,18},{3,17},{16,0},{17,3},{18,2},{19,1},{4,20},{5,... | collective-permute-start | bytes 393224 | tf_op jit(solution)/shard_map/ppermute | solution.py:270
  6.9 0.1 pad_add_fusion.place_ref
  7.0 2.5 %shard_map.56 = (s32[8,128]{1,0:T(8,128)S(1)}, bf16[96,128,128]{2,1,0:T(8,128)(2,1)S(1)}) custom-call(s32[2]{0:T(128)S(1)} %pad_add_fusion.place_ref, s32[2,96]{1,0:T(2,128)} %bitcast.9, bf16[96,128,128]{2,1,0:T(8,128)(2,1)} %bitcast.6), custom_call_target="tpu_custom_call" | custom-call | tf_op jit(solution)/shard_map/pallas_call | solution.py:157
  9.5 0.0 collective-permute-done.1
  9.5 0.0 collective-permute-done
  9.5 0.1 multiply_convert_fusion.panel.refs_0_
  9.6 0.1 collective-permute-start.2
  9.7 1.1 %shard_map.57.refs_2_ = f32[5,128,128]{2,1,0:T(8,128)S(1)} custom-call(s32[8,128]{1,0:T(8,128)S(1)} %get-tuple-element.45.order_ref, bf16[4,128,128]{2,1,0:T(8,128)(2,1)S(1)} %multiply_convert_fusion.panel.refs_0_, bf16[96,128,128]{2,1,0:T(8,128)(2,1)S(1)} %get-tuple-element.36.blocks.refs_1_.refs_2_.refs_4_), custom_call_target="tpu_custom_call" | custom-call | flops 50331648 | bytes 393216 | tf_op jit(solution)/shard_map/pallas_call | solution.py:288
  10.8 0.3 %collective-permute-start.4 = (bf16[4,128,128]{2,1,0:T(8,128)(2,1)S(1)}, bf16[4,128,128]{2,1,0:T(8,128)(2,1)S(1)}, u32[]{:S(2)}, u32[]{:S(2)}) collective-permute-start(bf16[4,128,128]{2,1,0:T(8,128)(2,1)S(1)} %collective-permute-done.3.refs_0_.refs_1_), channel_id=1, source_target_pairs={{0,1},{1,0},{2,3},{3,2},{4,5},{5,4},{6,7},{7,6},{8,9},{9,8},{10,11... | collective-permute-start | bytes 393224 | tf_op jit(solution)/shard_map/ppermute | solution.py:273
  11.2 0.8 %shard_map.58.refs_3_ = f32[5,128,128]{2,1,0:T(8,128)S(1)} custom-call(s32[8,128]{1,0:T(8,128)S(1)} %get-tuple-element.45.order_ref, bf16[4,128,128]{2,1,0:T(8,128)(2,1)S(1)} %collective-permute-done.3.refs_0_.refs_1_, bf16[96,128,128]{2,1,0:T(8,128)(2,1)S(1)} %get-tuple-element.36.blocks.refs_1_.refs_2_.refs_4_, ...), custom_call_target="tpu_custom_call", output_to_operand_aliasing={{}: (3, {})} | custom-call | flops 50331648 | bytes 393216 | tf_op jit(solution)/shard_map/pallas_call | solution.py:298
  12.0 0.2 collective-permute-done.4.refs_1_.refs_3_
  12.2 0.6 %shard_map.59 = (bf16[4,128,128]{2,1,0:T(8,128)(2,1)S(1)}, f32[5,128,128]{2,1,0:T(8,128)S(1)}) custom-call(s32[8,128]{1,0:T(8,128)S(1)} %get-tuple-element.45.order_ref, bf16[4,128,128]{2,1,0:T(8,128)(2,1)S(1)} %collective-permute-done.2.refs_0_.refs_2_, ...), custom_call_target="tpu_custom_call", output_to_operand_aliasing={{1}: (4, {})} | custom-call | flops 50331648 | bytes 393216 | tf_op jit(solution)/shard_map/pallas_call | solution.py:309
  12.9 2.1 %collective-permute-start.6 = (bf16[4,128,128]{2,1,0:T(8,128)(2,1)S(1)}, bf16[4,128,128]{2,1,0:T(8,128)(2,1)S(1)}, u32[]{:S(2)}, u32[]{:S(2)}) collective-permute-start(bf16[4,128,128]{2,1,0:T(8,128)(2,1)S(1)} %get-tuple-element.50), channel_id=1, source_target_pairs={{0,4},{1,9},{2,6},{3,11},{4,0},{5,13},{6,2},{7,15},{8,12},{9,1},{1... | collective-permute-start | bytes 393224 | tf_op jit(solution)/shard_map/ppermute | solution.py:363
  15.0 1.9 %shard_map.60 = (bf16[4,128,128]{2,1,0:T(8,128)(2,1)S(1)}, f32[4,128,128]{2,1,0:T(8,128)S(1)}) custom-call(s32[8,128]{1,0:T(8,128)S(1)} %get-tuple-element.45.order_ref, bf16[4,128,128]{2,1,0:T(8,128)(2,1)S(1)} %multiply_convert_fusion.panel.refs_0_, bf16[4,128,128]{2,1,0:T(8,128)(2,1)S(1)} %collective-permute-done.3.refs_0_.refs_1_, ...), custom_call_target="tpu_custom_call" | custom-call | flops 100663296 | bytes 786432 | tf_op jit(solution)/shard_map/pallas_call | solution.py:324
  16.9 0.1 collective-permute-start.5
  17.0 1.4 %shard_map.61 = (f32[4,128,128]{2,1,0:T(8,128)S(1)}, f32[4,128,128]{2,1,0:T(8,128)S(1)}) custom-call(s32[8,128]{1,0:T(8,128)S(1)} %get-tuple-element.45.order_ref, bf16[4,128,128]{2,1,0:T(8,128)(2,1)S(1)} %multiply_convert_fusion.panel.refs_0_, bf16[4,128,128]{2,1,0:T(8,128)(2,1)S(1)} %collective-permute-done.3.refs_0_.refs_1_, ...), custom_call_target="tpu_custom_call" | custom-call | flops 201326592 | bytes 1572864 | tf_op jit(solution)/shard_map/pallas_call | solution.py:340
  18.4 1.0 %collective-permute-done.6 = bf16[4,128,128]{2,1,0:T(8,128)(2,1)S(1)} collective-permute-done((bf16[4,128,128]{2,1,0:T(8,128)(2,1)S(1)}, bf16[4,128,128]{2,1,0:T(8,128)(2,1)S(1)}, u32[]{:S(2)}, u32[]{:S(2)}) %collective-permute-start.6) | collective-permute-done | bytes 131104 | tf_op jit(solution)/shard_map/ppermute | solution.py:363
  19.4 2.6 %collective-permute-start.7 = (bf16[4,128,128]{2,1,0:T(8,128)(2,1)S(1)}, bf16[4,128,128]{2,1,0:T(8,128)(2,1)S(1)}, u32[]{:S(2)}, u32[]{:S(2)}) collective-permute-start(bf16[4,128,128]{2,1,0:T(8,128)(2,1)S(1)} %add_convert_fusion), channel_id=1, source_target_pairs={{0,8},{1,5},{2,10},{3,7},{4,12},{5,1},{6,14},{7,3},{8,0},{9,13},{1... | collective-permute-start | bytes 393224 | tf_op jit(solution)/shard_map/ppermute | solution.py:363
  22.0 1.9 %collective-permute-done.5 = bf16[4,128,128]{2,1,0:T(8,128)(2,1)S(1)} collective-permute-done((bf16[4,128,128]{2,1,0:T(8,128)(2,1)S(1)}, bf16[4,128,128]{2,1,0:T(8,128)(2,1)S(1)}, u32[]{:S(2)}, u32[]{:S(2)}) %collective-permute-start.5) | collective-permute-done | bytes 131104 | tf_op jit(solution)/shard_map/ppermute | solution.py:363
  23.9 1.7 %collective-permute-done.7.refs_0_ = bf16[4,128,128]{2,1,0:T(8,128)(2,1)S(1)} collective-permute-done((bf16[4,128,128]{2,1,0:T(8,128)(2,1)S(1)}, bf16[4,128,128]{2,1,0:T(8,128)(2,1)S(1)}, u32[]{:S(2)}, u32[]{:S(2)}) %collective-permute-start.7) | collective-permute-done | bytes 131104 | tf_op jit(solution)/shard_map/ppermute | solution.py:363
  25.6 0.7 %shard_map.62 = bf16[4,128,128]{2,1,0:T(8,128)(2,1)} custom-call(f32[4,128,128]{2,1,0:T(8,128)S(1)} %get-tuple-element.29.factors, f32[4,128,128]{2,1,0:T(8,128)S(1)} %convert_add_fusion.own, bf16[4,128,128]{2,1,0:T(8,128)(2,1)S(1)} %collective-permute-done.7.refs_0_), custom_call_target="tpu_custom_call" | custom-call | tf_op jit(solution)/shard_map/pallas_call | solution.py:383
  (4 shorter events, 0.1 us)
Async XLA Ops:
  0.0 9.5 %collective-permute-start = (bf16[4,128,128]{2,1,0:T(8,128)(2,1)}, bf16[4,128,128]{2,1,0:T(8,128)(2,1)S(1)}, u32[]{:S(2)}, u32[]{:S(2)}) collective-permute-start(bf16[4,128,128]{2,1,0:T(8,128)(2,1)} %bitcast.7), channel_id=1, source_target_pairs={{0,18},{1,17},{2,16},{3,19},{16,2},{17,1},{18,0},{19,3},{4,22},{5,... | collective-permute-start | bytes 393224 | tf_op jit(solution)/shard_map/ppermute | solution.py:270
  4.9 4.6 %collective-permute-start.1 = (f32[4,128]{1,0:T(4,128)S(1)}, f32[4,128]{1,0:T(4,128)S(1)}, u32[]{:S(2)}, u32[]{:S(2)}) collective-permute-start(f32[4,128]{1,0:T(4,128)S(1)} %get-tuple-element.30), channel_id=1, source_target_pairs={{0,18},{1,17},{2,16},{3,19},{16,2},{17,1},{18,0},{19,3},{4,22},{5,... | collective-permute-start | bytes 6152 | tf_op jit(solution)/shard_map/ppermute | solution.py:270
  5.0 5.8 %collective-permute-start.3 = (bf16[4,128,128]{2,1,0:T(8,128)(2,1)S(1)}, bf16[4,128,128]{2,1,0:T(8,128)(2,1)S(1)}, u32[]{:S(2)}, u32[]{:S(2)}) collective-permute-start(bf16[4,128,128]{2,1,0:T(8,128)(2,1)S(1)} %get-tuple-element.35), channel_id=1, source_target_pairs={{0,16},{1,19},{2,18},{3,17},{16,0},{17,3},{18,2},{19,1},{4,20},{5,... | collective-permute-start | bytes 393224 | tf_op jit(solution)/shard_map/ppermute | solution.py:270
  9.6 2.4 %collective-permute-start.2 = (bf16[4,128,128]{2,1,0:T(8,128)(2,1)S(1)}, bf16[4,128,128]{2,1,0:T(8,128)(2,1)S(1)}, u32[]{:S(2)}, u32[]{:S(2)}) collective-permute-start(bf16[4,128,128]{2,1,0:T(8,128)(2,1)S(1)} %multiply_convert_fusion.panel.refs_0_), channel_id=1, source_target_pairs={{0,1},{1,0},{2,3},{3,2},{4,5},{5,4},{6,7},{7,6},{8,9},{9,8},{10,11... | collective-permute-start | bytes 393224 | tf_op jit(solution)/shard_map/ppermute | solution.py:273
  10.8 1.4 %collective-permute-start.4 = (bf16[4,128,128]{2,1,0:T(8,128)(2,1)S(1)}, bf16[4,128,128]{2,1,0:T(8,128)(2,1)S(1)}, u32[]{:S(2)}, u32[]{:S(2)}) collective-permute-start(bf16[4,128,128]{2,1,0:T(8,128)(2,1)S(1)} %collective-permute-done.3.refs_0_.refs_1_), channel_id=1, source_target_pairs={{0,1},{1,0},{2,3},{3,2},{4,5},{5,4},{6,7},{7,6},{8,9},{9,8},{10,11... | collective-permute-start | bytes 393224 | tf_op jit(solution)/shard_map/ppermute | solution.py:273
  12.9 6.5 %collective-permute-start.6 = (bf16[4,128,128]{2,1,0:T(8,128)(2,1)S(1)}, bf16[4,128,128]{2,1,0:T(8,128)(2,1)S(1)}, u32[]{:S(2)}, u32[]{:S(2)}) collective-permute-start(bf16[4,128,128]{2,1,0:T(8,128)(2,1)S(1)} %get-tuple-element.50), channel_id=1, source_target_pairs={{0,4},{1,9},{2,6},{3,11},{4,0},{5,13},{6,2},{7,15},{8,12},{9,1},{1... | collective-permute-start | bytes 393224 | tf_op jit(solution)/shard_map/ppermute | solution.py:363
  16.9 7.0 %collective-permute-start.5 = (bf16[4,128,128]{2,1,0:T(8,128)(2,1)S(1)}, bf16[4,128,128]{2,1,0:T(8,128)(2,1)S(1)}, u32[]{:S(2)}, u32[]{:S(2)}) collective-permute-start(bf16[4,128,128]{2,1,0:T(8,128)(2,1)S(1)} %get-tuple-element.48), channel_id=1, source_target_pairs={{0,4},{1,9},{2,6},{3,11},{4,0},{5,13},{6,2},{7,15},{8,12},{9,1},{1... | collective-permute-start | bytes 393224 | tf_op jit(solution)/shard_map/ppermute | solution.py:363
  19.4 6.2 %collective-permute-start.7 = (bf16[4,128,128]{2,1,0:T(8,128)(2,1)S(1)}, bf16[4,128,128]{2,1,0:T(8,128)(2,1)S(1)}, u32[]{:S(2)}, u32[]{:S(2)}) collective-permute-start(bf16[4,128,128]{2,1,0:T(8,128)(2,1)S(1)} %add_convert_fusion), channel_id=1, source_target_pairs={{0,8},{1,5},{2,10},{3,7},{4,12},{5,1},{6,14},{7,3},{8,0},{9,13},{1... | collective-permute-start | bytes 393224 | tf_op jit(solution)/shard_map/ppermute | solution.py:363

commit v11 on v9

--- a/solution.py
+++ b/solution.py
@@ -79,15 +79,15 @@
 
 
 def stage_kernel(
-    blks, groups, tiles_dev, place_ref, index_hbm, blocks_hbm, order_ref, blocks, index_ref, sems
+    blks, groups, tiles_dev, index_hbm, blocks_hbm, order_ref, blocks, index_ref, sems
 ):
     fetch = pltpu.make_async_copy(index_hbm, index_ref, sems.at[0])
     fetch.start()
     copy = pltpu.make_async_copy(blocks_hbm, blocks, sems.at[1])
     copy.start()
     fetch.wait()
-    my_blk = place_ref[0]
-    my_grp = place_ref[1]
+    my_blk = lax.axis_index("blk")
+    my_grp = lax.axis_index("grp")
     capacity = index_ref.shape[1]
     width = order_ref.shape[1]
     source_tiles = blks * tiles_dev
@@ -149,7 +149,7 @@
     return word >> 16, (word >> 8) & 255, word & 255
 
 
-def stage_blocks(index, place, blocks, blks, groups, tiles_dev):
+def stage_blocks(index, blocks, blks, groups, tiles_dev):
     capacity = blocks.shape[0]
     assert blks * tiles_dev < 256 and groups * tiles_dev < 256 and capacity < 2**15
     width = -(-(capacity + 2 * UNROLL) // 128) * 128
@@ -159,7 +159,7 @@
             jax.ShapeDtypeStruct((8, width), jnp.int32),
             jax.ShapeDtypeStruct(blocks.shape, blocks.dtype),
         ],
-        in_specs=[SMEM, HBM, HBM],
+        in_specs=[HBM, HBM],
         out_specs=[VMEM, VMEM],
         scratch_shapes=[
             pltpu.VMEM(index.shape, index.dtype),
@@ -167,7 +167,7 @@
         ],
         compiler_params=LIMIT,
         cost_estimate=pl.CostEstimate(flops=0, bytes_accessed=0, transcendentals=0),
-    )(place, *in_hbm(index, blocks))
+    )(*in_hbm(index, blocks))
 
 
 def add_products(stage, order_ref, blocks, source, total):
@@ -271,11 +271,10 @@
     def paired(value, axis, hop):
         return lax.ppermute(value, axis, [(at, at ^ hop) for at in range(lax.axis_size(axis))])
 
-    place = jnp.stack([lax.axis_index("blk"), lax.axis_index("grp")]).astype(jnp.int32)
     early = across(codes, 0)
     middle = [across(source, step) for step in range(1, blks // 2)]
     early_scales = across(scales, 0)
-    order, blocks = stage_blocks(block_index[0], place, adjacency[0], blks, groups, tiles_dev)
+    order, blocks = stage_blocks(block_index[0], adjacency[0], blks, groups, tiles_dev)
     early, early_scales, order = lax.optimization_barrier((early, early_scales, order))
     early = (early.astype(jnp.float32) * early_scales[:, :, None]).astype(jnp.bfloat16)
     other = paired(early, "blk", 1)

time: 27.2 us -> 27.3 us (level); the launches traced: 27.5 us -> 26.9 us
  starting transfers between devices: 11.8 us -> 10.2 us
  waiting for transfers between devices: 6.14 us -> 6.91 us
  Pallas kernels: 9.1 us -> 9.49 us
    ppermute x3, starting transfers between devices: 4.86 us -> 3.55 us  [turned(): return lax.ppermute(value, ('grp', 'blk'), pairs)]
    pallas_call x1, Pallas kernels: 0.63 us -> 1.35 us  [shards(): pl.pallas_call(far_kernel, out_shape=[jax.ShapeDtypeStruct((far_tiles, ti...]
    ppermute x3, waiting for transfers between devices: 0.07 us -> 0.7 us  [across(): return lax.ppermute(value, ('side', 'blk'), pairs)]
    pallas_call x1, Pallas kernels: 2.46 us -> 1.92 us  [stage_blocks(): pl.pallas_call(functools.partial(stage_kernel, blks, groups, tiles_dev),...]
    pallas_call x1, Pallas kernels: 1.09 us -> 0.61 us  [shards(): pl.pallas_call(middle_kernel, out_shape=jax.ShapeDtypeStruct(total.shape,...]
    pallas_call x1, Pallas kernels: 1.41 us -> 1.88 us  [shards(): pl.pallas_call(first_kernel, out_shape=[jax.ShapeDtypeStruct(part, jnp.bf...]
    ppermute x2, waiting for transfers between devices: 0.01 us -> 0.36 us  [paired(): lax.ppermute(value, axis, [(at, at ^ hop) for at in range(lax.axis_size(a...]
    ppermute x2, starting transfers between devices: 1.04 us -> 0.75 us  [paired(): lax.ppermute(value, axis, [(at, at ^ hop) for at in range(lax.axis_size(a...]
  transfers between devices with their start and end apart: 8 -> 8, of which waited for: 4 -> 6; matrix products, arithmetic and copies ran while one was open for 1% -> 1% of each run, Pallas kernels for 28% -> 28%
where the time goes in v11:
time: 27.3 us; the launch traced here: 26.9 us
  starting transfers between devices  10.2 us (37%)
  Pallas kernels  9.49 us (35%)
  waiting for transfers between devices  6.91 us (25%)
    ppermute x3, starting transfers between devices, across(): return lax.ppermute(value, ('side', 'blk'), pairs)  5.92 us
    ppermute x3, waiting for transfers between devices, turned(): return lax.ppermute(value, ('grp', 'blk'), pairs)  5.85 us
    ppermute x3, starting transfers between devices, turned(): return lax.ppermute(value, ('grp', 'blk'), pairs)  3.55 us
    pallas_call x1, Pallas kernels, stage_blocks(): pl.pallas_call(functools.partial(stage_kernel, blks, groups, tiles_dev),...  1.92 us
    pallas_call x1, Pallas kernels, shards(): pl.pallas_call(first_kernel, out_shape=[jax.ShapeDtypeStruct(part, jnp.bf...  1.88 us
    pallas_call x1, Pallas kernels, shards(): pl.pallas_call(rest_kernel, out_shape=[jax.ShapeDtypeStruct(part, jnp.flo...  1.41 us
    pallas_call x1, Pallas kernels, shards(): pl.pallas_call(far_kernel, out_shape=[jax.ShapeDtypeStruct((far_tiles, ti...  1.35 us
    pallas_call x1, Pallas kernels, scale_rows(): pl.pallas_call(scale_kernel, out_shape=[jax.ShapeDtypeStruct(codes.shape,...  1 us
  transfers between devices with their start and end apart: 8, of which 6 were waited for; matrix products, arithmetic and copies ran while one was open for 1% of the time, Pallas kernels for 28%

profile of v11, /device:TPU:0, one launch (start us, length us, event | category | flops | bytes accessed | tf_op | source)
XLA Modules:
  0.0 26.9 jit_solution(346541839558471919)
XLA Ops:
  0.0 3.9 %collective-permute-start = (bf16[4,128,128]{2,1,0:T(8,128)(2,1)}, bf16[4,128,128]{2,1,0:T(8,128)(2,1)S(1)}, u32[]{:S(2)}, u32[]{:S(2)}) collective-permute-start(bf16[4,128,128]{2,1,0:T(8,128)(2,1)} %bitcast.5), channel_id=1, source_target_pairs={{0,18},{1,17},{2,16},{3,19},{16,2},{17,1},{18,0},{19,3},{4,22},{5,... | collective-permute-start | bytes 393224 | tf_op jit(solution)/shard_map/ppermute | solution.py:269
  3.9 1.0 %shard_map.55 = (bf16[4,128,128]{2,1,0:T(8,128)(2,1)S(1)}, f32[4,128,128]{2,1,0:T(8,128)S(1)}, f32[4,128]{1,0:T(4,128)S(1)}) custom-call(s32[1,4]{1,0:T(1,128)} %exps_hbm.1, s32[1,512]{1,0:T(1,128)} %degrees_hbm.1, bf16[4,128,128]{2,1,0:T(8,128)(2,1)} %bitcast.6), custom_call_target="tpu_custom_call" | custom-call | flops 65536 | bytes 262144 | tf_op jit(solution)/shard_map/pallas_call | solution.py:55
  4.9 0.1 collective-permute-start.1
  5.0 2.0 %collective-permute-start.3 = (bf16[4,128,128]{2,1,0:T(8,128)(2,1)S(1)}, bf16[4,128,128]{2,1,0:T(8,128)(2,1)S(1)}, u32[]{:S(2)}, u32[]{:S(2)}) collective-permute-start(bf16[4,128,128]{2,1,0:T(8,128)(2,1)S(1)} %get-tuple-element.35), channel_id=1, source_target_pairs={{0,16},{1,19},{2,18},{3,17},{16,0},{17,3},{18,2},{19,1},{4,20},{5,... | collective-permute-start | bytes 393224 | tf_op jit(solution)/shard_map/ppermute | solution.py:269
  6.9 1.9 %shard_map.56 = (s32[8,128]{1,0:T(8,128)S(1)}, bf16[96,128,128]{2,1,0:T(8,128)(2,1)S(1)}) custom-call(s32[2,96]{1,0:T(2,128)} %bitcast.7, bf16[96,128,128]{2,1,0:T(8,128)(2,1)} %bitcast.4), custom_call_target="tpu_custom_call" | custom-call | tf_op jit(solution)/shard_map/pallas_call | solution.py:156
  8.9 0.6 %collective-permute-done.1 = f32[4,128]{1,0:T(4,128)S(1)} collective-permute-done((f32[4,128]{1,0:T(4,128)S(1)}, f32[4,128]{1,0:T(4,128)S(1)}, u32[]{:S(2)}, u32[]{:S(2)}) %collective-permute-start.1) | collective-permute-done | bytes 2080 | tf_op jit(solution)/shard_map/ppermute | solution.py:269
  9.5 0.0 collective-permute-done
  9.5 0.1 multiply_convert_fusion.panel.refs_0_
  9.6 0.1 collective-permute-start.2
  9.7 0.6 %shard_map.57.refs_2_ = f32[5,128,128]{2,1,0:T(8,128)S(1)} custom-call(s32[8,128]{1,0:T(8,128)S(1)} %get-tuple-element.45.order_ref, bf16[4,128,128]{2,1,0:T(8,128)(2,1)S(1)} %multiply_convert_fusion.panel.refs_0_, bf16[96,128,128]{2,1,0:T(8,128)(2,1)S(1)} %get-tuple-element.36.blocks.refs_1_.refs_2_.refs_4_), custom_call_target="tpu_custom_call" | custom-call | flops 50331648 | bytes 393216 | tf_op jit(solution)/shard_map/pallas_call | solution.py:286
  10.3 0.1 collective-permute-done.3.refs_0_.refs_1_
  10.4 0.7 %collective-permute-start.4 = (bf16[4,128,128]{2,1,0:T(8,128)(2,1)S(1)}, bf16[4,128,128]{2,1,0:T(8,128)(2,1)S(1)}, u32[]{:S(2)}, u32[]{:S(2)}) collective-permute-start(bf16[4,128,128]{2,1,0:T(8,128)(2,1)S(1)} %collective-permute-done.3.refs_0_.refs_1_), channel_id=1, source_target_pairs={{0,1},{1,0},{2,3},{3,2},{4,5},{5,4},{6,7},{7,6},{8,9},{9,8},{10,11... | collective-permute-start | bytes 393224 | tf_op jit(solution)/shard_map/ppermute | solution.py:272
  11.1 0.6 %shard_map.58.refs_3_ = f32[5,128,128]{2,1,0:T(8,128)S(1)} custom-call(s32[8,128]{1,0:T(8,128)S(1)} %get-tuple-element.45.order_ref, bf16[4,128,128]{2,1,0:T(8,128)(2,1)S(1)} %collective-permute-done.3.refs_0_.refs_1_, bf16[96,128,128]{2,1,0:T(8,128)(2,1)S(1)} %get-tuple-element.36.blocks.refs_1_.refs_2_.refs_4_, ...), custom_call_target="tpu_custom_call", output_to_operand_aliasing={{}: (3, {})} | custom-call | flops 50331648 | bytes 393216 | tf_op jit(solution)/shard_map/pallas_call | solution.py:296
  11.7 0.4 %collective-permute-done.4.refs_1_.refs_3_ = bf16[4,128,128]{2,1,0:T(8,128)(2,1)S(1)} collective-permute-done((bf16[4,128,128]{2,1,0:T(8,128)(2,1)S(1)}, bf16[4,128,128]{2,1,0:T(8,128)(2,1)S(1)}, u32[]{:S(2)}, u32[]{:S(2)}) %collective-permute-start.4) | collective-permute-done | bytes 131104 | tf_op jit(solution)/shard_map/ppermute | solution.py:272
  12.1 1.4 %shard_map.59 = (bf16[4,128,128]{2,1,0:T(8,128)(2,1)S(1)}, f32[5,128,128]{2,1,0:T(8,128)S(1)}) custom-call(s32[8,128]{1,0:T(8,128)S(1)} %get-tuple-element.45.order_ref, bf16[4,128,128]{2,1,0:T(8,128)(2,1)S(1)} %collective-permute-done.2.refs_0_.refs_2_, ...), custom_call_target="tpu_custom_call", output_to_operand_aliasing={{1}: (4, {})} | custom-call | flops 50331648 | bytes 393216 | tf_op jit(solution)/shard_map/pallas_call | solution.py:307
  13.5 1.3 %collective-permute-start.6 = (bf16[4,128,128]{2,1,0:T(8,128)(2,1)S(1)}, bf16[4,128,128]{2,1,0:T(8,128)(2,1)S(1)}, u32[]{:S(2)}, u32[]{:S(2)}) collective-permute-start(bf16[4,128,128]{2,1,0:T(8,128)(2,1)S(1)} %get-tuple-element.50), channel_id=1, source_target_pairs={{0,4},{1,9},{2,6},{3,11},{4,0},{5,13},{6,2},{7,15},{8,12},{9,1},{1... | collective-permute-start | bytes 393224 | tf_op jit(solution)/shard_map/ppermute | solution.py:361
  14.7 1.9 %shard_map.60 = (bf16[4,128,128]{2,1,0:T(8,128)(2,1)S(1)}, f32[4,128,128]{2,1,0:T(8,128)S(1)}) custom-call(s32[8,128]{1,0:T(8,128)S(1)} %get-tuple-element.45.order_ref, bf16[4,128,128]{2,1,0:T(8,128)(2,1)S(1)} %multiply_convert_fusion.panel.refs_0_, bf16[4,128,128]{2,1,0:T(8,128)(2,1)S(1)} %collective-permute-done.3.refs_0_.refs_1_, ...), custom_call_target="tpu_custom_call" | custom-call | flops 100663296 | bytes 786432 | tf_op jit(solution)/shard_map/pallas_call | solution.py:322
  16.6 0.6 %collective-permute-start.5 = (bf16[4,128,128]{2,1,0:T(8,128)(2,1)S(1)}, bf16[4,128,128]{2,1,0:T(8,128)(2,1)S(1)}, u32[]{:S(2)}, u32[]{:S(2)}) collective-permute-start(bf16[4,128,128]{2,1,0:T(8,128)(2,1)S(1)} %get-tuple-element.48), channel_id=1, source_target_pairs={{0,4},{1,9},{2,6},{3,11},{4,0},{5,13},{6,2},{7,15},{8,12},{9,1},{1... | collective-permute-start | bytes 393224 | tf_op jit(solution)/shard_map/ppermute | solution.py:361
  17.3 1.4 %shard_map.61 = (f32[4,128,128]{2,1,0:T(8,128)S(1)}, f32[4,128,128]{2,1,0:T(8,128)S(1)}) custom-call(s32[8,128]{1,0:T(8,128)S(1)} %get-tuple-element.45.order_ref, bf16[4,128,128]{2,1,0:T(8,128)(2,1)S(1)} %multiply_convert_fusion.panel.refs_0_, bf16[4,128,128]{2,1,0:T(8,128)(2,1)S(1)} %collective-permute-done.3.refs_0_.refs_1_, ...), custom_call_target="tpu_custom_call" | custom-call | flops 201326592 | bytes 1572864 | tf_op jit(solution)/shard_map/pallas_call | solution.py:338
  18.7 1.0 %collective-permute-done.6 = bf16[4,128,128]{2,1,0:T(8,128)(2,1)S(1)} collective-permute-done((bf16[4,128,128]{2,1,0:T(8,128)(2,1)S(1)}, bf16[4,128,128]{2,1,0:T(8,128)(2,1)S(1)}, u32[]{:S(2)}, u32[]{:S(2)}) %collective-permute-start.6) | collective-permute-done | bytes 131104 | tf_op jit(solution)/shard_map/ppermute | solution.py:361
  19.7 1.6 %collective-permute-start.7 = (bf16[4,128,128]{2,1,0:T(8,128)(2,1)S(1)}, bf16[4,128,128]{2,1,0:T(8,128)(2,1)S(1)}, u32[]{:S(2)}, u32[]{:S(2)}) collective-permute-start(bf16[4,128,128]{2,1,0:T(8,128)(2,1)S(1)} %add_convert_fusion), channel_id=1, source_target_pairs={{0,8},{1,5},{2,10},{3,7},{4,12},{5,1},{6,14},{7,3},{8,0},{9,13},{1... | collective-permute-start | bytes 393224 | tf_op jit(solution)/shard_map/ppermute | solution.py:361
  21.4 2.6 %collective-permute-done.5 = bf16[4,128,128]{2,1,0:T(8,128)(2,1)S(1)} collective-permute-done((bf16[4,128,128]{2,1,0:T(8,128)(2,1)S(1)}, bf16[4,128,128]{2,1,0:T(8,128)(2,1)S(1)}, u32[]{:S(2)}, u32[]{:S(2)}) %collective-permute-start.5) | collective-permute-done | bytes 131104 | tf_op jit(solution)/shard_map/ppermute | solution.py:361
  24.1 2.2 %collective-permute-done.7.refs_0_ = bf16[4,128,128]{2,1,0:T(8,128)(2,1)S(1)} collective-permute-done((bf16[4,128,128]{2,1,0:T(8,128)(2,1)S(1)}, bf16[4,128,128]{2,1,0:T(8,128)(2,1)S(1)}, u32[]{:S(2)}, u32[]{:S(2)}) %collective-permute-start.7) | collective-permute-done | bytes 131104 | tf_op jit(solution)/shard_map/ppermute | solution.py:361
  26.2 0.7 %shard_map.62 = bf16[4,128,128]{2,1,0:T(8,128)(2,1)} custom-call(f32[4,128,128]{2,1,0:T(8,128)S(1)} %get-tuple-element.29.factors, f32[4,128,128]{2,1,0:T(8,128)S(1)} %convert_add_fusion.own, bf16[4,128,128]{2,1,0:T(8,128)(2,1)S(1)} %collective-permute-done.7.refs_0_), custom_call_target="tpu_custom_call" | custom-call | tf_op jit(solution)/shard_map/pallas_call | solution.py:381
  (3 shorter events, 0.1 us)
Async XLA Ops:
  0.0 9.5 %collective-permute-start = (bf16[4,128,128]{2,1,0:T(8,128)(2,1)}, bf16[4,128,128]{2,1,0:T(8,128)(2,1)S(1)}, u32[]{:S(2)}, u32[]{:S(2)}) collective-permute-start(bf16[4,128,128]{2,1,0:T(8,128)(2,1)} %bitcast.5), channel_id=1, source_target_pairs={{0,18},{1,17},{2,16},{3,19},{16,2},{17,1},{18,0},{19,3},{4,22},{5,... | collective-permute-start | bytes 393224 | tf_op jit(solution)/shard_map/ppermute | solution.py:269
  4.9 4.5 %collective-permute-start.1 = (f32[4,128]{1,0:T(4,128)S(1)}, f32[4,128]{1,0:T(4,128)S(1)}, u32[]{:S(2)}, u32[]{:S(2)}) collective-permute-start(f32[4,128]{1,0:T(4,128)S(1)} %get-tuple-element.30), channel_id=1, source_target_pairs={{0,18},{1,17},{2,16},{3,19},{16,2},{17,1},{18,0},{19,3},{4,22},{5,... | collective-permute-start | bytes 6152 | tf_op jit(solution)/shard_map/ppermute | solution.py:269
  5.0 5.4 %collective-permute-start.3 = (bf16[4,128,128]{2,1,0:T(8,128)(2,1)S(1)}, bf16[4,128,128]{2,1,0:T(8,128)(2,1)S(1)}, u32[]{:S(2)}, u32[]{:S(2)}) collective-permute-start(bf16[4,128,128]{2,1,0:T(8,128)(2,1)S(1)} %get-tuple-element.35), channel_id=1, source_target_pairs={{0,16},{1,19},{2,18},{3,17},{16,0},{17,3},{18,2},{19,1},{4,20},{5,... | collective-permute-start | bytes 393224 | tf_op jit(solution)/shard_map/ppermute | solution.py:269
  9.6 2.1 %collective-permute-start.2 = (bf16[4,128,128]{2,1,0:T(8,128)(2,1)S(1)}, bf16[4,128,128]{2,1,0:T(8,128)(2,1)S(1)}, u32[]{:S(2)}, u32[]{:S(2)}) collective-permute-start(bf16[4,128,128]{2,1,0:T(8,128)(2,1)S(1)} %multiply_convert_fusion.panel.refs_0_), channel_id=1, source_target_pairs={{0,1},{1,0},{2,3},{3,2},{4,5},{5,4},{6,7},{7,6},{8,9},{9,8},{10,11... | collective-permute-start | bytes 393224 | tf_op jit(solution)/shard_map/ppermute | solution.py:272
  10.4 1.7 %collective-permute-start.4 = (bf16[4,128,128]{2,1,0:T(8,128)(2,1)S(1)}, bf16[4,128,128]{2,1,0:T(8,128)(2,1)S(1)}, u32[]{:S(2)}, u32[]{:S(2)}) collective-permute-start(bf16[4,128,128]{2,1,0:T(8,128)(2,1)S(1)} %collective-permute-done.3.refs_0_.refs_1_), channel_id=1, source_target_pairs={{0,1},{1,0},{2,3},{3,2},{4,5},{5,4},{6,7},{7,6},{8,9},{9,8},{10,11... | collective-permute-start | bytes 393224 | tf_op jit(solution)/shard_map/ppermute | solution.py:272
  13.5 6.3 %collective-permute-start.6 = (bf16[4,128,128]{2,1,0:T(8,128)(2,1)S(1)}, bf16[4,128,128]{2,1,0:T(8,128)(2,1)S(1)}, u32[]{:S(2)}, u32[]{:S(2)}) collective-permute-start(bf16[4,128,128]{2,1,0:T(8,128)(2,1)S(1)} %get-tuple-element.50), channel_id=1, source_target_pairs={{0,4},{1,9},{2,6},{3,11},{4,0},{5,13},{6,2},{7,15},{8,12},{9,1},{1... | collective-permute-start | bytes 393224 | tf_op jit(solution)/shard_map/ppermute | solution.py:361
  16.6 7.4 %collective-permute-start.5 = (bf16[4,128,128]{2,1,0:T(8,128)(2,1)S(1)}, bf16[4,128,128]{2,1,0:T(8,128)(2,1)S(1)}, u32[]{:S(2)}, u32[]{:S(2)}) collective-permute-start(bf16[4,128,128]{2,1,0:T(8,128)(2,1)S(1)} %get-tuple-element.48), channel_id=1, source_target_pairs={{0,4},{1,9},{2,6},{3,11},{4,0},{5,13},{6,2},{7,15},{8,12},{9,1},{1... | collective-permute-start | bytes 393224 | tf_op jit(solution)/shard_map/ppermute | solution.py:361
  19.7 6.5 %collective-permute-start.7 = (bf16[4,128,128]{2,1,0:T(8,128)(2,1)S(1)}, bf16[4,128,128]{2,1,0:T(8,128)(2,1)S(1)}, u32[]{:S(2)}, u32[]{:S(2)}) collective-permute-start(bf16[4,128,128]{2,1,0:T(8,128)(2,1)S(1)} %add_convert_fusion), channel_id=1, source_target_pairs={{0,8},{1,5},{2,10},{3,7},{4,12},{5,1},{6,14},{7,3},{8,0},{9,13},{1... | collective-permute-start | bytes 393224 | tf_op jit(solution)/shard_map/ppermute | solution.py:361
